TPU v7x, 32 devices: a whole 2x2x4 slice. The times are simulated.
32 devices in a mesh: fsdp: 4 (over y, x), ctx: 8 (over z, core).
Axes of the slice: x: 2, y: 2, z: 4, core: 2. Of those that a mesh axis runs over, the one named last changes fastest.
Arguments:
- inputs: bfloat16 [4, 2048, 768], P('fsdp', 'ctx'), may hold values from -6 to 6
- positions: int32 [4, 2048], P('fsdp', 'ctx'), may hold values from 0 to 2047, as said below
- in_weight: bfloat16 [768, 2304], P('fsdp'), may hold values from -0.21875 to 0.21875
- in_bias: bfloat16 [2304], P('fsdp'), may hold values from -0.3125 to 0.3125
- out_weight: bfloat16 [768, 768], P('fsdp'), may hold values from -0.109375 to 0.109375
- out_bias: bfloat16 [768], P('fsdp'), may hold values from -4 to 4
- up_weight: bfloat16 [768, 3072], P('fsdp'), may hold values from -0.21875 to 0.21875
- up_bias: bfloat16 [3072], P('fsdp'), may hold values from -6 to 6
- down_weight: bfloat16 [3072, 768], P('fsdp'), may hold values from -0.109375 to 0.109375
- down_bias: bfloat16 [768], P('fsdp'), may hold values from -4 to 4
- first_gain: bfloat16 [768], P('fsdp'), may hold values from 0.25 to 1.75
- first_shift: bfloat16 [768], P('fsdp'), may hold values from -4 to 4
- second_gain: bfloat16 [768], P('fsdp'), may hold values from 0.25 to 1.75
- second_shift: bfloat16 [768], P('fsdp'), may hold values from -4 to 4
- out_grad: bfloat16 [4, 2048, 768], P('fsdp', 'ctx'), may hold values from -6 to 6
Outputs:
- output: bfloat16 [4, 2048, 768], P('fsdp', 'ctx')
- input_gradient: float32 [4, 2048, 768], P('fsdp', 'ctx')
- in_weight_gradient: float32 [768, 2304], P('fsdp')
- in_bias_gradient: float32 [2304], P('fsdp')
- out_weight_gradient: float32 [768, 768], P('fsdp')
- out_bias_gradient: float32 [768], P('fsdp')
- up_weight_gradient: float32 [768, 3072], P('fsdp')
- up_bias_gradient: float32 [3072], P('fsdp')
- down_weight_gradient: float32 [3072, 768], P('fsdp')
- down_bias_gradient: float32 [768], P('fsdp')
- first_gain_gradient: float32 [768], P('fsdp')
- first_shift_gradient: float32 [768], P('fsdp')
- second_gain_gradient: float32 [768], P('fsdp')
- second_shift_gradient: float32 [768], P('fsdp')
Inputs may be any that keep to these rules, and one draw needn't show every extreme that they name: Each row holds every position of its sequence once, in runs of 128 consecutive rising positions that start at multiples of 128; the order of the runs differs from row to row.
All inputs are finite; a program needn't handle non-finite values.
Results may differ from a plain program's by a relative error of at most 0.018.
Values may be sent and summed in bfloat16 or wider, within the bound.
No kernel may reach another device: no remote copies, remote signals or barrier semaphores. Data moves between devices by JAX's collectives and lax.ppermute only.
A program may use at most 192 MiB of HBM per device.

v0:
```python
import math

import jax
import jax.numpy as jnp
from jax import lax
from jax.sharding import PartitionSpec as P

HEAD = 64
ROT = 16


NEG = -1e30
EPS = 1e-05


def from_behind(x, axis, by):
    size = lax.axis_size(axis)
    return lax.ppermute(x, axis, [(i, (i + by) % size) for i in range(size)])


def layer_norm(values, gain, shift):
    mean = jnp.mean(values, -1, keepdims=True)
    centred = values - mean
    spread = jnp.mean(centred * centred, -1, keepdims=True)
    return centred * lax.rsqrt(spread + EPS) * gain + shift


def turn_tables(positions):
    ladder = 10000.0 ** (-jnp.arange(0, ROT, 2, dtype=jnp.float32) / ROT)
    angle = positions.astype(jnp.float32)[..., None] * ladder
    angle = jnp.concatenate([angle, angle], -1)
    return (jnp.cos(angle), jnp.sin(angle))


def rotate(values, cosine, sine):
    half = ROT // 2
    part = values[..., :ROT]
    turned = jnp.concatenate([-part[..., half:], part[..., :half]], -1)
    part = part * cosine[..., None, :] + turned * sine[..., None, :]
    return jnp.concatenate([part, values[..., ROT:]], -1)


def across(left, right):
    return lax.dot_general(
        left, right, (((0,), (0,)), ((), ())), preferred_element_type=jnp.float32
    )


def against(left, right):
    return lax.dot_general(
        left, right, (((1,), (1,)), ((), ())), preferred_element_type=jnp.float32
    )


def softmax_step(carry, queries, query_pos, keys, values, key_pos, scale):
    peak, total, summed = carry
    scores = jnp.einsum("qhd,khd->hqk", queries, keys, preferred_element_type=jnp.float32) * scale
    allowed = (key_pos[None, :] <= query_pos[:, None])[None]
    new_peak = jnp.maximum(peak, jnp.max(jnp.where(allowed, scores, NEG), -1))
    weights = jnp.where(allowed, jnp.exp(scores - new_peak[..., None]), 0.0)
    fade = jnp.exp(peak - new_peak)
    total = total * fade + jnp.sum(weights, -1)
    added = jnp.einsum(
        "hqk,khd->qhd", weights.astype(jnp.bfloat16), values, preferred_element_type=jnp.float32
    )
    summed = summed * jnp.transpose(fade)[:, :, None] + added
    return (new_peak, total, summed)


def gradient_step(
    state, queries, query_pos, outs_back, log_total, spread, keys, values, key_pos, scale
):
    back_query, back_key, back_value = state
    scores = jnp.einsum("qhd,khd->hqk", queries, keys, preferred_element_type=jnp.float32) * scale
    allowed = (key_pos[None, :] <= query_pos[:, None])[None]
    probs = jnp.where(allowed, jnp.exp(scores - log_total[..., None]), 0.0)
    back_probs = jnp.einsum("qhd,khd->hqk", outs_back, values, preferred_element_type=jnp.float32)
    back_scores = (probs * (back_probs - spread[..., None])).astype(jnp.bfloat16)
    back_query = (
        back_query
        + jnp.einsum("hqk,khd->qhd", back_scores, keys, preferred_element_type=jnp.float32) * scale
    )
    back_key = (
        back_key
        + jnp.einsum("hqk,qhd->khd", back_scores, queries, preferred_element_type=jnp.float32)
        * scale
    )
    back_value = back_value + jnp.einsum(
        "hqk,qhd->khd", probs.astype(jnp.bfloat16), outs_back, preferred_element_type=jnp.float32
    )
    return (back_query, back_key, back_value)


def on_device(
    inputs,
    positions,
    in_weight,
    in_bias,
    out_weight,
    out_bias,
    up_weight,
    up_bias,
    down_weight,
    down_bias,
    first_gain,
    first_shift,
    second_gain,
    second_shift,
    out_grad,
):
    gathered = (
        lax.all_gather(in_weight, "fsdp", axis=0, tiled=True),
        lax.all_gather(in_bias, "fsdp", axis=0, tiled=True),
        lax.all_gather(out_weight, "fsdp", axis=0, tiled=True),
        lax.all_gather(out_bias, "fsdp", axis=0, tiled=True),
        lax.all_gather(up_weight, "fsdp", axis=0, tiled=True),
        lax.all_gather(up_bias, "fsdp", axis=0, tiled=True),
        lax.all_gather(down_weight, "fsdp", axis=0, tiled=True),
        lax.all_gather(down_bias, "fsdp", axis=0, tiled=True),
        lax.all_gather(first_gain, "fsdp", axis=0, tiled=True),
        lax.all_gather(first_shift, "fsdp", axis=0, tiled=True),
        lax.all_gather(second_gain, "fsdp", axis=0, tiled=True),
        lax.all_gather(second_shift, "fsdp", axis=0, tiled=True),
    )
    (
        full_in,
        full_in_bias,
        full_out,
        full_out_bias,
        full_up,
        full_up_bias,
        full_down,
        full_down_bias,
        gain_one,
        shift_one,
        gain_two,
        shift_two,
    ) = gathered
    tokens = inputs.shape[1]
    width = inputs.shape[2]
    heads = width // HEAD
    scale = 1.0 / math.sqrt(HEAD)
    query_pos = positions[0]
    all_pos = lax.all_gather(query_pos, "ctx", axis=0, tiled=True)
    resid = inputs[0].astype(jnp.float32)

    def norms(values, gain_a, shift_a, gain_b, shift_b):
        return (layer_norm(values, gain_a, shift_a), layer_norm(values, gain_b, shift_b))

    (normed_one, normed_two), norm_back = jax.vjp(
        norms,
        resid,
        gain_one.astype(jnp.float32),
        shift_one.astype(jnp.float32),
        gain_two.astype(jnp.float32),
        shift_two.astype(jnp.float32),
    )
    first = normed_one.astype(jnp.bfloat16)
    second = normed_two.astype(jnp.bfloat16)
    projected = jnp.dot(first, full_in, preferred_element_type=jnp.float32) + full_in_bias.astype(
        jnp.float32
    )
    projected = projected.reshape(tokens, 3, heads, HEAD)
    cosine, sine = turn_tables(query_pos)
    queries = rotate(projected[:, 0], cosine, sine).astype(jnp.bfloat16)
    keys = rotate(projected[:, 1], cosine, sine).astype(jnp.bfloat16)
    values = projected[:, 2].astype(jnp.bfloat16)
    start_state = (
        jnp.full((heads, tokens), NEG, jnp.float32),
        jnp.zeros((heads, tokens), jnp.float32),
        jnp.zeros((tokens, heads, HEAD), jnp.float32),
    )
    carry = start_state
    key_piece = lax.all_gather(keys, "ctx", axis=0, tiled=True)
    value_piece = lax.all_gather(values, "ctx", axis=0, tiled=True)
    count = key_piece.shape[0]
    size = 512

    def one_block(inner, offset):
        key_block = lax.dynamic_slice_in_dim(key_piece, offset, size, 0)
        value_block = lax.dynamic_slice_in_dim(value_piece, offset, size, 0)
        key_pos = lax.dynamic_slice_in_dim(all_pos, offset, size, 0)
        result = softmax_step(inner, queries, query_pos, key_block, value_block, key_pos, scale)
        return (result, None)

    carry, _ = lax.scan(one_block, carry, jnp.arange(0, count, size, dtype=jnp.int32))
    peak, total, summed = carry
    attended = summed / jnp.transpose(total)[:, :, None]
    log_total = peak + jnp.log(total)
    mixed = attended.reshape(tokens, width).astype(jnp.bfloat16)
    up = jnp.dot(second, full_up, preferred_element_type=jnp.float32) + full_up_bias.astype(
        jnp.float32
    )
    activated, gelu_back = jax.vjp(lambda value: jax.nn.gelu(value, approximate=False), up)
    activated = activated.astype(jnp.bfloat16)
    branch_attn = jnp.dot(
        mixed, full_out, preferred_element_type=jnp.float32
    ) + full_out_bias.astype(jnp.float32)
    branch_ff = jnp.dot(
        activated, full_down, preferred_element_type=jnp.float32
    ) + full_down_bias.astype(jnp.float32)
    output = resid + branch_attn + branch_ff
    cotangent = out_grad[0]
    back_out = cotangent.astype(jnp.float32)
    bias_sum = jnp.sum(back_out, 0)
    out_weight_part = across(mixed, cotangent)
    down_weight_part = across(activated, cotangent)
    back_mixed = against(cotangent, full_out).astype(jnp.bfloat16)
    back_active = against(cotangent, full_down)
    back_up = gelu_back(back_active)[0].astype(jnp.bfloat16)
    up_weight_part = across(second, back_up)
    up_bias_part = jnp.sum(back_up.astype(jnp.float32), 0)
    back_second = against(back_up, full_up)
    outs_back = back_mixed.reshape(tokens, heads, HEAD)
    spread = jnp.einsum("qhd,qhd->hq", outs_back.astype(jnp.float32), attended)
    cycle_size = lax.axis_size("ctx")
    here = lax.axis_index("ctx")
    zeros = jnp.zeros((tokens, heads, HEAD), jnp.float32)

    def key_turn(turn, state):
        moving_key, moving_value, back_key, back_value, back_query = state
        owner = (here - turn) % cycle_size
        key_pos = lax.dynamic_slice_in_dim(all_pos, owner * tokens, tokens, 0)
        back_query, back_key, back_value = gradient_step(
            (back_query, back_key, back_value),
            queries,
            query_pos,
            outs_back,
            log_total,
            spread,
            moving_key,
            moving_value,
            key_pos,
            scale,
        )
        moving_key, moving_value = from_behind((moving_key, moving_value), "ctx", 1)
        back_key, back_value = (
            from_behind(back_key.astype(jnp.bfloat16), "ctx", 1).astype(back_key.dtype),
            from_behind(back_value.astype(jnp.bfloat16), "ctx", 1).astype(back_value.dtype),
        )
        return (moving_key, moving_value, back_key, back_value, back_query)

    final = lax.fori_loop(0, cycle_size, key_turn, (keys, values, zeros, zeros, zeros))
    back_query, back_key, back_value = (final[4], final[2], final[3])
    back_query = rotate(back_query, cosine, -sine)
    back_key = rotate(back_key, cosine, -sine)
    back_projected = (
        jnp.stack([back_query, back_key, back_value], 1)
        .reshape(tokens, 3 * width)
        .astype(jnp.bfloat16)
    )
    in_weight_part = across(first, back_projected)
    in_bias_part = jnp.sum(back_projected.astype(jnp.float32), 0)
    back_first = against(back_projected, full_in)
    back_resid, gain_one_part, shift_one_part, gain_two_part, shift_two_part = norm_back(
        (back_first, back_second)
    )
    input_gradient = back_out + back_resid
    shares = (
        lax.psum_scatter(
            in_weight_part.astype(jnp.bfloat16), "fsdp", scatter_dimension=0, tiled=True
        ).astype(jnp.float32),
        lax.psum_scatter(
            in_bias_part.astype(jnp.bfloat16), "fsdp", scatter_dimension=0, tiled=True
        ).astype(jnp.float32),
        lax.psum_scatter(
            out_weight_part.astype(jnp.bfloat16), "fsdp", scatter_dimension=0, tiled=True
        ).astype(jnp.float32),
        lax.psum_scatter(
            bias_sum.astype(jnp.bfloat16), "fsdp", scatter_dimension=0, tiled=True
        ).astype(jnp.float32),
        lax.psum_scatter(
            up_weight_part.astype(jnp.bfloat16), "fsdp", scatter_dimension=0, tiled=True
        ).astype(jnp.float32),
        lax.psum_scatter(
            up_bias_part.astype(jnp.bfloat16), "fsdp", scatter_dimension=0, tiled=True
        ).astype(jnp.float32),
        lax.psum_scatter(
            down_weight_part.astype(jnp.bfloat16), "fsdp", scatter_dimension=0, tiled=True
        ).astype(jnp.float32),
        lax.psum_scatter(
            gain_one_part.astype(jnp.bfloat16), "fsdp", scatter_dimension=0, tiled=True
        ).astype(jnp.float32),
        lax.psum_scatter(
            shift_one_part.astype(jnp.bfloat16), "fsdp", scatter_dimension=0, tiled=True
        ).astype(jnp.float32),
        lax.psum_scatter(
            gain_two_part.astype(jnp.bfloat16), "fsdp", scatter_dimension=0, tiled=True
        ).astype(jnp.float32),
        lax.psum_scatter(
            shift_two_part.astype(jnp.bfloat16), "fsdp", scatter_dimension=0, tiled=True
        ).astype(jnp.float32),
    )
    totals = (
        lax.psum(shares[0].astype(jnp.bfloat16), "ctx").astype(jnp.float32),
        lax.psum(shares[1].astype(jnp.bfloat16), "ctx").astype(jnp.float32),
        lax.psum(shares[2].astype(jnp.bfloat16), "ctx").astype(jnp.float32),
        lax.psum(shares[3].astype(jnp.bfloat16), "ctx").astype(jnp.float32),
        lax.psum(shares[4].astype(jnp.bfloat16), "ctx").astype(jnp.float32),
        lax.psum(shares[5].astype(jnp.bfloat16), "ctx").astype(jnp.float32),
        lax.psum(shares[6].astype(jnp.bfloat16), "ctx").astype(jnp.float32),
        lax.psum(shares[7].astype(jnp.bfloat16), "ctx").astype(jnp.float32),
        lax.psum(shares[8].astype(jnp.bfloat16), "ctx").astype(jnp.float32),
        lax.psum(shares[9].astype(jnp.bfloat16), "ctx").astype(jnp.float32),
        lax.psum(shares[10].astype(jnp.bfloat16), "ctx").astype(jnp.float32),
    )
    return (
        output.astype(jnp.bfloat16)[None],
        input_gradient[None],
        totals[0],
        totals[1],
        totals[2],
        totals[3],
        totals[4],
        totals[5],
        totals[6],
        totals[3],
        totals[7],
        totals[8],
        totals[9],
        totals[10],
    )


def solution(mesh):
    return jax.shard_map(
        on_device,
        mesh=mesh,
        in_specs=(
            P("fsdp", "ctx", None),
            P("fsdp", "ctx"),
            P("fsdp", None),
            P("fsdp"),
            P("fsdp", None),
            P("fsdp"),
            P("fsdp", None),
            P("fsdp"),
            P("fsdp", None),
            P("fsdp"),
            P("fsdp"),
            P("fsdp"),
            P("fsdp"),
            P("fsdp"),
            P("fsdp", "ctx", None),
        ),
        out_specs=(
            P("fsdp", "ctx", None),
            P("fsdp", "ctx", None),
            P("fsdp", None),
            P("fsdp"),
            P("fsdp", None),
            P("fsdp"),
            P("fsdp", None),
            P("fsdp"),
            P("fsdp", None),
            P("fsdp"),
            P("fsdp"),
            P("fsdp"),
            P("fsdp"),
            P("fsdp"),
        ),
        check_vma=False,
    )
```

profile of v0, /device:TPU:0, one launch (start us, length us, event | category | flops | bytes accessed | tf_op | source)
XLA Modules:
  0.0 707.0 jit_solution(10681487738134994407)
XLA Ops:
  14.8 18.4 %all-reduce.17 = (bf16[768]{0:T(1024)(128)(2,1)}, bf16[768]{0:T(1024)(128)(2,1)}, bf16[2304]{0:T(1024)(128)(2,1)S(1)}, bf16[768]{0:T(1024)(128)(2,1)S(1)}, bf16[768]{0:T(1024)(128)(2,1)S(1)}) all-reduce(bf16[768]{0:T(1024)(128)(2,1)S(1)} %dynamic-update-slice.5, ...), channel_id=1, replica_groups=mesh['fsdp'=4,'ctx'=8] {'fsdp'}, use_global_device_ids=true, to_apply=%add.5 | all-reduce | flops 5376 | bytes 21504
  37.1 22.8 %all-gather.10.cloned.1.call-done = bf16[768,2304]{1,0:T(8,128)(2,1)} async-done(((bf16[192,2304]{1,0:T(8,128)(2,1)}), bf16[768,2304]{1,0:T(8,128)(2,1)}) %all-gather.10.cloned.1.call-update) | async-done | bytes 3538960 | tf_op jit(solution)/shard_map/all_gather | solution.py:112
  59.9 4.7 convolution_add_fusion
  71.0 12.8 %all-gather = s32[1,2048]{1,0:T(1,128)} all-gather(s32[1,256]{1,0:T(1,128)} %param.20), channel_id=2, replica_groups=mesh['fsdp'=4,'ctx'=8] {'ctx'}, dimensions={1}, use_global_device_ids=true | all-gather | bytes 9216 | tf_op jit(solution)/shard_map/all_gather | solution.py:144
  85.9 8.1 %all-gather.2 = bf16[4,1,768]{2,1,0:T(2,128)(2,1)S(1)} all-gather(bf16[1,1,768]{2,1,0:T(2,128)(2,1)S(1)} %reshape.293), channel_id=1, replica_groups=mesh['fsdp'=4,'ctx'=8] {'fsdp'}, dimensions={0}, use_global_device_ids=true | all-gather | bytes 7680 | tf_op jit(solution)/shard_map/all_gather | solution.py:117
  94.1 13.7 %all-gather.12.cloned.1.call-done = bf16[2048,12,64]{0,2,1:T(8,128)(2,1)} async-done(((bf16[256,12,64]{0,2,1:T(8,128)(2,1)}), bf16[2048,12,64]{0,2,1:T(8,128)(2,1)}) %all-gather.12.cloned.1.call-update) | async-done | bytes 3145744 | tf_op jit(solution)/shard_map/all_gather | solution.py:174
  107.7 41.4 %all-gather.20.cloned.1.call-done = bf16[2048,1,12,64]{0,3,2,1:T(8,128)(2,1)} async-done(((bf16[256,1,12,64]{0,3,2,1:T(8,128)(2,1)}), bf16[2048,1,12,64]{0,3,2,1:T(8,128)(2,1)}) %all-gather.20.cloned.1.call-update) | async-done | bytes 3145744 | tf_op jit(solution)/shard_map/all_gather | solution.py:175
  149.1 64.1 %while.39 = (s32[]{:T(128)}, f32[12,256]{1,0:T(8,128)S(1)}, f32[12,256]{1,0:T(8,128)S(1)}, f32[256,12,64]{0,2,1:T(8,128)S(1)}, s32[4]{0:T(128)S(1)}, /*index=5*/...) while((s32[]{:T(128)}, f32[12,256]{1,0:T(8,128)S(1)}, ...), condition=%wide.region_5.6_spmd.clone, body=%wide.region_2.5_spmd.clone.sunk | while | flops 420694016 | bytes 48307420 | solution.py:186
  153.2 5.7 fusion.173
  158.9 4.8 fusion.177
  169.2 5.5 fusion.173
  174.7 4.8 fusion.177
  185.8 5.5 fusion.173
  191.3 4.8 fusion.177
  201.6 5.4 fusion.173
  207.1 4.7 fusion.177
  215.2 11.6 %multiply_convert_fusion.1 = (bf16[256,3072]{1,0:T(8,128)(2,1)S(1)}, f32[256,3072]{1,0:T(8,128)}, f32[256,3072]{1,0:T(8,128)}) fusion(f32[3072]{0:T(1024)S(1)} %bitcast.232, bf16[768,3072]{1,0:T(8,128)(2,1)} %all-gather.16.cloned.1.call-done, bf16[1,256,768]{2,1,0:T(8,128)(2,1)S(1)} %copy-done.3, f32[768]{0:T(1024)S(1)} %convert_element_type.251, ...), kind=kOutput, calls=%fused_computation.54 | convolution fusion | flops 1261043712 | bytes 12996608 | tf_op jit(solution)/shard_map/dot_general | solution.py:191
  226.7 38.2 %all-gather.18.cloned.1.call-done = bf16[3072,768]{1,0:T(8,128)(2,1)} async-done(((bf16[768,768]{1,0:T(8,128)(2,1)}), bf16[3072,768]{1,0:T(8,128)(2,1)}) %all-gather.18.cloned.1.call-update) | async-done | bytes 4718608 | tf_op jit(solution)/shard_map/all_gather | solution.py:118
  264.9 6.8 fusion.119
  276.7 17.6 %all-gather.14.cloned.1.call-done = bf16[768,768]{1,0:T(8,128)(2,1)} async-done(((bf16[192,768]{1,0:T(8,128)(2,1)}), bf16[768,768]{1,0:T(8,128)(2,1)}) %all-gather.14.cloned.1.call-update) | async-done | bytes 1179664 | tf_op jit(solution)/shard_map/all_gather | solution.py:114
  307.7 244.7 %while.40 = (s32[]{:T(128)}, bf16[256,12,64]{0,2,1:T(8,128)(2,1)}, bf16[256,12,64]{0,2,1:T(8,128)(2,1)}, f32[256,12,64]{0,2,1:T(8,128)S(1)}, f32[256,12,64]{0,2,...) while((s32[]{:T(128)}, bf16[256,12,64]{0,2,1:T(8,128)(2,1)}, ...), condition=%wide.region_9.10_spmd.clone, body=%wide.region_8.9_spmd.clone.sunk | while | flops 513605632 | bytes 40837772 | solution.py:243
  381.9 5.1 collective-permute-done.2
  412.6 5.0 collective-permute-done.2
  443.1 5.1 collective-permute-done.2
  473.6 5.1 collective-permute-done.2
  504.2 5.1 collective-permute-done.2
  534.7 5.1 collective-permute-done.2
  563.0 4.8 fusion.121
  570.0 34.4 %reduce-scatter.5.cloned.1.call-done = bf16[192,2304]{1,0:T(8,128)(2,1)} async-done(((bf16[768,2304]{1,0:T(8,128)(2,1)}), bf16[192,2304]{1,0:T(8,128)(2,1)}) %reduce-scatter.5.cloned.1.call-update) | async-done | bytes 884752 | tf_op jit(solution)/shard_map/reduce_scatter | solution.py:260
  606.4 15.3 %all-reduce.16 = (bf16[768]{0:T(1024)(128)(2,1)S(1)}, bf16[768]{0:T(1024)(128)(2,1)S(1)}, bf16[2304]{0:T(1024)(128)(2,1)S(1)}, bf16[768]{0:T(1024)(128)(2,1)S(1)...) all-reduce(bf16[768]{0:T(1024)(128)(2,1)S(1)} %dynamic-update-slice, ...), channel_id=1, replica_groups=mesh['fsdp'=4,'ctx'=8] {'fsdp'}, use_global_device_ids=true, to_apply=%add.6 | all-reduce | flops 10752 | bytes 43008
  622.3 15.3 %all-reduce.14 = (bf16[576]{0:T(1024)(128)(2,1)S(1)}, bf16[192]{0:T(256)(128)(2,1)S(1)}, bf16[768]{0:T(1024)(128)(2,1)S(1)}, bf16[192]{0:T(256)(128)(2,1)S(1)}, ...) all-reduce(bf16[576]{0:T(1024)(128)(2,1)S(1)} %dynamic-slice.8, ...), channel_id=1, replica_groups=mesh['fsdp'=4,'ctx'=8] {'ctx'}, use_global_device_ids=true, to_apply=%region_16.17 | all-reduce | flops 2304 | bytes 9216 | tf_op jit(solution)/shard_map/psum | solution.py:296
  647.7 45.3 %all-reduce.20.cloned.1.call-done = (bf16[192,2304]{1,0:T(8,128)(2,1)}, bf16[192,768]{1,0:T(8,128)(2,1)}, bf16[192,3072]{1,0:T(8,128)(2,1)}, bf16[768,768]{1,0:T(8,128)(2,1)}) async-done(((bf16[192,2304]{1,0:T(8,128)(2,1)}, bf16[192,768]{1,0:T(8,128)(2,1)}, bf16[192,3072]{1,0:T(8,128)(2,1)}, bf16[768,768]{1,0:T(8,128)(2,1)}), (bf16[192,2304]{1,0:T(8,128)(2,1)}, bf16[192,768]{1,0:T(8,128)(2,1)}, ...) | async-done | bytes 3538960 | tf_op jit(solution)/shard_map/psum | solution.py:295
  (466 shorter events, 297.8 us)
Async XLA Ops:
  7.2 52.8 %all-gather.10.cloned.1.call-start = ((), (), s32[]{:S(2)}) async-start(), calls=%async_computation.4 | async-start | bytes 4423680 | tf_op jit(solution)/shard_map/all_gather | solution.py:112
  7.9 99.8 %all-gather.12.cloned.1.call-start = ((), (), s32[]{:S(2)}) async-start(), calls=%async_computation.5 | async-start | bytes 3538944 | tf_op jit(solution)/shard_map/all_gather | solution.py:174
  68.4 80.7 %all-gather.20.cloned.1.call-start = ((), (), s32[]{:S(2)}) async-start(), calls=%async_computation.13 | async-start | bytes 3538944 | tf_op jit(solution)/shard_map/all_gather | solution.py:175
  69.2 145.9 %all-gather.16.cloned.1.call-start = ((), (), s32[]{:S(2)}) async-start(), calls=%async_computation.7 | async-start | bytes 5898240 | tf_op jit(solution)/shard_map/all_gather | solution.py:116
  69.8 195.1 %all-gather.18.cloned.1.call-start = ((), (), s32[]{:S(2)}) async-start(), calls=%async_computation.8 | async-start | bytes 5898240 | tf_op jit(solution)/shard_map/all_gather | solution.py:118
  70.4 223.9 %all-gather.14.cloned.1.call-start = ((), (), s32[]{:S(2)}) async-start(), calls=%async_computation.6 | async-start | bytes 1474560 | tf_op jit(solution)/shard_map/all_gather | solution.py:114
  71.0 499.0 %reduce-scatter.7.cloned.1.call-start = ((), (), s32[]{:S(2)}) async-start(), calls=%async_computation.10 | async-start | bytes 1474560 | tf_op jit(solution)/shard_map/reduce_scatter | solution.py:266
  214.9 355.1 %reduce-scatter.9.cloned.1.call-start = ((), (), s32[]{:S(2)}) async-start(), calls=%async_computation.11 | async-start | bytes 5898240 | tf_op jit(solution)/shard_map/reduce_scatter | solution.py:272
  276.6 293.4 %reduce-scatter.11.cloned.1.call-start = ((), (), s32[]{:S(2)}) async-start(), calls=%async_computation.12 | async-start | bytes 5898240 | tf_op jit(solution)/shard_map/reduce_scatter | solution.py:278
  304.3 300.2 %reduce-scatter.5.cloned.1.call-start = ((), (), s32[]{:S(2)}) async-start(), calls=%async_computation.9 | async-start | bytes 4423680 | tf_op jit(solution)/shard_map/reduce_scatter | solution.py:260
  319.0 10.9 %collective-permute-start.3 = (bf16[256,12,64]{0,2,1:T(8,128)(2,1)}, bf16[256,12,64]{0,2,1:T(8,128)(2,1)}, u32[]{:S(2)}, u32[]{:S(2)}) collective-permute-start(bf16[256,12,64]{0,2,1:T(8,128)(2,1)} %fusion.190), channel_id=1, source_target_pairs={{0,1},{1,2},{2,3},{3,4},{4,5},{5,6},{6,7},{7,0},{8,9},{9,10},{10,1... | collective-permute-start | bytes 1179656 | tf_op jit(solution)/shard_map/while/body/eval_jaxpr/ppermute | solution.py:18
  320.5 13.6 %collective-permute-start = (bf16[256,12,64]{0,2,1:T(8,128)(2,1)S(1)}, bf16[256,12,64]{0,2,1:T(8,128)(2,1)}, u32[]{:S(2)}, u32[]{:S(2)}) collective-permute-start(bf16[256,12,64]{0,2,1:T(8,128)(2,1)S(1)} %copy.76), channel_id=1, source_target_pairs={{0,1},{1,2},{2,3},{3,4},{4,5},{5,6},{6,7},{7,0},{8,9},{9,10},{10,1... | collective-permute-start | bytes 1179656 | tf_op jit(solution)/shard_map/while/body/eval_jaxpr/ppermute | solution.py:18
  320.6 17.7 %collective-permute-start.1 = (bf16[256,12,64]{0,2,1:T(8,128)(2,1)}, bf16[256,12,64]{0,2,1:T(8,128)(2,1)}, u32[]{:S(2)}, u32[]{:S(2)}) collective-permute-start(bf16[256,12,64]{0,2,1:T(8,128)(2,1)} %copy.77), channel_id=1, source_target_pairs={{0,1},{1,2},{2,3},{3,4},{4,5},{5,6},{6,7},{7,0},{8,9},{9,10},{10,1... | collective-permute-start | bytes 1179656 | tf_op jit(solution)/shard_map/while/body/eval_jaxpr/ppermute | solution.py:18
  349.6 10.9 %collective-permute-start.3 = (bf16[256,12,64]{0,2,1:T(8,128)(2,1)}, bf16[256,12,64]{0,2,1:T(8,128)(2,1)}, u32[]{:S(2)}, u32[]{:S(2)}) collective-permute-start(bf16[256,12,64]{0,2,1:T(8,128)(2,1)} %fusion.190), channel_id=1, source_target_pairs={{0,1},{1,2},{2,3},{3,4},{4,5},{5,6},{6,7},{7,0},{8,9},{9,10},{10,1... | collective-permute-start | bytes 1179656 | tf_op jit(solution)/shard_map/while/body/eval_jaxpr/ppermute | solution.py:18
  349.6 15.1 %collective-permute-start = (bf16[256,12,64]{0,2,1:T(8,128)(2,1)S(1)}, bf16[256,12,64]{0,2,1:T(8,128)(2,1)}, u32[]{:S(2)}, u32[]{:S(2)}) collective-permute-start(bf16[256,12,64]{0,2,1:T(8,128)(2,1)S(1)} %copy.76), channel_id=1, source_target_pairs={{0,1},{1,2},{2,3},{3,4},{4,5},{5,6},{6,7},{7,0},{8,9},{9,10},{10,1... | collective-permute-start | bytes 1179656 | tf_op jit(solution)/shard_map/while/body/eval_jaxpr/ppermute | solution.py:18
  349.6 19.3 %collective-permute-start.1 = (bf16[256,12,64]{0,2,1:T(8,128)(2,1)}, bf16[256,12,64]{0,2,1:T(8,128)(2,1)}, u32[]{:S(2)}, u32[]{:S(2)}) collective-permute-start(bf16[256,12,64]{0,2,1:T(8,128)(2,1)} %copy.77), channel_id=1, source_target_pairs={{0,1},{1,2},{2,3},{3,4},{4,5},{5,6},{6,7},{7,0},{8,9},{9,10},{10,1... | collective-permute-start | bytes 1179656 | tf_op jit(solution)/shard_map/while/body/eval_jaxpr/ppermute | solution.py:18
  380.3 10.9 %collective-permute-start.3 = (bf16[256,12,64]{0,2,1:T(8,128)(2,1)}, bf16[256,12,64]{0,2,1:T(8,128)(2,1)}, u32[]{:S(2)}, u32[]{:S(2)}) collective-permute-start(bf16[256,12,64]{0,2,1:T(8,128)(2,1)} %fusion.190), channel_id=1, source_target_pairs={{0,1},{1,2},{2,3},{3,4},{4,5},{5,6},{6,7},{7,0},{8,9},{9,10},{10,1... | collective-permute-start | bytes 1179656 | tf_op jit(solution)/shard_map/while/body/eval_jaxpr/ppermute | solution.py:18
  380.3 15.1 %collective-permute-start = (bf16[256,12,64]{0,2,1:T(8,128)(2,1)S(1)}, bf16[256,12,64]{0,2,1:T(8,128)(2,1)}, u32[]{:S(2)}, u32[]{:S(2)}) collective-permute-start(bf16[256,12,64]{0,2,1:T(8,128)(2,1)S(1)} %copy.76), channel_id=1, source_target_pairs={{0,1},{1,2},{2,3},{3,4},{4,5},{5,6},{6,7},{7,0},{8,9},{9,10},{10,1... | collective-permute-start | bytes 1179656 | tf_op jit(solution)/shard_map/while/body/eval_jaxpr/ppermute | solution.py:18
  380.3 19.3 %collective-permute-start.1 = (bf16[256,12,64]{0,2,1:T(8,128)(2,1)}, bf16[256,12,64]{0,2,1:T(8,128)(2,1)}, u32[]{:S(2)}, u32[]{:S(2)}) collective-permute-start(bf16[256,12,64]{0,2,1:T(8,128)(2,1)} %copy.77), channel_id=1, source_target_pairs={{0,1},{1,2},{2,3},{3,4},{4,5},{5,6},{6,7},{7,0},{8,9},{9,10},{10,1... | collective-permute-start | bytes 1179656 | tf_op jit(solution)/shard_map/while/body/eval_jaxpr/ppermute | solution.py:18
  410.9 15.0 %collective-permute-start = (bf16[256,12,64]{0,2,1:T(8,128)(2,1)S(1)}, bf16[256,12,64]{0,2,1:T(8,128)(2,1)}, u32[]{:S(2)}, u32[]{:S(2)}) collective-permute-start(bf16[256,12,64]{0,2,1:T(8,128)(2,1)S(1)} %copy.76), channel_id=1, source_target_pairs={{0,1},{1,2},{2,3},{3,4},{4,5},{5,6},{6,7},{7,0},{8,9},{9,10},{10,1... | collective-permute-start | bytes 1179656 | tf_op jit(solution)/shard_map/while/body/eval_jaxpr/ppermute | solution.py:18
  410.9 19.2 %collective-permute-start.1 = (bf16[256,12,64]{0,2,1:T(8,128)(2,1)}, bf16[256,12,64]{0,2,1:T(8,128)(2,1)}, u32[]{:S(2)}, u32[]{:S(2)}) collective-permute-start(bf16[256,12,64]{0,2,1:T(8,128)(2,1)} %copy.77), channel_id=1, source_target_pairs={{0,1},{1,2},{2,3},{3,4},{4,5},{5,6},{6,7},{7,0},{8,9},{9,10},{10,1... | collective-permute-start | bytes 1179656 | tf_op jit(solution)/shard_map/while/body/eval_jaxpr/ppermute | solution.py:18
  441.5 15.1 %collective-permute-start = (bf16[256,12,64]{0,2,1:T(8,128)(2,1)S(1)}, bf16[256,12,64]{0,2,1:T(8,128)(2,1)}, u32[]{:S(2)}, u32[]{:S(2)}) collective-permute-start(bf16[256,12,64]{0,2,1:T(8,128)(2,1)S(1)} %copy.76), channel_id=1, source_target_pairs={{0,1},{1,2},{2,3},{3,4},{4,5},{5,6},{6,7},{7,0},{8,9},{9,10},{10,1... | collective-permute-start | bytes 1179656 | tf_op jit(solution)/shard_map/while/body/eval_jaxpr/ppermute | solution.py:18
  441.5 19.3 %collective-permute-start.1 = (bf16[256,12,64]{0,2,1:T(8,128)(2,1)}, bf16[256,12,64]{0,2,1:T(8,128)(2,1)}, u32[]{:S(2)}, u32[]{:S(2)}) collective-permute-start(bf16[256,12,64]{0,2,1:T(8,128)(2,1)} %copy.77), channel_id=1, source_target_pairs={{0,1},{1,2},{2,3},{3,4},{4,5},{5,6},{6,7},{7,0},{8,9},{9,10},{10,1... | collective-permute-start | bytes 1179656 | tf_op jit(solution)/shard_map/while/body/eval_jaxpr/ppermute | solution.py:18
  472.0 15.1 %collective-permute-start = (bf16[256,12,64]{0,2,1:T(8,128)(2,1)S(1)}, bf16[256,12,64]{0,2,1:T(8,128)(2,1)}, u32[]{:S(2)}, u32[]{:S(2)}) collective-permute-start(bf16[256,12,64]{0,2,1:T(8,128)(2,1)S(1)} %copy.76), channel_id=1, source_target_pairs={{0,1},{1,2},{2,3},{3,4},{4,5},{5,6},{6,7},{7,0},{8,9},{9,10},{10,1... | collective-permute-start | bytes 1179656 | tf_op jit(solution)/shard_map/while/body/eval_jaxpr/ppermute | solution.py:18
  472.0 19.3 %collective-permute-start.1 = (bf16[256,12,64]{0,2,1:T(8,128)(2,1)}, bf16[256,12,64]{0,2,1:T(8,128)(2,1)}, u32[]{:S(2)}, u32[]{:S(2)}) collective-permute-start(bf16[256,12,64]{0,2,1:T(8,128)(2,1)} %copy.77), channel_id=1, source_target_pairs={{0,1},{1,2},{2,3},{3,4},{4,5},{5,6},{6,7},{7,0},{8,9},{9,10},{10,1... | collective-permute-start | bytes 1179656 | tf_op jit(solution)/shard_map/while/body/eval_jaxpr/ppermute | solution.py:18
  502.6 10.9 %collective-permute-start.3 = (bf16[256,12,64]{0,2,1:T(8,128)(2,1)}, bf16[256,12,64]{0,2,1:T(8,128)(2,1)}, u32[]{:S(2)}, u32[]{:S(2)}) collective-permute-start(bf16[256,12,64]{0,2,1:T(8,128)(2,1)} %fusion.190), channel_id=1, source_target_pairs={{0,1},{1,2},{2,3},{3,4},{4,5},{5,6},{6,7},{7,0},{8,9},{9,10},{10,1... | collective-permute-start | bytes 1179656 | tf_op jit(solution)/shard_map/while/body/eval_jaxpr/ppermute | solution.py:18
  502.6 15.1 %collective-permute-start = (bf16[256,12,64]{0,2,1:T(8,128)(2,1)S(1)}, bf16[256,12,64]{0,2,1:T(8,128)(2,1)}, u32[]{:S(2)}, u32[]{:S(2)}) collective-permute-start(bf16[256,12,64]{0,2,1:T(8,128)(2,1)S(1)} %copy.76), channel_id=1, source_target_pairs={{0,1},{1,2},{2,3},{3,4},{4,5},{5,6},{6,7},{7,0},{8,9},{9,10},{10,1... | collective-permute-start | bytes 1179656 | tf_op jit(solution)/shard_map/while/body/eval_jaxpr/ppermute | solution.py:18
  502.6 19.3 %collective-permute-start.1 = (bf16[256,12,64]{0,2,1:T(8,128)(2,1)}, bf16[256,12,64]{0,2,1:T(8,128)(2,1)}, u32[]{:S(2)}, u32[]{:S(2)}) collective-permute-start(bf16[256,12,64]{0,2,1:T(8,128)(2,1)} %copy.77), channel_id=1, source_target_pairs={{0,1},{1,2},{2,3},{3,4},{4,5},{5,6},{6,7},{7,0},{8,9},{9,10},{10,1... | collective-permute-start | bytes 1179656 | tf_op jit(solution)/shard_map/while/body/eval_jaxpr/ppermute | solution.py:18
  533.1 10.9 %collective-permute-start.3 = (bf16[256,12,64]{0,2,1:T(8,128)(2,1)}, bf16[256,12,64]{0,2,1:T(8,128)(2,1)}, u32[]{:S(2)}, u32[]{:S(2)}) collective-permute-start(bf16[256,12,64]{0,2,1:T(8,128)(2,1)} %fusion.190), channel_id=1, source_target_pairs={{0,1},{1,2},{2,3},{3,4},{4,5},{5,6},{6,7},{7,0},{8,9},{9,10},{10,1... | collective-permute-start | bytes 1179656 | tf_op jit(solution)/shard_map/while/body/eval_jaxpr/ppermute | solution.py:18
  533.1 15.1 %collective-permute-start = (bf16[256,12,64]{0,2,1:T(8,128)(2,1)S(1)}, bf16[256,12,64]{0,2,1:T(8,128)(2,1)}, u32[]{:S(2)}, u32[]{:S(2)}) collective-permute-start(bf16[256,12,64]{0,2,1:T(8,128)(2,1)S(1)} %copy.76), channel_id=1, source_target_pairs={{0,1},{1,2},{2,3},{3,4},{4,5},{5,6},{6,7},{7,0},{8,9},{9,10},{10,1... | collective-permute-start | bytes 1179656 | tf_op jit(solution)/shard_map/while/body/eval_jaxpr/ppermute | solution.py:18
  533.1 19.3 %collective-permute-start.1 = (bf16[256,12,64]{0,2,1:T(8,128)(2,1)}, bf16[256,12,64]{0,2,1:T(8,128)(2,1)}, u32[]{:S(2)}, u32[]{:S(2)}) collective-permute-start(bf16[256,12,64]{0,2,1:T(8,128)(2,1)} %copy.77), channel_id=1, source_target_pairs={{0,1},{1,2},{2,3},{3,4},{4,5},{5,6},{6,7},{7,0},{8,9},{9,10},{10,1... | collective-permute-start | bytes 1179656 | tf_op jit(solution)/shard_map/while/body/eval_jaxpr/ppermute | solution.py:18
  559.5 133.5 %all-reduce.20.cloned.1.call-start = ((), (), s32[]{:S(2)}) async-start(), calls=%async_computation.14 | async-start | bytes 7077888 | tf_op jit(solution)/shard_map/psum | solution.py:295
  (96 other events, 1218.4 us)
Sparse Core Ops, SparseCore 0:
  9.9 50.0 all-gather.9
  68.5 39.1 all-gather.11
  109.9 39.1 all-gather.19
  150.8 55.2 all-gather.15
  207.8 57.0 all-gather.17
  266.6 27.7 all-gather.13
  297.3 28.5 reduce-scatter.6
  328.8 57.0 reduce-scatter.8
  388.9 57.0 reduce-scatter.10
  559.6 44.8 reduce-scatter.4
  607.1 85.8 all-reduce.19
where the time goes:
time: 711 us; the launch traced here: 707 us
  waiting for transfers between devices  329 us (46%)
  matrix products  151 us (21%)
  blocking collectives  69.9 us (10%)
  other arithmetic  63.4 us (9%)
  local copies, waits for them, and re-layouts  62.1 us (9%)
  between operations  17.8 us (3%)
  loops' own time  8.68 us (1%)
    ppermute x32, waiting for transfers between devices, from_behind(): return lax.ppermute(x, axis, [(i, (i + by) % size) for i in range(size)])  113 us
    psum x1, waiting for transfers between devices, on_device(): lax.psum(shares[0].astype(jnp.bfloat16), 'ctx').astype(jnp.float32)  45.3 us
    all_gather x1, waiting for transfers between devices, on_device(): value_piece = lax.all_gather(values, 'ctx', axis=0, tiled=True)  41.4 us
    all_gather x1, waiting for transfers between devices, on_device(): lax.all_gather(down_weight, 'fsdp', axis=0, tiled=True)  38.2 us
    reduce_scatter x1, waiting for transfers between devices, on_device(): lax.psum_scatter(in_weight_part.astype(jnp.bfloat16), 'fsdp', scatter_dim...  34.4 us
    unnamed x2, blocking collectives  33.7 us
    while x108, local copies, waits for them, and re-layouts  31 us
    all_gather x1, waiting for transfers between devices, on_device(): lax.all_gather(in_weight, 'fsdp', axis=0, tiled=True)  22.8 us
  transfers between devices with their start and end apart: 43, of which 39 were waited for; matrix products, arithmetic and copies ran while one was open for 35% of the time, Pallas kernels for 0%

commit v1 on v0

v1 whole, which is shorter than its diff:
```python
import functools
import math

import jax
import jax.numpy as jnp
from jax import lax
from jax.experimental import pallas as pl
from jax.experimental.pallas import tpu as pltpu
from jax.sharding import PartitionSpec as P

HEAD = 64
ROT = 16
HALF = ROT // 2
RUN = 128
TILE = 256
NEG = -1e30
EPS = 1e-05
BF = jnp.bfloat16
F32 = jnp.float32
VMEM_LIMIT = 60 * 1024 * 1024


def mm(left, right, dims):
    return lax.dot_general(left, right, ((dims[:1], dims[1:]), ((), ())), preferred_element_type=F32)


def flip(x):
    return x.astype(F32).T.astype(x.dtype)


def normalize(values):
    mean = jnp.mean(values, -1, keepdims=True)
    centred = values - mean
    spread = jnp.mean(centred * centred, -1, keepdims=True)
    inverse = lax.rsqrt(spread + EPS)
    return centred * inverse, inverse


def turn(values, cosine, sine):
    one, two = values[:HALF], values[HALF:ROT]
    return jnp.concatenate([one * cosine - two * sine, two * cosine + one * sine, values[ROT:]], 0)


def ff_kernel(x_ref, g_ref, up_ref, down_ref, upb_ref, gain_ref, shift_ref,
              out_ref, back_ref, dup_ref, ddown_ref, dbias_ref, dgain_ref, dshift_ref,
              acc_up, acc_down):
    step = pl.program_id(0)

    @pl.when(step == 0)
    def _():
        acc_up[...] = jnp.zeros_like(acc_up)
        acc_down[...] = jnp.zeros_like(acc_down)
        dbias_ref[...] = jnp.zeros_like(dbias_ref)
        dgain_ref[...] = jnp.zeros_like(dgain_ref)
        dshift_ref[...] = jnp.zeros_like(dshift_ref)

    xhat, _ = normalize(x_ref[0].astype(F32))
    second = (xhat * gain_ref[...] + shift_ref[...]).astype(BF)
    up = mm(second, up_ref[...], (1, 0)) + upb_ref[...]
    phi = 0.5 * (1.0 + lax.erf(up * (1.0 / math.sqrt(2.0))))
    active = (up * phi).astype(BF)
    slope = phi + up * jnp.exp(-0.5 * up * up) * (1.0 / math.sqrt(2.0 * math.pi))
    out_ref[0] = mm(active, down_ref[...], (1, 0)).astype(BF)
    grad = g_ref[0]
    back_up = mm(grad, down_ref[...], (1, 1)) * slope
    low_up = back_up.astype(BF)
    dbias_ref[...] += jnp.sum(low_up.astype(F32), 0, keepdims=True)
    acc_up[...] += mm(second, low_up, (0, 0))
    acc_down[...] += mm(active, grad, (0, 0))
    back = mm(low_up, up_ref[...], (1, 1))
    dgain_ref[...] += jnp.sum(back * xhat, 0, keepdims=True)
    dshift_ref[...] += jnp.sum(back, 0, keepdims=True)
    back_ref[0] = (back * gain_ref[...]).astype(BF)

    @pl.when(step == pl.num_programs(0) - 1)
    def _():
        dup_ref[...] = acc_up[...].astype(BF)
        ddown_ref[...] = acc_down[...].astype(BF)


def whole(shape):
    return pl.BlockSpec(shape, lambda *_: (0,) * len(shape))


def feed_forward(x, grad, up, down, up_bias, gain, shift):
    groups, tokens, width = x.shape
    hidden = up.shape[1]
    tile = pl.BlockSpec((1, tokens, width), lambda i: (i, 0, 0))
    row = jax.ShapeDtypeStruct((1, width), F32)
    return pl.pallas_call(
        ff_kernel,
        grid=(groups,),
        in_specs=[tile, tile, whole((width, hidden)), whole((hidden, width)), whole((1, hidden)),
                  whole((1, width)), whole((1, width))],
        out_specs=[tile, tile, whole((width, hidden)), whole((hidden, width)), whole((1, hidden)),
                   whole((1, width)), whole((1, width))],
        out_shape=[jax.ShapeDtypeStruct(x.shape, BF), jax.ShapeDtypeStruct(x.shape, BF),
                   jax.ShapeDtypeStruct((width, hidden), BF), jax.ShapeDtypeStruct((hidden, width), BF),
                   jax.ShapeDtypeStruct((1, hidden), F32), row, row],
        scratch_shapes=[pltpu.VMEM((width, hidden), F32), pltpu.VMEM((hidden, width), F32)],
        compiler_params=pltpu.CompilerParams(vmem_limit_bytes=VMEM_LIMIT),
        name="feed_forward",
    )(x, grad, up, down, up_bias, gain, shift)


def qkv_kernel(order_ref, xa_ref, xb_ref, w_ref, bias_ref, gain_ref, shift_ref, cos_ref, sin_ref, out_ref):
    values = jnp.concatenate([xa_ref[0], xb_ref[0]], 0).astype(F32)
    xhat, _ = normalize(values)
    first = (xhat * gain_ref[...] + shift_ref[...]).astype(BF)
    proj = mm(w_ref[...], first, (1, 1)) + bias_ref[...]
    heads = out_ref.shape[0] // 3
    cosine, sine = cos_ref[0], sin_ref[0]
    for i in range(3 * heads):
        part = proj[i * HEAD:(i + 1) * HEAD]
        if i < 2 * heads:
            part = turn(part, cosine, sine)
        part = part.astype(BF)
        if i < heads:
            part = part * jnp.asarray(1.0 / math.sqrt(HEAD), BF)
        out_ref[i, 0] = part


def run_specs(width):
    return [pl.BlockSpec((1, RUN, width), lambda i, order, k=k: (order[2 * i + k], 0, 0)) for k in (0, 1)]


def project(order, x, w, bias, gain, shift, cosine, sine):
    runs, _, width = x.shape
    rows = w.shape[0]
    tiles = runs // 2
    parts = rows // HEAD
    table = pl.BlockSpec((1, HALF, TILE), lambda i, order: (i, 0, 0))
    return pl.pallas_call(
        qkv_kernel,
        grid_spec=pltpu.PrefetchScalarGridSpec(
            num_scalar_prefetch=1,
            grid=(tiles,),
            in_specs=run_specs(width) + [whole((rows, width)), whole((rows, 1)), whole((1, width)),
                                         whole((1, width)), table, table],
            out_specs=pl.BlockSpec((parts, 1, HEAD, TILE), lambda i, order: (0, i, 0, 0)),
        ),
        out_shape=jax.ShapeDtypeStruct((parts, tiles, HEAD, TILE), BF),
        compiler_params=pltpu.CompilerParams(vmem_limit_bytes=VMEM_LIMIT),
        name="project",
    )(order, x, x, w, bias, gain, shift, cosine, sine)


def attention_kernel(share, place_ref, q_ref, k_ref, v_ref, da_ref, db_ref, cos_ref, sin_ref,
                     mix_ref, back_ref, keys, values, dkeys, dvalues, sbuf, pbuf):
    head, step = pl.program_id(0), pl.program_id(1)
    heads, steps = pl.num_programs(0), pl.num_programs(1)
    tiles = k_ref.shape[1]
    block = share(step, place_ref)

    @pl.when((head == 0) & (step == 0))
    def _():
        mix_ref[...] = jnp.zeros_like(mix_ref)
        back_ref[...] = jnp.zeros_like(back_ref)

    @pl.when(step == 0)
    def _():
        @pl.loop(0, tiles)
        def _(j):
            keys[j] = flip(k_ref[0, j])
            values[j] = flip(v_ref[0, j])
            dkeys[j] = jnp.zeros((TILE, HEAD), F32)
            dvalues[j] = jnp.zeros((TILE, HEAD), F32)

    query = q_ref[0, 0]

    def fold(x, op):
        return op(x.reshape(TILE // 8, 8, TILE), 0)

    def score(j, peak):
        s = mm(keys[j], query, (1, 0))
        sbuf[j] = s
        return jnp.maximum(peak, fold(s, jnp.max))

    peak = lax.fori_loop(0, block, score, jnp.full((8, TILE), NEG, F32))
    s = mm(keys[block], query, (1, 0))
    key_at = lax.broadcasted_iota(jnp.int32, (TILE, TILE), 0)
    query_at = lax.broadcasted_iota(jnp.int32, (TILE, TILE), 1)
    s = jnp.where(key_at <= query_at, s, NEG)
    sbuf[block] = s
    peak = jnp.maximum(peak, fold(s, jnp.max))
    peak = jnp.max(peak, 0, keepdims=True)

    def weigh(j, carry):
        total, mixed = carry
        p = jnp.exp(sbuf[j] - peak)
        low = p.astype(BF)
        pbuf[j] = low
        return total + fold(p, jnp.sum), mixed + mm(v_ref[0, j], low, (1, 0))

    total, mixed = lax.fori_loop(
        0, block + 1, weigh, (jnp.zeros((8, TILE), F32), jnp.zeros((HEAD, TILE), F32)))
    inverse = 1.0 / jnp.sum(total, 0, keepdims=True)
    mixed = mixed * inverse
    low_mixed = mixed.astype(BF)
    for k in (0, 1):
        at = place_ref[1 + 2 * block + k]
        mix_ref[at // 2, head, at % 2] = low_mixed[:, k * RUN:(k + 1) * RUN]
    back = jnp.concatenate([da_ref[0], db_ref[0]], 1).astype(F32) * inverse
    spread = jnp.sum(back * mixed, 0, keepdims=True)
    back = back.astype(BF)
    back_rows = flip(back)
    query_rows = flip(query)

    def pull(j, dquery):
        low = pbuf[j]
        dp = mm(values[j], back, (1, 0))
        ds = (low.astype(F32) * (dp - spread)).astype(BF)
        dvalues[j] += mm(low, back_rows, (1, 0))
        dkeys[j] += mm(ds, query_rows, (1, 0))
        return dquery + mm(k_ref[0, j], ds, (1, 0))

    dquery = lax.fori_loop(0, block + 1, pull, jnp.zeros((HEAD, TILE), F32))
    dquery = dquery * (1.0 / math.sqrt(HEAD))
    back_ref[head, block] = turn(dquery, cos_ref[block], -sin_ref[block]).astype(BF)

    @pl.when(step == steps - 1)
    def _():
        @pl.loop(0, tiles)
        def _(j):
            back_ref[heads + head, j] = turn(dkeys[j].T, cos_ref[j], -sin_ref[j]).astype(BF)
            back_ref[2 * heads + head, j] = dvalues[j].T.astype(BF)


def attend(place, qkv, back, cosine, sine, sharers):
    parts, tiles, _, _ = qkv.shape
    heads = parts // 3
    owners = back.shape[0]
    steps = tiles // sharers

    def share(step, place_ref):
        return 2 * sharers * (step // 2) + jnp.where(step % 2 == 0, place_ref[0], 2 * sharers - 1 - place_ref[0])

    def run_of(h, n, place_ref, k):
        at = place_ref[1 + 2 * share(n, place_ref) + k]
        return at // 2, h, at % 2

    all_tiles = (1, tiles, HEAD, TILE)
    return pl.pallas_call(
        functools.partial(attention_kernel, share),
        grid_spec=pltpu.PrefetchScalarGridSpec(
            num_scalar_prefetch=1,
            grid=(heads, steps),
            in_specs=[
                pl.BlockSpec((1, 1, HEAD, TILE), lambda h, n, p: (h, share(n, p), 0, 0)),
                pl.BlockSpec(all_tiles, lambda h, n, p: (heads + h, 0, 0, 0)),
                pl.BlockSpec(all_tiles, lambda h, n, p: (2 * heads + h, 0, 0, 0)),
                pl.BlockSpec((1, HEAD, RUN), lambda h, n, p: run_of(h, n, p, 0)),
                pl.BlockSpec((1, HEAD, RUN), lambda h, n, p: run_of(h, n, p, 1)),
                whole((tiles, HALF, TILE)),
                whole((tiles, HALF, TILE)),
            ],
            out_specs=[whole((owners, heads, 2, HEAD, RUN)), whole((parts, tiles, HEAD, TILE))],
            scratch_shapes=[
                pltpu.VMEM((tiles, TILE, HEAD), BF),
                pltpu.VMEM((tiles, TILE, HEAD), BF),
                pltpu.VMEM((tiles, TILE, HEAD), F32),
                pltpu.VMEM((tiles, TILE, HEAD), F32),
                pltpu.VMEM((tiles, TILE, TILE), F32),
                pltpu.VMEM((tiles, TILE, TILE), BF),
            ],
        ),
        out_shape=[jax.ShapeDtypeStruct((owners, heads, 2, HEAD, RUN), BF),
                   jax.ShapeDtypeStruct((parts, tiles, HEAD, TILE), BF)],
        compiler_params=pltpu.CompilerParams(vmem_limit_bytes=VMEM_LIMIT),
        name="attend",
    )(place, qkv, qkv, qkv, back, back, cosine, sine)


def back_kernel(order_ref, b_ref, w_ref, xa_ref, xb_ref, gain_ref, shift_ref,
                e_ref, dw_ref, dbias_ref, dgain_ref, dshift_ref, acc):
    step = pl.program_id(0)

    @pl.when(step == 0)
    def _():
        acc[...] = jnp.zeros_like(acc)
        dbias_ref[...] = jnp.zeros_like(dbias_ref)
        dgain_ref[...] = jnp.zeros_like(dgain_ref)
        dshift_ref[...] = jnp.zeros_like(dshift_ref)

    values = jnp.concatenate([xa_ref[0], xb_ref[0]], 0).astype(F32)
    xhat, _ = normalize(values)
    first = (xhat * gain_ref[...] + shift_ref[...]).astype(BF)
    rows = b_ref.shape[0] * HEAD
    back = b_ref[...].reshape(rows, TILE)
    acc[...] += mm(back, first, (1, 0))
    dbias_ref[...] += jnp.sum(back.astype(F32), 1, keepdims=True)
    e = mm(back, w_ref[...], (0, 0))
    dgain_ref[...] += jnp.sum(e * xhat, 0, keepdims=True)
    dshift_ref[...] += jnp.sum(e, 0, keepdims=True)
    e = (e * gain_ref[...]).astype(BF)
    e_ref[order_ref[2 * step]] = e[:RUN]
    e_ref[order_ref[2 * step + 1]] = e[RUN:]

    @pl.when(step == pl.num_programs(0) - 1)
    def _():
        dw_ref[...] = acc[...].T.astype(BF)


def project_back(order, back, w, x, gain, shift):
    runs, _, width = x.shape
    rows = w.shape[0]
    parts, tiles, _, _ = back.shape
    line = jax.ShapeDtypeStruct((1, width), F32)
    return pl.pallas_call(
        back_kernel,
        grid_spec=pltpu.PrefetchScalarGridSpec(
            num_scalar_prefetch=1,
            grid=(tiles,),
            in_specs=[pl.BlockSpec((parts, 1, HEAD, TILE), lambda i, order: (0, i, 0, 0)), whole((rows, width))]
            + run_specs(width) + [whole((1, width)), whole((1, width))],
            out_specs=[whole((runs, RUN, width)), whole((width, rows)), whole((rows, 1)), whole((1, width)),
                       whole((1, width))],
            scratch_shapes=[pltpu.VMEM((rows, width), F32)],
        ),
        out_shape=[jax.ShapeDtypeStruct((runs, RUN, width), BF), jax.ShapeDtypeStruct((width, rows), BF),
                   jax.ShapeDtypeStruct((rows, 1), F32), line, line],
        compiler_params=pltpu.CompilerParams(vmem_limit_bytes=VMEM_LIMIT),
        name="project_back",
    )(order, back, w, x, x, gain, shift)


def spread_out(pieces, axis, groups=None):
    return lax.all_to_all(pieces, axis, 0, 0, axis_index_groups=groups)


def to_all(x, axis, groups=None, count=None):
    count = count or lax.axis_size(axis)
    return spread_out(jnp.broadcast_to(x[None], (count,) + x.shape), axis, groups)


def on_device(
    inputs, positions, in_weight, in_bias, out_weight, out_bias, up_weight, up_bias, down_weight, down_bias,
    first_gain, first_shift, second_gain, second_shift, out_grad,
):
    x, grad, place = inputs[0], out_grad[0], positions[0]
    tokens, width = x.shape
    owners, shards = lax.axis_size("ctx"), lax.axis_size("fsdp")
    here, shard = lax.axis_index("ctx"), lax.axis_index("fsdp")
    heads = width // HEAD
    groups = math.gcd(heads, owners // 2)
    sharers = owners // groups
    own_heads = heads // groups
    cols = own_heads * HEAD
    group, sharer, core = here // sharers, here % sharers, here % 2
    hidden = down_weight.shape[0]
    rows = in_weight.shape[0]
    half = rows // 2
    length = tokens * owners
    tiles = length // TILE
    parity = [[i for i in range(owners) if i % 2 == k] for k in (0, 1)]
    pairs = [(i, i ^ 1) for i in range(owners)]

    def swap(value):
        return lax.ppermute(value, "ctx", pairs)

    def both(mine, other):
        return jnp.stack([jnp.where(core == 0, mine, other), jnp.where(core == 0, other, mine)], 1)

    x_all = lax.all_gather(x, "ctx", axis=0, tiled=True)

    smalls = [in_bias, out_bias, down_bias, first_gain, first_shift, second_gain, second_shift]
    sizes = [s.shape[0] for s in smalls]
    packed = jnp.concatenate(smalls)
    small_rows = -(-packed.shape[0] // hidden)
    packed = jnp.pad(packed, (0, small_rows * hidden - packed.shape[0])).reshape(small_rows, hidden)

    def own_half(value):
        return lax.dynamic_slice_in_dim(value, core * half, half, 0)

    up_pieces = own_half(up_weight).reshape(half, shards, hidden).transpose(1, 0, 2)
    packed = jnp.broadcast_to(packed[None], (shards, small_rows, hidden))
    up_got = spread_out(jnp.concatenate([up_pieces, packed], 1), "fsdp")
    x_plane = to_all(x, "fsdp")
    grad_plane = to_all(grad, "fsdp")
    in_own = own_half(in_weight).reshape(half, 3, groups, cols)
    in_own = lax.dynamic_index_in_dim(in_own, group, 2, keepdims=False).reshape(half, 3 * cols)
    in_own = jnp.pad(in_own, ((0, 0), (0, width - 3 * cols)))
    io_got = to_all(jnp.concatenate([own_half(out_weight), in_own], 0), "fsdp")

    up_own, small_got = up_got[:, :half], up_got[:, half:].reshape(shards, -1)
    up_full = both(up_own, swap(up_own)).reshape(width, hidden)
    small, at = [], 0
    for size in sizes:
        small.append(small_got[:, at:at + size].reshape(-1).astype(F32))
        at += size
    full_in_bias, full_out_bias, full_down_bias, gain_one, shift_one, gain_two, shift_two = small

    out_part, back_part, up_part, down_part, up_bias_part, gain_two_part, shift_two_part = feed_forward(
        x_plane, grad_plane, up_full, down_weight, up_bias.astype(F32)[None], gain_two[None], shift_two[None])
    ff_got = spread_out(jnp.concatenate([out_part, back_part], 1), "fsdp")
    ff_sum = jnp.sum(ff_got.astype(F32), 0)

    small_step = rows // owners
    up_pieces = up_part.reshape(shards, owners, small_step, hidden).transpose(1, 0, 2, 3)
    up_pieces = up_pieces.reshape(owners, shards * small_step, hidden)
    down_pieces = down_part.reshape(owners, hidden // owners, width)
    joined = hidden == width

    def joint(values, call):
        if not joined:
            return [call(v) for v in values]
        got = call(jnp.concatenate(values, -2))
        cut = values[0].shape[-2]
        return [got[..., :cut, :], got[..., cut:, :]]

    up_sum, down_sum = joint(
        [up_pieces, down_pieces], lambda v: lax.psum_scatter(v, "ctx", scatter_dimension=0, tiled=False))
    up_sum = spread_out(up_sum.reshape(shards, small_step, hidden), "fsdp").reshape(shards * small_step, hidden)

    def gather_owners(value):
        mine = to_all(value, "ctx", parity, owners // 2)
        return both(mine, swap(mine)).reshape((owners,) + value.shape)

    up_all, down_all = joint([up_sum, down_sum], gather_owners)
    up_weight_gradient = up_all.reshape(owners, shards, small_step, hidden).transpose(0, 2, 1, 3)
    up_weight_gradient = up_weight_gradient.reshape(rows, shards * hidden).astype(F32)
    down_weight_gradient = down_all.reshape(hidden, width).astype(F32)

    io_full = both(io_got, swap(io_got)).reshape(shards, 2, 2, half, width)
    out_full = io_full[:, :, 0].reshape(width, width)
    in_full = io_full[:, :, 1].reshape(width, width)[:, :3 * cols].T
    back_mixed = mm(out_full, grad, (1, 1)).astype(BF).reshape(groups, 1, cols, tokens)
    back_mixed = jnp.broadcast_to(back_mixed, (groups, sharers, cols, tokens)).reshape(owners, cols, tokens)
    run_rows = jnp.broadcast_to((place // RUN).astype(BF)[None, None], (owners, 8, tokens))
    back_got = spread_out(jnp.concatenate([back_mixed, run_rows], 1), "ctx")
    run_at = back_got[:, cols, ::RUN].reshape(-1).astype(jnp.int32)
    runs = run_at.shape[0]
    at_run = lax.broadcasted_iota(jnp.int32, (runs, runs), 0)
    of_run = lax.broadcasted_iota(jnp.int32, (runs, runs), 1)
    order = jnp.sum(jnp.where(run_at[None] == at_run, of_run, 0), 1)

    ladder = 10000.0 ** (-jnp.arange(0, ROT, 2, dtype=F32) / ROT)
    angle = jnp.arange(length, dtype=jnp.int32).astype(F32).reshape(tiles, 1, TILE) * ladder[None, :, None]
    cosine, sine = jnp.cos(angle), jnp.sin(angle)

    x_runs = x_all.reshape(runs, RUN, width)
    bias_own = lax.dynamic_index_in_dim(full_in_bias.reshape(3, groups, cols), group, 1, keepdims=False)
    qkv = project(order, x_runs, in_full, bias_own.reshape(-1, 1), gain_one[None], shift_one[None], cosine, sine)
    spots = jnp.concatenate([sharer[None].astype(jnp.int32), order])
    mixed_out, back_qkv = attend(spots, qkv, back_got, cosine, sine, sharers)
    e_runs, in_part, in_bias_part, gain_one_part, shift_one_part = project_back(
        order, back_qkv, in_full, x_runs, gain_one[None], shift_one[None])
    e_sum = lax.psum_scatter(e_runs.reshape(length, width), "ctx", scatter_dimension=0, tiled=True)

    mixed_got = spread_out(mixed_out, "ctx").astype(F32)
    mixed = jnp.sum(mixed_got.reshape(groups, sharers, own_heads, 2, HEAD, RUN), 1)
    mixed = mixed.transpose(0, 1, 3, 2, 4).reshape(width, tokens).astype(BF)
    branch = mm(mixed, out_full, (0, 0))
    out_part = mm(mixed, grad, (1, 0)).astype(BF)

    x32, grad32 = x.astype(F32), grad.astype(F32)
    output = x32 + (branch + full_out_bias) + (ff_sum[:tokens] + full_down_bias)

    in_bias_full = lax.dynamic_update_slice_in_dim(
        jnp.zeros((3, groups, cols), F32), in_bias_part.reshape(3, 1, cols), group, 1)
    lines = [in_bias_full.reshape(-1), jnp.sum(grad32, 0), gain_one_part[0], shift_one_part[0], gain_two_part[0],
             shift_two_part[0]]
    lines = [v.reshape(shards, -1) for v in lines]
    mine = (jnp.arange(shards) == shard)[:, None]
    lines.append(jnp.where(mine, up_bias_part, 0.0))
    line_sizes = [v.shape[1] for v in lines]
    lines = jnp.concatenate(lines, 1).astype(BF).reshape(shards, 2, -1, width - 3 * cols)
    line_rows = lines.shape[2]
    lines = jnp.pad(lines, ((0, 0), (0, 0), (0, half - line_rows), (0, 0)))
    in_pieces = jnp.concatenate([in_part.reshape(shards, 2, half, 3 * cols), lines], 3)
    pieces = jnp.concatenate([out_part.reshape(shards, 2, half, width), in_pieces], 2)
    keep = lax.dynamic_index_in_dim(pieces, core, 1, keepdims=False)
    give = lax.dynamic_index_in_dim(pieces, 1 - core, 1, keepdims=False)
    pieces = (keep.astype(F32) + swap(give).astype(F32)).astype(BF)
    pieces = jnp.sum(spread_out(pieces, "fsdp").astype(F32), 0).astype(BF)
    gathered = gather_owners(pieces).astype(F32).reshape(groups, sharers // 2, 2, 2, half, width)
    out_weight_gradient = jnp.sum(gathered[:, :, :, 0], (0, 1)).reshape(rows, width)
    in_sum = jnp.sum(gathered[:, :, :, 1], 1)
    in_weight_gradient = in_sum[..., :3 * cols].reshape(groups, rows, 3, cols).transpose(1, 2, 0, 3)
    in_weight_gradient = in_weight_gradient.reshape(rows, 3 * width)
    line_sum = jnp.sum(in_sum[:, :, :line_rows, 3 * cols:], 0).reshape(-1)
    totals, at = [], 0
    for size in line_sizes:
        totals.append(line_sum[at:at + size])
        at += size

    e = e_sum.astype(F32) + ff_sum[tokens:]
    xhat, inverse = normalize(x32)
    input_gradient = grad32 + inverse * (
        e - jnp.mean(e, -1, keepdims=True) - xhat * jnp.mean(e * xhat, -1, keepdims=True))
    return (
        output.astype(BF)[None], input_gradient[None], in_weight_gradient, totals[0], out_weight_gradient, totals[1],
        up_weight_gradient, totals[6], down_weight_gradient, totals[1], totals[2], totals[3], totals[4], totals[5],
    )


def solution(mesh):
    token, matrix, vector = P("fsdp", "ctx", None), P("fsdp", None), P("fsdp")
    return jax.shard_map(
        on_device,
        mesh=mesh,
        in_specs=(token, P("fsdp", "ctx"), matrix, vector, matrix, vector, matrix, vector, matrix, vector,
                  vector, vector, vector, vector, token),
        out_specs=(token, token, matrix, vector, matrix, vector, matrix, vector, matrix, vector,
                   vector, vector, vector, vector),
        check_vma=False,
    )
```

time: 711 us -> 448 us (0.63)
  waiting for transfers between devices: 329 us -> 159 us
  matrix products: 151 us -> 2.3 us
  Pallas kernels: 0 us -> 86.3 us
  starting transfers between devices: 5.51 us -> 30.9 us
  other arithmetic: 63.4 us -> 39.9 us
  blocking collectives: 69.9 us -> 54 us
  loops' own time: 8.68 us -> 0 us
    dot_general x60 -> x3, matrix products: 151 us -> 2.3 us  [mm(): lax.dot_general(left, right, ((dims[:1], dims[1:]), ((), ())), preferred_...]
    all_to_all x0 -> x8, waiting for transfers between devices: none -> 135 us  [spread_out(): return lax.all_to_all(pieces, axis, 0, 0, axis_index_groups=groups)]
    all_gather x6 -> x1, waiting for transfers between devices: 134 us -> 17.4 us  [on_device(): x_all = lax.all_gather(x, 'ctx', axis=0, tiled=True)]
    ppermute x32 -> x5, waiting for transfers between devices: 113 us -> 6.18 us  [swap(): return lax.ppermute(value, 'ctx', pairs)]
    pallas_call x0 -> x4, Pallas kernels: none -> 86.3 us  [the longest x1 48.9 us: attend(): pl.pallas_call(functools.partial(attention_kernel, share), grid_spec=pltp...]
    all_to_all x0 -> x3, blocking collectives: none -> 54 us  [spread_out(): return lax.all_to_all(pieces, axis, 0, 0, axis_index_groups=groups)]
    psum x1 -> x0, waiting for transfers between devices: 45.3 us -> none  [on_device(): lax.psum(shares[0].astype(jnp.bfloat16), 'ctx').astype(jnp.float32)]
    reduce_scatter x4 -> x2, waiting for transfers between devices: 34.5 us -> 0.02 us  [the longest x1 0.02 us: on_device(): lax.psum_scatter(v, 'ctx', scatter_dimension=0, tiled=False)]
  transfers between devices with their start and end apart: 43 -> 16, of which waited for: 39 -> 11; matrix products, arithmetic and copies ran while one was open for 35% -> 10% of each run, Pallas kernels for 0% -> 16%
where the time goes in v1:
time: 448 us; the launch traced here: 446 us
  waiting for transfers between devices  159 us (35%)
  Pallas kernels  86.3 us (19%)
  local copies, waits for them, and re-layouts  58.9 us (13%)
  blocking collectives  54 us (12%)
  other arithmetic  39.9 us (9%)
  starting transfers between devices  30.9 us (7%)
  between operations  14.4 us (3%)
    all_to_all x8, waiting for transfers between devices, spread_out(): return lax.all_to_all(pieces, axis, 0, 0, axis_index_groups=groups)  135 us
    all_to_all x3, blocking collectives, spread_out(): return lax.all_to_all(pieces, axis, 0, 0, axis_index_groups=groups)  54 us
    pallas_call x1, Pallas kernels, attend(): pl.pallas_call(functools.partial(attention_kernel, share), grid_spec=pltp...  48.9 us
    all_to_all x8, starting transfers between devices, spread_out(): return lax.all_to_all(pieces, axis, 0, 0, axis_index_groups=groups)  30.7 us
    all_gather x1, waiting for transfers between devices, on_device(): x_all = lax.all_gather(x, 'ctx', axis=0, tiled=True)  17.4 us
    pallas_call x1, Pallas kernels, feed_forward(): pl.pallas_call(ff_kernel, grid=(groups,), in_specs=[tile, tile, whole((wi...  13.9 us
    pallas_call x1, Pallas kernels, project_back(): pl.pallas_call(back_kernel, grid_spec=pltpu.PrefetchScalarGridSpec(num_sc...  13.5 us
    another operation x4, local copies, waits for them, and re-layouts, both(): jnp.stack([jnp.where(core == 0, mine, other), jnp.where(core == 0, other,...  12.4 us
  transfers between devices with their start and end apart: 16, of which 11 were waited for; matrix products, arithmetic and copies ran while one was open for 10% of the time, Pallas kernels for 16%

profile of v1, /device:TPU:0, one launch (start us, length us, event | category | flops | bytes accessed | tf_op | source)
XLA Modules:
  0.0 446.1 jit_solution(4954080243680932697)
XLA Ops:
  7.2 4.9 %concatenate.45 = bf16[1728]{0:T(1024)(128)(2,1)S(1)} concatenate(bf16[576]{0:T(1024)(128)(2,1)} %param.18, bf16[192]{0:T(256)(128)(2,1)} %param.20, bf16[192]{0:T(256)(128)(2,1)} %param.24, bf16[192]{0:T(256)(128)(2,1)} %param.25, bf16[192]{0:T(256)(128)(2,1)} %param.26, bf16[192]{0:T(256)(128)(2,1)} %param.27, bf16[192]{0:T(256)(128)(2,1)} %param.28), dimensions={0} | concatenate | bytes 6912 | tf_op jit(solution)/shard_map/concatenate | solution.py:368
  13.1 14.8 %all_to_all.55 = bf16[4,99,768]{2,1,0:T(8,128)(2,1)S(1)} all-to-all(bf16[4,99,768]{2,1,0:T(8,128)(2,1)S(1)} %copy.110), channel_id=1, replica_groups=mesh['fsdp'=4,'ctx'=8] {'fsdp'}, dimensions={0} | all-to-all | bytes 1216512 | tf_op jit(solution)/shard_map/all_to_all | solution.py:328
  28.0 21.9 %all_to_all.56.x_ref = bf16[4,256,768]{2,1,0:T(8,128)(2,1)} all-to-all(bf16[4,256,768]{2,1,0:T(8,128)(2,1)S(1)} %broadcast_in_dim.114), channel_id=1, replica_groups=mesh['fsdp'=4,'ctx'=8] {'fsdp'}, dimensions={0} | all-to-all | bytes 3145728 | tf_op jit(solution)/shard_map/all_to_all | solution.py:328
  51.1 3.7 all-to-all-start.5
  59.2 12.1 %all-to-all-done.5.g_ref = bf16[4,256,768]{2,1,0:T(8,128)(2,1)S(1)} async-done(((bf16[4,256,768]{2,1,0:T(8,128)(2,1)}), bf16[4,256,768]{2,1,0:T(8,128)(2,1)S(1)}, u32[]{:S(2)}, u32[]{:S(2)}) %all-to-all-start.5) | async-done | bytes 1572896 | tf_op jit(solution)/shard_map/all_to_all | solution.py:328
  72.5 13.9 %feed_forward.1 = (bf16[4,256,768]{2,1,0:T(8,128)(2,1)}, bf16[4,256,768]{2,1,0:T(8,128)(2,1)}, bf16[768,768]{1,0:T(8,128)(2,1)}, bf16[768,768]{1,0:T(8,128)(2,1)...) custom-call(bf16[4,256,768]{2,1,0:T(8,128)(2,1)} %all_to_all.56.x_ref, bf16[4,256,768]{2,1,0:T(8,128)(2,1)} %copy-done.5, ...), custom_call_target="tpu_custom_call" | custom-call | tf_op jit(solution)/shard_map/feed_forward/pallas_call | solution.py:90
  92.5 17.4 %all_to_all.57 = bf16[4,192,768]{2,1,0:T(8,128)(2,1)S(1)} all-to-all(bf16[4,192,768]{2,1,0:T(8,128)(2,1)S(1)} %broadcast_in_dim.59), channel_id=1, replica_groups=mesh['fsdp'=4,'ctx'=8] {'fsdp'}, dimensions={0} | all-to-all | bytes 2359296 | tf_op jit(solution)/shard_map/all_to_all | solution.py:328
  110.0 2.8 collective-permute-done
  115.2 4.9 %all-to-all-start.1 = ((bf16[8,200,256]{2,1,0:T(8,128)(2,1)}), bf16[8,200,256]{2,1,0:T(8,128)(2,1)S(1)}, u32[]{:S(2)}, u32[]{:S(2)}) async-start(bf16[8,200,256]{2,1,0:T(8,128)(2,1)} %pad_maximum_fusion.5), calls=%async_computation.1 | async-start | bytes 1638400 | tf_op jit(solution)/shard_map/all_to_all | solution.py:328
  124.9 21.1 %all-to-all-done.1.da_ref.db_ref = bf16[8,200,256]{2,1,0:T(8,128)(2,1)S(1)} async-done(((bf16[8,200,256]{2,1,0:T(8,128)(2,1)}), bf16[8,200,256]{2,1,0:T(8,128)(2,1)S(1)}, u32[]{:S(2)}, u32[]{:S(2)}) %all-to-all-start.1) | async-done | bytes 819232 | tf_op jit(solution)/shard_map/all_to_all | solution.py:328
  148.0 3.3 all-to-all-start.9
  152.0 17.4 %all-gather.3.cloned.1.call-done = bf16[1,2048,768]{2,1,0:T(8,128)(2,1)} async-done(((bf16[1,256,768]{2,1,0:T(8,128)(2,1)}), bf16[1,2048,768]{2,1,0:T(8,128)(2,1)}) %all-gather.3.cloned.1.call-update) | async-done | bytes 3145744 | tf_op jit(solution)/shard_map/all_gather | solution.py:364
  169.4 10.0 %project.1.q_ref.k_ref.v_ref = bf16[9,8,64,256]{3,2,1,0:T(8,128)(2,1)} custom-call(s32[16]{0:T(128)} %copy-done.29, bf16[16,128,768]{2,1,0:T(8,128)(2,1)} %bitcast.88, bf16[16,128,768]{2,1,0:T(8,128)(2,1)} %bitcast.89, bf16[576,768]{1,0:T(8,128)(2,1)} %bitcast.96, f32[576,1]{1,0:T(8,128)} %reshape.375.bias_ref, f32[1,768]{1,0:T(1,128)} %reshape.350.gain_ref, ...), custom_call_target="tpu_custom_call" | custom-call | tf_op jit(solution)/shard_map/project/pallas_call | solution.py:133
  179.4 48.9 %attend.1 = (bf16[8,3,2,64,128]{4,3,2,1,0:T(8,128)(2,1)}, bf16[9,8,64,256]{3,2,1,0:T(8,128)(2,1)}) custom-call(s32[17]{0:T(128)} %pad_add_fusion.place_ref, bf16[9,8,64,256]{3,2,1,0:T(8,128)(2,1)} %project.1.q_ref.k_ref.v_ref, bf16[9,8,64,256]{3,2,1,0:T(8,128)(2,1)} %project.1.q_ref.k_ref.v_ref, bf16[9,8,64,256]{3,2,1,0:T(8,128)(2,1)} %project.1.q_ref.k_ref.v_ref, ...), custom_call_target="tpu_custom_call" | custom-call | tf_op jit(solution)/shard_map/attend/pallas_call | solution.py:243
  228.3 3.7 all-to-all-start.3
  232.5 13.5 %project_back.1 = (bf16[16,128,768]{2,1,0:T(8,128)(2,1)}, bf16[768,576]{1,0:T(8,128)(2,1)}, f32[576,1]{1,0:T(8,128)}, f32[1,768]{1,0:T(1,128)}, f32[1,768]{1,0:T(1,128)}) custom-call(s32[16]{0:T(128)} %copy-done.29, bf16[9,8,64,256]{3,2,1,0:T(8,128)(2,1)} %get-tuple-element.31.b_ref, bf16[576,768]{1,0:T(8,128)(2,1)} %bitcast.97, ...), custom_call_target="tpu_custom_call" | custom-call | tf_op jit(solution)/shard_map/project_back/pallas_call | solution.py:309
  249.2 3.6 all-to-all-done.3
  253.8 3.5 all-to-all-start.10
  260.2 3.2 collective-permute-done.2
  266.0 35.6 %all-to-all-done.10 = bf16[4,192,768]{2,1,0:T(8,128)(2,1)S(1)} async-done(((bf16[4,192,768]{2,1,0:T(8,128)(2,1)}), bf16[4,192,768]{2,1,0:T(8,128)(2,1)S(1)}, u32[]{:S(2)}, u32[]{:S(2)}) %all-to-all-start.10) | async-done | bytes 1179680 | tf_op jit(solution)/shard_map/all_to_all | solution.py:328
  301.6 3.5 all-to-all-start.7
  305.1 3.8 pad_maximum_fusion
  308.9 8.2 %all-to-all-done.7 = bf16[4,192,768]{2,1,0:T(8,128)(2,1)S(1)} async-done(((bf16[4,192,768]{2,1,0:T(8,128)(2,1)}), bf16[4,192,768]{2,1,0:T(8,128)(2,1)S(1)}, u32[]{:S(2)}, u32[]{:S(2)}) %all-to-all-start.7) | async-done | bytes 1179680 | tf_op jit(solution)/shard_map/all_to_all | solution.py:328
  318.2 3.7 all-to-all-start.6
  324.3 32.7 %all-to-all-done.6 = bf16[4,512,768]{2,1,0:T(8,128)(2,1)S(1)} async-done(((bf16[4,512,768]{2,1,0:T(8,128)(2,1)}), bf16[4,512,768]{2,1,0:T(8,128)(2,1)S(1)}, u32[]{:S(2)}, u32[]{:S(2)}) %all-to-all-start.6) | async-done | bytes 3145760 | tf_op jit(solution)/shard_map/all_to_all | solution.py:328
  359.1 4.3 all-to-all-start.8
  369.8 21.7 %all-to-all-done.8 = bf16[4,192,768]{2,1,0:T(8,128)(2,1)} async-done(((bf16[4,192,768]{2,1,0:T(8,128)(2,1)}), bf16[4,192,768]{2,1,0:T(8,128)(2,1)}, u32[]{:S(2)}, u32[]{:S(2)}) %all-to-all-start.8) | async-done | bytes 1179680 | tf_op jit(solution)/shard_map/all_to_all | solution.py:328
  400.8 5.5 %copy.117 = bf16[4,1,1,2,96,768]{4,2,5,0,3,1:T(2,128)(2,1)} copy(bf16[4,1,1,2,96,768]{5,4,3,0,2,1:T(8,128)(2,1)S(1)} %bitcast.103) | data formatting | bytes 2359296 | tf_op jit(solution)/shard_map/stack | solution.py:362
  406.3 5.6 %copy.116 = bf16[4,1,1,2,96,768]{4,2,5,0,3,1:T(2,128)(2,1)} copy(bf16[4,1,1,2,96,768]{5,4,3,0,2,1:T(8,128)(2,1)S(1)} %bitcast.102) | data formatting | bytes 2359296 | tf_op jit(solution)/shard_map/stack | solution.py:362
  411.9 10.9 %maximum_convert_fusion = f32[4,1,2,2,96,768]{4,2,5,0,3,1:T(2,128)S(1)} fusion(bf16[4,1,1,2,96,768]{4,2,5,0,3,1:T(2,128)(2,1)} %copy.117, bf16[4,1,1,2,96,768]{4,2,5,0,3,1:T(2,128)(2,1)} %copy.116), kind=kLoop, calls=%fused_computation.9 | loop fusion | flops 4718592 | bytes 7077888 | tf_op jit(solution)/shard_map/convert_element_type | solution.py:476
  422.8 3.4 slice_reduce_fusion
  431.2 3.0 copy.118
  (194 shorter events, 65.1 us)
Async XLA Ops:
  7.2 4.9 %copy-start = (bf16[192,3072]{1,0:T(8,128)(2,1)S(1)}, bf16[192,3072]{1,0:T(8,128)(2,1)}, u32[]{:S(2)}) copy-start(bf16[192,3072]{1,0:T(8,128)(2,1)} %param.21) | copy-start | bytes 3538948
  12.6 15.3 %copy-start.2 = (bf16[1,256,768]{2,1,0:T(8,128)(2,1)S(1)}, bf16[1,256,768]{2,1,0:T(8,128)(2,1)}, u32[]{:S(2)}) copy-start(bf16[1,256,768]{2,1,0:T(8,128)(2,1)} %param.15) | copy-start | bytes 1179652
  28.0 21.9 %copy-start.8 = (bf16[1,256,768]{2,1,0:T(8,128)(2,1)S(1)}, bf16[1,256,768]{2,1,0:T(8,128)(2,1)}, u32[]{:S(2)}) copy-start(bf16[1,256,768]{2,1,0:T(8,128)(2,1)} %param.29) | copy-start | bytes 1179652
  51.1 4.6 %copy-start.28 = (bf16[768]{0:T(1024)(128)(2,1)S(1)}, bf16[768]{0:T(1024)(128)(2,1)}, u32[]{:S(2)}) copy-start(bf16[768]{0:T(1024)(128)(2,1)} %param.22) | copy-start | bytes 4612
  51.1 20.2 %all-to-all-start.5 = ((bf16[4,256,768]{2,1,0:T(8,128)(2,1)}), bf16[4,256,768]{2,1,0:T(8,128)(2,1)S(1)}, u32[]{:S(2)}, u32[]{:S(2)}) async-start(bf16[4,256,768]{2,1,0:T(8,128)(2,1)} %broadcast_in_dim.115), calls=%async_computation.5 | async-start | bytes 3145728 | tf_op jit(solution)/shard_map/all_to_all | solution.py:328
  54.8 91.6 %reduce-scatter.5.cloned.1.call-start = ((), (), s32[]{:S(2)}) async-start(), calls=%async_computation.14 | async-start | bytes 2654208 | tf_op jit(solution)/shard_map/reduce_scatter | solution.py:412
  55.7 2.2 collective-permute-start.1
  89.6 79.8 %all-gather.3.cloned.1.call-start = ((), (), s32[]{:S(2)}) async-start(), calls=%async_computation.15 | async-start | bytes 3538944 | tf_op jit(solution)/shard_map/all_gather | solution.py:364
  92.4 17.5 %copy-start.30 = (s32[1,256]{1,0:T(1,128)S(1)}, s32[1,256]{1,0:T(1,128)}, u32[]{:S(2)}) copy-start(s32[1,256]{1,0:T(1,128)} %param.16) | copy-start | bytes 3076
  109.9 2.8 collective-permute-start
  115.2 30.8 %all-to-all-start.1 = ((bf16[8,200,256]{2,1,0:T(8,128)(2,1)}), bf16[8,200,256]{2,1,0:T(8,128)(2,1)S(1)}, u32[]{:S(2)}, u32[]{:S(2)}) async-start(bf16[8,200,256]{2,1,0:T(8,128)(2,1)} %pad_maximum_fusion.5), calls=%async_computation.1 | async-start | bytes 1638400 | tf_op jit(solution)/shard_map/all_to_all | solution.py:328
  146.0 33.4 %copy-start.4 = (bf16[8,200,256]{2,1,0:T(8,128)(2,1)}, bf16[8,200,256]{2,1,0:T(8,128)(2,1)S(1)}, u32[]{:S(2)}) copy-start(bf16[8,200,256]{2,1,0:T(8,128)(2,1)S(1)} %all-to-all-done.1.da_ref.db_ref) | copy-start | bytes 2457604
  146.3 23.0 %copy-start.29 = (s32[16]{0:T(128)}, s32[16]{0:T(128)S(1)}, u32[]{:S(2)}) copy-start(s32[16]{0:T(128)S(1)} %select_reduce_fusion.order_ref) | copy-start | bytes 196
  148.0 80.2 %all-to-all-start.9 = ((bf16[4,24,768]{2,1,0:T(8,128)(2,1)}), bf16[4,24,768]{2,1,0:T(8,128)(2,1)S(1)}, u32[]{:S(2)}, u32[]{:S(2)}) async-start(bf16[4,24,768]{2,1,0:T(8,128)(2,1)} %bitcast.35), calls=%async_computation.11 | async-start | bytes 294912 | tf_op jit(solution)/shard_map/all_to_all | solution.py:328
  228.3 4.0 copy-start.26
  228.3 4.0 copy-start.27
  228.3 4.2 copy-start.25
  228.3 24.5 %all-to-all-start.3 = ((bf16[8,3,2,64,128]{4,3,2,1,0:T(8,128)(2,1)}), bf16[8,3,2,64,128]{4,3,2,1,0:T(8,128)(2,1)S(1)}, u32[]{:S(2)}, u32[]{:S(2)}) async-start(bf16[8,3,2,64,128]{4,3,2,1,0:T(8,128)(2,1)} %get-tuple-element.28), calls=%async_computation.3 | async-start | bytes 1572864 | tf_op jit(solution)/shard_map/all_to_all | solution.py:328
  253.8 47.7 %all-to-all-start.10 = ((bf16[4,192,768]{2,1,0:T(8,128)(2,1)}), bf16[4,192,768]{2,1,0:T(8,128)(2,1)S(1)}, u32[]{:S(2)}, u32[]{:S(2)}) async-start(bf16[4,192,768]{2,1,0:T(8,128)(2,1)} %broadcast_in_dim.126), calls=%async_computation.12 | async-start | bytes 2359296 | tf_op jit(solution)/shard_map/all_to_all | solution.py:328
  257.4 138.7 %reduce-scatter.3.cloned.1.call-start = ((), (), s32[]{:S(2)}) async-start(), calls=%async_computation.13 | async-start | bytes 3538944 | tf_op jit(solution)/shard_map/reduce_scatter | solution.py:448
  260.2 3.2 collective-permute-start.2
  301.6 7.3 %copy-start.10 = (bf16[4,192,768]{2,1,0:T(8,128)(2,1)}, bf16[4,192,768]{2,1,0:T(8,128)(2,1)S(1)}, u32[]{:S(2)}) copy-start(bf16[4,192,768]{2,1,0:T(8,128)(2,1)S(1)} %all-to-all-done.10) | copy-start | bytes 3538948
  301.6 15.6 %all-to-all-start.7 = ((bf16[4,192,768]{2,1,0:T(8,128)(2,1)}), bf16[4,192,768]{2,1,0:T(8,128)(2,1)S(1)}, u32[]{:S(2)}, u32[]{:S(2)}) async-start(bf16[4,192,768]{2,1,0:T(8,128)(2,1)} %fusion.5), calls=%async_computation.8 | async-start | bytes 2359296 | tf_op jit(solution)/shard_map/all_to_all | solution.py:328
  308.9 13.0 %copy-start.3 = (bf16[1,256,768]{2,1,0:T(8,128)(2,1)S(1)}, bf16[1,256,768]{2,1,0:T(8,128)(2,1)}, u32[]{:S(2)}) copy-start(bf16[1,256,768]{2,1,0:T(8,128)(2,1)} %param.15) | copy-start | bytes 1179652
  318.2 38.9 %all-to-all-start.6 = ((bf16[4,512,768]{2,1,0:T(8,128)(2,1)}), bf16[4,512,768]{2,1,0:T(8,128)(2,1)S(1)}, u32[]{:S(2)}, u32[]{:S(2)}) async-start(bf16[4,512,768]{2,1,0:T(8,128)(2,1)} %pad_maximum_fusion), calls=%async_computation.6 | async-start | bytes 6291456 | tf_op jit(solution)/shard_map/all_to_all | solution.py:328
  321.9 45.3 %collective-permute-start.4 = (bf16[4,192,768]{2,1,0:T(8,128)(2,1)}, bf16[4,192,768]{2,1,0:T(8,128)(2,1)}, u32[]{:S(2)}, u32[]{:S(2)}) collective-permute-start(bf16[4,192,768]{2,1,0:T(8,128)(2,1)} %copy-done.10), channel_id=1, source_target_pairs={{0,1},{1,0},{2,3},{3,2},{4,5},{5,4},{6,7},{7,6},{8,9},{9,8},{10,11... | collective-permute-start | bytes 3538952 | tf_op jit(solution)/shard_map/ppermute | solution.py:359
  359.1 32.3 %all-to-all-start.8 = ((bf16[4,192,768]{2,1,0:T(8,128)(2,1)}), bf16[4,192,768]{2,1,0:T(8,128)(2,1)}, u32[]{:S(2)}, u32[]{:S(2)}) async-start(bf16[4,192,768]{2,1,0:T(8,128)(2,1)} %broadcast_in_dim.125), calls=%async_computation.9 | async-start | bytes 2359296 | tf_op jit(solution)/shard_map/all_to_all | solution.py:328
  365.8 2.0 copy-start.11
  391.4 7.5 %collective-permute-start.3 = (bf16[4,192,768]{2,1,0:T(8,128)(2,1)}, bf16[4,192,768]{2,1,0:T(8,128)(2,1)}, u32[]{:S(2)}, u32[]{:S(2)}) collective-permute-start(bf16[4,192,768]{2,1,0:T(8,128)(2,1)} %all-to-all-done.8), channel_id=1, source_target_pairs={{0,1},{1,0},{2,3},{3,2},{4,5},{5,4},{6,7},{7,6},{8,9},{9,8},{10,11... | collective-permute-start | bytes 3538952 | tf_op jit(solution)/shard_map/ppermute | solution.py:359
  394.4 1.9 copy-start.7
  428.1 10.9 %copy-start.23 = (f32[192]{0:T(256)}, f32[192]{0:T(256)S(1)}, u32[]{:S(2)}) copy-start(f32[192]{0:T(256)S(1)} %get-tuple-element.116) | copy-start | bytes 2308
  434.2 5.4 %copy-start.1 = (bf16[192,3072]{1,0:T(8,128)(2,1)S(1)}, bf16[192,3072]{1,0:T(8,128)(2,1)}, u32[]{:S(2)}) copy-start(bf16[192,3072]{1,0:T(8,128)(2,1)} %param.21) | copy-start | bytes 3538948
  (15 other events, 18.5 us)
Sparse Core Ops, SparseCore 0:
  89.7 37.1 reduce-scatter.4
  128.5 40.7 all-gather.2
  260.5 53.5 reduce-scatter.2

commit v2 on v1

v2 whole, which is shorter than its diff:
```python
import functools
import math

import jax
import jax.numpy as jnp
from jax import lax
from jax.experimental import pallas as pl
from jax.experimental.pallas import tpu as pltpu
from jax.sharding import PartitionSpec as P

HEAD = 64
ROT = 16
HALF = ROT // 2
RUN = 128
TILE = 256
NEG = -1e30
EPS = 1e-05
BF = jnp.bfloat16
F32 = jnp.float32
VMEM_LIMIT = 60 * 1024 * 1024


def mm(left, right, dims):
    return lax.dot_general(left, right, ((dims[:1], dims[1:]), ((), ())), preferred_element_type=F32)


def flip(x):
    return x.astype(F32).T.astype(x.dtype)


def normalize(values):
    mean = jnp.mean(values, -1, keepdims=True)
    centred = values - mean
    spread = jnp.mean(centred * centred, -1, keepdims=True)
    inverse = lax.rsqrt(spread + EPS)
    return centred * inverse, inverse


def turn(values, cosine, sine):
    one, two = values[:HALF], values[HALF:ROT]
    return jnp.concatenate([one * cosine - two * sine, two * cosine + one * sine, values[ROT:]], 0)


def ff_kernel(packed, core_ref, x_ref, g_ref, small_ref, mine_ref, mine_end_ref, other_ref, down_ref, upb_ref,
              *refs):
    shards = small_ref.shape[0]
    outs, refs = refs[:shards], refs[shards:]
    (dup_ref, ddown_ref, dbias_ref, dgain_ref, dshift_ref, acc_up, acc_down, up_ref, gain_ref, shift_ref) = refs
    step = pl.program_id(0)

    @pl.when(step == 0)
    def _():
        half = other_ref.shape[1]
        share = gain_ref.shape[1] // shards
        first = core_ref[0] == 0
        for f in range(shards):
            mine = jnp.concatenate([mine_ref[f].astype(F32), mine_end_ref[f].astype(F32)], 0)
            other = other_ref[f].astype(F32)
            at = 2 * f * half
            up_ref[at:at + half] = jnp.where(first, mine, other).astype(BF)
            up_ref[at + half:at + 2 * half] = jnp.where(first, other, mine).astype(BF)
            small = small_ref[f].astype(F32)
            gain_ref[:, f * share:(f + 1) * share] = small[0:1, :share]
            shift_ref[:, f * share:(f + 1) * share] = small[1:2, :share]
        acc_up[...] = jnp.zeros_like(acc_up)
        acc_down[...] = jnp.zeros_like(acc_down)
        dbias_ref[...] = jnp.zeros_like(dbias_ref)
        dgain_ref[...] = jnp.zeros_like(dgain_ref)
        dshift_ref[...] = jnp.zeros_like(dshift_ref)

    xhat, _ = normalize(x_ref[0].astype(F32))
    second = (xhat * gain_ref[...] + shift_ref[...]).astype(BF)
    up = mm(second, up_ref[...], (1, 0)) + upb_ref[...]
    phi = 0.5 * (1.0 + lax.erf(up * (1.0 / math.sqrt(2.0))))
    active = (up * phi).astype(BF)
    slope = phi + up * jnp.exp(-0.5 * up * up) * (1.0 / math.sqrt(2.0 * math.pi))
    tokens = x_ref.shape[1]
    part = mm(active, down_ref[...], (1, 0)).astype(BF)
    grad = g_ref[0]
    back_up = mm(grad, down_ref[...], (1, 1)) * slope
    low_up = back_up.astype(BF)
    dbias_ref[...] += jnp.sum(low_up.astype(F32), 0, keepdims=True)
    acc_up[...] += mm(second, low_up, (0, 0))
    acc_down[...] += mm(active, grad, (0, 0))
    back = mm(low_up, up_ref[...], (1, 1))
    dgain_ref[...] += jnp.sum(back * xhat, 0, keepdims=True)
    dshift_ref[...] += jnp.sum(back, 0, keepdims=True)
    back = (back * gain_ref[...]).astype(BF)
    for k in range(shards):
        @pl.when(step == k)
        def _(k=k):
            outs[k][:tokens] = part
            outs[k][tokens:] = back

    @pl.when(step == pl.num_programs(0) - 1)
    def _():
        if packed:
            owners = dup_ref.shape[0]
            rows = acc_up.shape[0] // shards
            few = rows // owners
            down_rows = acc_down.shape[0] // owners
            for c in range(owners):
                up_rows = [acc_up[f * rows + c * few:f * rows + (c + 1) * few] for f in range(shards)]
                dup_ref[c] = jnp.concatenate(
                    up_rows + [acc_down[c * down_rows:(c + 1) * down_rows]], 0).astype(BF)
            ddown_ref[...] = jnp.zeros_like(ddown_ref)
        else:
            dup_ref[...] = acc_up[...].astype(BF)
            ddown_ref[...] = acc_down[...].astype(BF)


def whole(shape):
    return pl.BlockSpec(shape, lambda *_: (0,) * len(shape))


def cost(macs, size):
    return pl.CostEstimate(flops=int(2 * macs), bytes_accessed=int(size), transcendentals=0)


def feed_forward(at, got, tokens, up_mine, up_other, skip, down, up_bias, owners):
    groups, _, width = got.shape
    hidden = down.shape[0]
    half = width // groups // 2
    quarter = half // 2
    at_up = skip // quarter if up_mine is got else 0
    x_tile = pl.BlockSpec((1, tokens, width), lambda i, at: (at[1] ^ i, 0, 0))
    g_tile = pl.BlockSpec((1, tokens, width), lambda i, at: (at[1] ^ i, 1, 0))
    small_tile = pl.BlockSpec((groups, 16, width), lambda i, at: (0, 2 * tokens // 16, 0))
    row = jax.ShapeDtypeStruct((1, width), F32)
    if owners:
        shapes = [(owners, (width + hidden) // owners, hidden), (16, 128)]
    else:
        shapes = [(width, hidden), (hidden, width)]
    return pl.pallas_call(
        functools.partial(ff_kernel, bool(owners)),
        grid_spec=pltpu.PrefetchScalarGridSpec(
            num_scalar_prefetch=1,
            grid=(groups,),
            in_specs=[x_tile, g_tile, small_tile,
                      pl.BlockSpec((groups, quarter, hidden), lambda i, at: (0, at_up, 0)),
                      pl.BlockSpec((groups, quarter, hidden), lambda i, at: (0, at_up + 1, 0)),
                      whole((groups, half, hidden)), whole((hidden, width)), whole((1, hidden))],
            out_specs=[whole((2 * tokens, width))] * groups + [whole(shape) for shape in shapes]
            + [whole((1, hidden)), whole((1, width)), whole((1, width))],
            scratch_shapes=[pltpu.VMEM((width, hidden), F32), pltpu.VMEM((hidden, width), F32),
                            pltpu.VMEM((width, hidden), BF), pltpu.VMEM((1, width), F32),
                            pltpu.VMEM((1, width), F32)],
        ),
        out_shape=[jax.ShapeDtypeStruct((2 * tokens, width), BF)] * groups
        + [jax.ShapeDtypeStruct(shape, BF) for shape in shapes]
        + [jax.ShapeDtypeStruct((1, hidden), F32), row, row],
        compiler_params=pltpu.CompilerParams(vmem_limit_bytes=VMEM_LIMIT),
        cost_estimate=cost(12 * groups * tokens * width * hidden, 4 * got.size),
        name="feed_forward",
    )(at, got, got, got, up_mine, up_mine, up_other, down, up_bias)


def qkv_kernel(order_ref, xa_ref, xb_ref, ga_ref, gb_ref, w_ref, wo_ref, bias_ref, gain_ref, shift_ref, cos_ref,
               sin_ref, out_ref):
    values = jnp.concatenate([xa_ref[0], xb_ref[0]], 0).astype(F32)
    xhat, _ = normalize(values)
    first = (xhat * gain_ref[...] + shift_ref[...]).astype(BF)
    proj = mm(w_ref[...], first, (1, 1)) + bias_ref[...]
    heads = out_ref.shape[0] // 4
    cosine, sine = cos_ref[0], sin_ref[0]
    for i in range(3 * heads):
        part = proj[i * HEAD:(i + 1) * HEAD]
        if i < 2 * heads:
            part = turn(part, cosine, sine)
        part = part.astype(BF)
        if i < heads:
            part = part * jnp.asarray(1.0 / math.sqrt(HEAD), BF)
        out_ref[i, 0] = part
    back = mm(wo_ref[...], jnp.concatenate([ga_ref[0], gb_ref[0]], 0), (1, 1)).astype(BF)
    for i in range(heads):
        out_ref[3 * heads + i, 0] = back[i * HEAD:(i + 1) * HEAD]


def run_specs(width, held, skip):
    def at(i, order, k):
        run = order[2 * i + k]
        return run // held, run % held + skip, 0

    return [pl.BlockSpec((1, RUN, width), lambda i, order, k=k: at(i, order, k)) for k in (0, 1)]


def project(order, both_all, w, w_out, bias, gain, shift, cosine, sine):
    owners, _, width = both_all.shape
    held = order.shape[0] // owners
    rows, cols = w.shape[0], w_out.shape[0]
    tiles = order.shape[0] // 2
    parts = (rows + cols) // HEAD
    table = pl.BlockSpec((1, HALF, TILE), lambda i, order: (i, 0, 0))
    return pl.pallas_call(
        qkv_kernel,
        grid_spec=pltpu.PrefetchScalarGridSpec(
            num_scalar_prefetch=1,
            grid=(tiles,),
            in_specs=run_specs(width, held, 0) + run_specs(width, held, held)
            + [whole((rows, width)), whole((cols, width)), whole((rows, 1)), whole((1, width)),
               whole((1, width)), table, table],
            out_specs=pl.BlockSpec((parts, 1, HEAD, TILE), lambda i, order: (0, i, 0, 0)),
        ),
        out_shape=jax.ShapeDtypeStruct((parts, tiles, HEAD, TILE), BF),
        compiler_params=pltpu.CompilerParams(vmem_limit_bytes=VMEM_LIMIT),
        cost_estimate=cost(5 * tiles * TILE * width * (rows + cols), 4 * both_all.size),
        name="project",
    )(order, both_all, both_all, both_all, both_all, w, w_out, bias, gain, shift, cosine, sine)


def attention_kernel(share, fused, held, place_ref, q_ref, k_ref, v_ref, d_ref, cos_ref, sin_ref,
                     mix_ref, back_ref, keys, values, dkeys, dvalues, sbuf, pbuf):
    turn_at, step = pl.program_id(0), pl.program_id(1)
    heads, steps = pl.num_programs(0) * fused, pl.num_programs(1)
    tiles = k_ref.shape[1]
    block = share(step, place_ref)
    every = range(fused)

    @pl.when((turn_at == 0) & (step == 0))
    def _():
        mix_ref[...] = jnp.zeros_like(mix_ref)
        back_ref[...] = jnp.zeros_like(back_ref)

    @pl.when(step == 0)
    def _():
        @pl.loop(0, tiles)
        def _(j):
            for h in every:
                keys[h, j] = flip(k_ref[h, j])
                values[h, j] = flip(v_ref[h, j])
                dkeys[h, j] = jnp.zeros((TILE, HEAD), F32)
                dvalues[h, j] = jnp.zeros((TILE, HEAD), F32)

    queries = [q_ref[h, 0] for h in every]

    def fold(x, op):
        return op(x.reshape(TILE // 8, 8, TILE), 0)

    def score(j, peaks):
        new = []
        for h in every:
            s = mm(keys[h, j], queries[h], (1, 0))
            sbuf[h, j] = s
            new.append(jnp.maximum(peaks[h], fold(s, jnp.max)))
        return tuple(new)

    peaks = lax.fori_loop(0, block, score, tuple(jnp.full((8, TILE), NEG, F32) for _ in every))
    key_at = lax.broadcasted_iota(jnp.int32, (TILE, TILE), 0)
    query_at = lax.broadcasted_iota(jnp.int32, (TILE, TILE), 1)
    last = []
    for h in every:
        s = jnp.where(key_at <= query_at, mm(keys[h, block], queries[h], (1, 0)), NEG)
        sbuf[h, block] = s
        last.append(jnp.max(jnp.maximum(peaks[h], fold(s, jnp.max)), 0, keepdims=True))
    peaks = last

    def weigh(j, carry):
        new = []
        for h in every:
            total, mixed = carry[h]
            p = jnp.exp(sbuf[h, j] - peaks[h])
            low = p.astype(BF)
            pbuf[h, j] = low
            new.append((total + fold(p, jnp.sum), mixed + mm(v_ref[h, j], low, (1, 0))))
        return tuple(new)

    sums = lax.fori_loop(
        0, block + 1, weigh,
        tuple((jnp.zeros((8, TILE), F32), jnp.zeros((HEAD, TILE), F32)) for _ in every))
    spreads, backs, back_rows, query_rows = [], [], [], []
    for h in every:
        total, mixed = sums[h]
        inverse = 1.0 / jnp.sum(total, 0, keepdims=True)
        mixed = mixed * inverse
        low_mixed = mixed.astype(BF)
        for k in (0, 1):
            at = place_ref[1 + 2 * block + k]
            mix_ref[at // held, turn_at * fused + h, at % held] = low_mixed[:, k * RUN:(k + 1) * RUN]
        back = d_ref[h, 0].astype(F32) * inverse
        spreads.append(jnp.sum(back * mixed, 0, keepdims=True))
        back = back.astype(BF)
        backs.append(back)
        back_rows.append(flip(back))
        query_rows.append(flip(queries[h]))

    def pull(j, dquery):
        new = []
        for h in every:
            low = pbuf[h, j]
            dp = mm(values[h, j], backs[h], (1, 0))
            ds = (low.astype(F32) * (dp - spreads[h])).astype(BF)
            dvalues[h, j] += mm(low, back_rows[h], (1, 0))
            dkeys[h, j] += mm(ds, query_rows[h], (1, 0))
            new.append(dquery[h] + mm(k_ref[h, j], ds, (1, 0)))
        return tuple(new)

    dquery = lax.fori_loop(0, block + 1, pull, tuple(jnp.zeros((HEAD, TILE), F32) for _ in every))
    for h in every:
        dq = dquery[h] * (1.0 / math.sqrt(HEAD))
        back_ref[turn_at * fused + h, block] = turn(dq, cos_ref[block], -sin_ref[block]).astype(BF)

    @pl.when(step == steps - 1)
    def _():
        @pl.loop(0, tiles)
        def _(j):
            for h in every:
                at = heads + turn_at * fused + h
                back_ref[at, j] = turn(dkeys[h, j].T, cos_ref[j], -sin_ref[j]).astype(BF)
                back_ref[heads + at, j] = dvalues[h, j].T.astype(BF)


def attend(place, qkv, cosine, sine, owners, sharers):
    parts, tiles, _, _ = qkv.shape
    heads = parts // 4
    held = (place.shape[0] - 1) // owners
    steps = tiles // sharers
    fused = heads if tiles <= 16 else 1
    turns = heads // fused

    def share(step, place_ref):
        return 2 * sharers * (step // 2) + jnp.where(step % 2 == 0, place_ref[0], 2 * sharers - 1 - place_ref[0])

    all_tiles, one_tile = (fused, tiles, HEAD, TILE), (fused, 1, HEAD, TILE)
    return pl.pallas_call(
        functools.partial(attention_kernel, share, fused, held),
        grid_spec=pltpu.PrefetchScalarGridSpec(
            num_scalar_prefetch=1,
            grid=(turns, steps),
            in_specs=[
                pl.BlockSpec(one_tile, lambda h, n, p: (h, share(n, p), 0, 0)),
                pl.BlockSpec(all_tiles, lambda h, n, p: (turns + h, 0, 0, 0)),
                pl.BlockSpec(all_tiles, lambda h, n, p: (2 * turns + h, 0, 0, 0)),
                pl.BlockSpec(one_tile, lambda h, n, p: (3 * turns + h, share(n, p), 0, 0)),
                whole((tiles, HALF, TILE)),
                whole((tiles, HALF, TILE)),
            ],
            out_specs=[whole((owners, heads, held, HEAD, RUN)), whole((3 * heads, tiles, HEAD, TILE))],
            scratch_shapes=[
                pltpu.VMEM((fused, tiles, TILE, HEAD), BF),
                pltpu.VMEM((fused, tiles, TILE, HEAD), BF),
                pltpu.VMEM((fused, tiles, TILE, HEAD), F32),
                pltpu.VMEM((fused, tiles, TILE, HEAD), F32),
                pltpu.VMEM((fused, tiles, TILE, TILE), F32),
                pltpu.VMEM((fused, tiles, TILE, TILE), BF),
            ],
        ),
        out_shape=[jax.ShapeDtypeStruct((owners, heads, held, HEAD, RUN), BF),
                   jax.ShapeDtypeStruct((3 * heads, tiles, HEAD, TILE), BF)],
        compiler_params=pltpu.CompilerParams(vmem_limit_bytes=VMEM_LIMIT),
        cost_estimate=cost(40 * heads * HEAD * tiles * TILE * steps * TILE, 4 * qkv.size),
        name="attend",
    )(place, qkv, qkv, qkv, qkv, cosine, sine)


def back_weight_kernel(order_ref, b_ref, w_ref, xa_ref, xb_ref, ga_ref, gb_ref, ma_ref, mb_ref, gain_ref, shift_ref,
                       _, __, dw_ref, dout_ref, dbias_ref, dgain_ref, dshift_ref, acc):
    step = pl.program_id(0)

    @pl.when(step == 0)
    def _():
        acc[...] = jnp.zeros_like(acc)
        dout_ref[...] = jnp.zeros_like(dout_ref)
        dbias_ref[...] = jnp.zeros_like(dbias_ref)

    xhat, _ = normalize(jnp.concatenate([xa_ref[0], xb_ref[0]], 0).astype(F32))
    rows, cols = b_ref.shape[0] * HEAD, ma_ref.shape[1] * HEAD
    back = b_ref[...].reshape(rows, TILE)
    acc[...] += mm(back, xhat.astype(BF), (1, 0))
    mixed = jnp.concatenate([r[0, :, 0].reshape(cols, RUN) for r in (ma_ref, mb_ref)], 1)
    dout_ref[...] += mm(mixed, jnp.concatenate([ga_ref[0], gb_ref[0]], 0), (1, 0))
    dbias_ref[...] += jnp.sum(back.astype(F32), 1, keepdims=True)

    @pl.when(step == pl.num_programs(0) - 1)
    def _():
        weight = w_ref[...].astype(F32)
        bias = dbias_ref[...]
        dgain_ref[...] = jnp.sum(acc[...] * weight, 0, keepdims=True)
        dshift_ref[...] = jnp.sum(bias * weight, 0, keepdims=True)
        dw_ref[...] = (acc[...] * gain_ref[...] + bias * shift_ref[...]).T.astype(BF)


def back_input_kernel(order_ref, b_ref, w_ref, gain_ref, _, __, e_ref):
    step = pl.program_id(0)
    back = b_ref[...].reshape(b_ref.shape[0] * HEAD, TILE)
    e = (mm(back, w_ref[...], (0, 0)) * gain_ref[...]).astype(BF)
    e_ref[order_ref[2 * step]] = e[:RUN]
    e_ref[order_ref[2 * step + 1]] = e[RUN:]


ANY = pl.BlockSpec(memory_space=pl.ANY)


def back_to_weight(order, back, w, both_all, mixed, gain, shift, earlier):
    owners, _, width = both_all.shape
    held = order.shape[0] // owners
    rows = w.shape[0]
    parts, tiles, _, _ = back.shape
    heads = parts // 3
    line = jax.ShapeDtypeStruct((1, width), F32)

    def mixed_at(i, order, k):
        run = order[2 * i + k]
        return run // held, 0, run % held, 0, 0

    mixed_specs = [pl.BlockSpec((1, heads, 1, HEAD, RUN), lambda i, order, k=k: mixed_at(i, order, k)) for k in (0, 1)]
    return pl.pallas_call(
        back_weight_kernel,
        grid_spec=pltpu.PrefetchScalarGridSpec(
            num_scalar_prefetch=1,
            grid=(tiles,),
            in_specs=[pl.BlockSpec((parts, 1, HEAD, TILE), lambda i, order: (0, i, 0, 0)), whole((rows, width))]
            + run_specs(width, held, 0) + run_specs(width, held, held) + mixed_specs
            + [whole((1, width)), whole((1, width)), ANY, ANY],
            out_specs=[whole((width, rows)), whole((heads * HEAD, width)), whole((rows, 1)), whole((1, width)),
                       whole((1, width))],
            scratch_shapes=[pltpu.VMEM((rows, width), F32)],
        ),
        out_shape=[jax.ShapeDtypeStruct((width, rows), BF), jax.ShapeDtypeStruct((heads * HEAD, width), F32),
                   jax.ShapeDtypeStruct((rows, 1), F32), line, line],
        compiler_params=pltpu.CompilerParams(vmem_limit_bytes=VMEM_LIMIT),
        cost_estimate=cost(5 * tiles * TILE * width * rows, 4 * both_all.size),
        name="back_to_weight",
    )(order, back, w, both_all, both_all, both_all, both_all, mixed, mixed, gain, shift, *earlier)


def back_to_input(order, back, w, gain, earlier):
    rows, width = w.shape
    parts, tiles, _, _ = back.shape
    runs = order.shape[0]
    return pl.pallas_call(
        back_input_kernel,
        grid_spec=pltpu.PrefetchScalarGridSpec(
            num_scalar_prefetch=1,
            grid=(tiles,),
            in_specs=[pl.BlockSpec((parts, 1, HEAD, TILE), lambda i, order: (0, i, 0, 0)), whole((rows, width)),
                      whole((1, width)), ANY, ANY],
            out_specs=whole((runs, RUN, width)),
        ),
        out_shape=jax.ShapeDtypeStruct((runs, RUN, width), BF),
        compiler_params=pltpu.CompilerParams(vmem_limit_bytes=VMEM_LIMIT),
        cost_estimate=cost(5 * tiles * TILE * width * rows, 8 * back.size),
        name="back_to_input",
    )(order, back, w, gain, *earlier)


def ff_place_kernel(at_ref, all_ref, up_ref, down_ref):
    step_rows, shards = up_ref.shape[0], up_ref.shape[1] // all_ref.shape[2]
    hidden = all_ref.shape[2]
    value = all_ref[0].astype(F32)
    for k in range(shards):
        at = pl.multiple_of((at_ref[0] ^ k) * hidden, hidden)
        up_ref[:, pl.ds(at, hidden)] = value[k * step_rows:(k + 1) * step_rows]
    down_ref[...] = value[shards * step_rows:]


def place_ff(at, gathered, shards, step_rows):
    owners, rows, width = gathered.shape
    down_rows = rows - shards * step_rows
    return pl.pallas_call(
        ff_place_kernel,
        grid_spec=pltpu.PrefetchScalarGridSpec(
            num_scalar_prefetch=1,
            grid=(owners,),
            in_specs=[pl.BlockSpec((1, rows, width), lambda i, at: (i, 0, 0))],
        out_specs=[pl.BlockSpec((step_rows, shards * width), lambda i, core: (i, 0)),
                       pl.BlockSpec((down_rows, width), lambda i, core: (i, 0))],
        ),
        out_shape=[jax.ShapeDtypeStruct((owners * step_rows, shards * width), F32),
                   jax.ShapeDtypeStruct((owners * down_rows, width), F32)],
        compiler_params=pltpu.CompilerParams(vmem_limit_bytes=VMEM_LIMIT),
        name="place_ff",
    )(at, gathered)


def io_place_kernel(cols, core_ref, mine_ref, other_ref, in_ref, out_ref, line_ref):
    parity = pl.program_id(0)
    own = parity == core_ref[0]
    count, rows, width = mine_ref.shape
    half = rows // 2
    groups = width // cols
    held = count // groups
    for g in range(groups):
        value = None
        for i in range(held):
            at = g * held + i
            one = jnp.where(own, mine_ref[at].astype(F32), other_ref[at].astype(F32))
            value = one if value is None else value + one
        for part in range(3):
            at = part * width + g * cols
            in_ref[:, at:at + cols] = value[half:, part * cols:(part + 1) * cols]
        if g == 0:
            out_ref[...] = value[:half]
            line_ref[...] = value[half:, 3 * cols:]
        else:
            out_ref[...] += value[:half]
            line_ref[...] += value[half:, 3 * cols:]


def place_io(core, mine, other, cols):
    count, rows, width = mine.shape
    half = rows // 2
    return pl.pallas_call(
        functools.partial(io_place_kernel, cols),
        grid_spec=pltpu.PrefetchScalarGridSpec(
            num_scalar_prefetch=1,
            grid=(2,),
            in_specs=[whole(mine.shape), whole(other.shape)],
            out_specs=[pl.BlockSpec((half, 3 * width), lambda i, core: (i, 0)),
                       pl.BlockSpec((half, width), lambda i, core: (i, 0)),
                       pl.BlockSpec((half, width - 3 * cols), lambda i, core: (i, 0))],
        ),
        out_shape=[jax.ShapeDtypeStruct((rows, 3 * width), F32), jax.ShapeDtypeStruct((rows, width), F32),
                   jax.ShapeDtypeStruct((rows, width - 3 * cols), F32)],
        compiler_params=pltpu.CompilerParams(vmem_limit_bytes=VMEM_LIMIT),
        name="place_io",
    )(core[None], mine, other)


def spread_out(pieces, axis, groups=None):
    return lax.all_to_all(pieces, axis, 0, 0, axis_index_groups=groups)


def to_all_value(x, count):
    return jnp.broadcast_to(x[None], (count,) + x.shape)


def to_all(x, axis, groups=None, count=None):
    return spread_out(to_all_value(x, count or lax.axis_size(axis)), axis, groups)


def at_distance(pieces):
    count = len(pieces)
    return [pieces[0]] + [
        lax.ppermute(pieces[k], "fsdp", [(i, i ^ k) for i in range(count)]) for k in range(1, count)]


def by_distance(pieces, shard):
    return at_distance([
        lax.dynamic_index_in_dim(pieces, shard ^ k, 0, keepdims=False) for k in range(pieces.shape[0])])


def total(values):
    result = values[0].astype(F32)
    for v in values[1:]:
        result = result + v.astype(F32)
    return result


def after(index, value):
    first = value[(0,) * value.ndim]
    return index + (first != first).astype(jnp.int32)


def on_device(
    inputs, positions, in_weight, in_bias, out_weight, out_bias, up_weight, up_bias, down_weight, down_bias,
    first_gain, first_shift, second_gain, second_shift, out_grad,
):
    x, grad, place = inputs[0], out_grad[0], positions[0]
    tokens, width = x.shape
    owners, shards = lax.axis_size("ctx"), lax.axis_size("fsdp")
    here, shard = lax.axis_index("ctx"), lax.axis_index("fsdp")
    heads = width // HEAD
    groups = math.gcd(heads, owners // 2)
    sharers = owners // groups
    own_heads = heads // groups
    cols = own_heads * HEAD
    group, sharer, core = here // sharers, here % sharers, here % 2
    hidden = down_weight.shape[0]
    rows = in_weight.shape[0]
    half = rows // 2
    length = tokens * owners
    held = tokens // RUN
    joined = hidden == width
    tiles = length // TILE
    parity = [[i for i in range(owners) if i % 2 == k] for k in (0, 1)]
    pairs = [(i, i ^ 1) for i in range(owners)]

    def swap(value):
        return lax.ppermute(value, "ctx", pairs)

    def both(mine, other):
        return jnp.stack([jnp.where(core == 0, mine, other), jnp.where(core == 0, other, mine)], 1)

    run_rows = jnp.broadcast_to(jnp.pad((place[::RUN] // RUN).astype(BF), (0, width - held))[None], (16, width))
    both_all = lax.all_gather(jnp.concatenate([x, grad, run_rows], 0), "ctx", axis=0, tiled=False)

    def block(values):
        lines = [jnp.pad(v[None], ((0, 0), (0, width - v.shape[0]))) for v in values]
        return jnp.pad(jnp.concatenate(lines, 0), ((0, 16 - len(values)), (0, 0)))

    small_block = block([second_gain, second_shift])
    smalls = [in_bias, out_bias, down_bias, first_gain, first_shift]

    def own_half(value, at=core):
        return lax.dynamic_slice_in_dim(value, at * half, half, 0)

    up_pieces = own_half(up_weight).reshape(half, shards, hidden).transpose(1, 0, 2)
    shared = to_all_value(jnp.concatenate([x, grad, small_block], 0), shards)
    skip = -(-(2 * tokens + 16) // (half // 2)) * (half // 2)
    if joined:
        gap = jnp.zeros((shards, skip - 2 * tokens - 16, width), BF)
        plane = spread_out(jnp.concatenate([shared, gap, up_pieces], 1), "fsdp")
        up_own = plane[:, skip:]
    else:
        plane, up_own = spread_out(shared, "fsdp"), spread_out(up_pieces, "fsdp")
    later = after(core, plane)
    in_own = own_half(in_weight, later).reshape(half, 3, groups, cols)
    in_own = lax.dynamic_index_in_dim(in_own, group, 2, keepdims=False).reshape(half, 3 * cols)
    in_own = jnp.pad(in_own, ((0, 0), (0, width - 3 * cols)))
    io_send = to_all_value(jnp.concatenate([own_half(out_weight, later), in_own, block(smalls)], 0), shards)
    io_got = spread_out(io_send, "fsdp")
    small_got, io_got = io_got[:, 2 * half:].astype(F32), io_got[:, :2 * half]

    full_in_bias, full_out_bias, full_down_bias, gain_one, shift_one = [
        small_got[:, i, :s.shape[0]].reshape(-1) for i, s in enumerate(smalls)]

    small_step = rows // owners
    packed = joined and small_step % 8 == 0
    up_other, up_bias_row = swap(up_own), up_bias.astype(F32)[None]
    *ff_parts, up_part, down_part, up_bias_part, gain_two_part, shift_two_part = feed_forward(
        jnp.stack([core, shard]), plane, tokens, plane if joined else up_own, up_other, skip, down_weight,
        up_bias_row, owners if packed else 0)

    def give_half(pieces, axis, mine=core):
        keep = lax.dynamic_index_in_dim(pieces, mine, axis, keepdims=False)
        give = lax.dynamic_index_in_dim(pieces, 1 - mine, axis, keepdims=False)
        return (keep.astype(F32) + swap(give).astype(F32)).astype(BF)

    def reduce_owners(pieces):
        return lax.psum_scatter(pieces, "ctx", scatter_dimension=0, tiled=False)

    def gather_owners(value):
        mine = to_all(value, "ctx", parity, owners // 2)
        return mine, swap(mine)

    cut = shards * small_step
    if packed:
        summed = reduce_owners(up_part + after(after(jnp.int32(0), both_all), io_got).astype(BF))
        up_sum, down_sum = summed[:cut], summed[cut:]
    else:
        up_pieces = up_part.reshape(shards, owners, small_step, hidden).transpose(1, 0, 2, 3)
        up_sum = reduce_owners(up_pieces.reshape(owners, cut, hidden))
        down_sum = reduce_owners(down_part.reshape(owners, hidden // owners, width))

    io_full = both(io_got, swap(io_got)).reshape(shards, 2, 2, half, width)
    out_full = io_full[:, :, 0].reshape(width, width)
    in_full = io_full[:, :, 1].reshape(width, width)[:, :3 * cols].T
    out_own = lax.dynamic_slice_in_dim(out_full, group * cols, cols, 0)
    run_at = both_all[:, 2 * tokens, :held].reshape(-1).astype(jnp.int32)
    runs = run_at.shape[0]
    at_run = lax.broadcasted_iota(jnp.int32, (runs, runs), 0)
    of_run = lax.broadcasted_iota(jnp.int32, (runs, runs), 1)
    order = jnp.sum(jnp.where(run_at[None] == at_run, of_run, 0), 1)

    ladder = 10000.0 ** (-jnp.arange(0, ROT, 2, dtype=F32) / ROT)
    angle = jnp.arange(length, dtype=jnp.int32).astype(F32).reshape(tiles, 1, TILE) * ladder[None, :, None]
    cosine, sine = jnp.cos(angle), jnp.sin(angle)

    bias_own = lax.dynamic_index_in_dim(full_in_bias.reshape(3, groups, cols), group, 1, keepdims=False)
    qkv = project(order, both_all, in_full, out_own, bias_own.reshape(-1, 1), gain_one[None], shift_one[None],
                  cosine, sine)
    spots = jnp.concatenate([sharer[None].astype(jnp.int32), order])
    ff_got = at_distance(ff_parts)
    mixed_out, back_qkv = attend(spots, qkv, cosine, sine, owners, sharers)
    up_sum = jnp.concatenate(by_distance(up_sum.reshape(shards, small_step, hidden), after(shard, back_qkv)), 0)
    mixed_own = give_half(mixed_out.reshape(owners // 2, 2, own_heads, held, HEAD, RUN), 1)
    mixed_got = spread_out(mixed_own, "ctx", parity)
    if joined:
        ff_own = jnp.concatenate([up_sum, down_sum], 0)
        ff_all = lax.all_gather(ff_own, "ctx", axis=0, tiled=False)
        up_all, down_all = ff_all[:, :cut], ff_all[:, cut:]
    else:
        ff_own = up_sum
        up_all, down_all = [lax.all_gather(v, "ctx", axis=0, tiled=False) for v in (up_sum, down_sum)]
    gain_row, shift_row = gain_one[None], shift_one[None]
    in_part, out_part, in_bias_part, gain_one_part, shift_one_part = back_to_weight(
        order, back_qkv, in_full, both_all, mixed_out, gain_row, shift_row, (mixed_own, ff_own))
    e_runs = back_to_input(order, back_qkv, in_full, gain_row, (in_part, mixed_got))
    e_sum = lax.psum_scatter(e_runs.reshape(length, width), "ctx", scatter_dimension=0, tiled=True)

    if packed:
        up_weight_gradient, down_weight_gradient = place_ff(shard[None], ff_all, shards, small_step)
    else:
        up_all = up_all.reshape(owners, shards, small_step, hidden)
        up_all = [lax.dynamic_index_in_dim(up_all, shard ^ f, 1, keepdims=False) for f in range(shards)]
        up_weight_gradient = jnp.concatenate(up_all, -1).reshape(rows, shards * hidden).astype(F32)
        down_weight_gradient = down_all.reshape(hidden, width).astype(F32)

    ff_sum = total(ff_got) + after(jnp.int32(0), down_weight_gradient).astype(F32)
    x32, grad32 = x.astype(F32), grad.astype(F32)
    mixed = jnp.sum(mixed_got.astype(F32).reshape(groups, sharers // 2, own_heads, held, HEAD, RUN), 1)
    mixed = mixed.transpose(0, 1, 3, 2, 4).reshape(width, tokens).astype(BF)
    branch = mm(mixed, out_full, (0, 0))
    output = x32 + (branch + full_out_bias) + (ff_sum[:tokens] + full_down_bias)

    in_bias_full = lax.dynamic_update_slice_in_dim(
        jnp.zeros((3, groups, cols), F32), in_bias_part.reshape(3, 1, cols), group, 1)
    lines = [in_bias_full.reshape(-1), jnp.sum(grad32, 0), gain_one_part[0], shift_one_part[0], gain_two_part[0],
             shift_two_part[0]]
    lines = [v.reshape(shards, -1) for v in lines]
    at_shard = (jnp.arange(shards) == shard)[:, None]
    lines.append(jnp.where(at_shard, up_bias_part, 0.0))
    line_sizes = [v.shape[1] for v in lines]
    lines = jnp.concatenate(lines, 1).astype(BF).reshape(shards, 2, -1, width - 3 * cols)
    line_rows = lines.shape[2]
    lines = jnp.pad(lines, ((0, 0), (0, 0), (0, half - line_rows), (0, 0)))
    out_rows = lax.dynamic_update_slice_in_dim(
        jnp.zeros((width, width), BF), out_part.astype(BF), group * cols, 0)
    in_pieces = jnp.concatenate([in_part.reshape(shards, 2, half, 3 * cols), lines], 3)
    pieces = jnp.concatenate([out_rows.reshape(shards, 2, half, width), in_pieces], 2)
    pieces = give_half(pieces, 1)
    pieces = total(by_distance(pieces, shard)).astype(BF)
    pieces = pieces + after(jnp.int32(0), down_weight_gradient).astype(BF)
    in_weight_gradient, out_weight_gradient, line_sum = place_io(
        core, *gather_owners(pieces), cols)
    line_sum = line_sum.reshape(2, half, -1)[:, :line_rows].reshape(-1)
    totals, at = [], 0
    for size in line_sizes:
        totals.append(line_sum[at:at + size])
        at += size

    e = e_sum.astype(F32) + ff_sum[tokens:]
    xhat, inverse = normalize(x32)
    input_gradient = grad32 + inverse * (
        e - jnp.mean(e, -1, keepdims=True) - xhat * jnp.mean(e * xhat, -1, keepdims=True))
    return (
        output.astype(BF)[None], input_gradient[None], in_weight_gradient, totals[0], out_weight_gradient, totals[1],
        up_weight_gradient, totals[6], down_weight_gradient, totals[1], totals[2], totals[3], totals[4], totals[5],
    )


def solution(mesh):
    token, matrix, vector = P("fsdp", "ctx", None), P("fsdp", None), P("fsdp")
    return jax.shard_map(
        on_device,
        mesh=mesh,
        in_specs=(token, P("fsdp", "ctx"), matrix, vector, matrix, vector, matrix, vector, matrix, vector,
                  vector, vector, vector, vector, token),
        out_specs=(token, token, matrix, vector, matrix, vector, matrix, vector, matrix, vector,
                   vector, vector, vector, vector),
        check_vma=False,
    )
```

time: 448 us -> 308 us (0.69)
  blocking collectives: 54 us -> 0 us
  waiting for transfers between devices: 159 us -> 109 us
  local copies, waits for them, and re-layouts: 58.9 us -> 31.6 us
  other arithmetic: 39.9 us -> 23.2 us
  between operations: 14.4 us -> 21.1 us
    all_to_all x3 -> x0, blocking collectives: 54 us -> none  [spread_out(): return lax.all_to_all(pieces, axis, 0, 0, axis_index_groups=groups)]
    all_to_all x8 -> x4, waiting for transfers between devices: 135 us -> 93.2 us  [spread_out(): return lax.all_to_all(pieces, axis, 0, 0, axis_index_groups=groups)]
    all_gather x1 -> x2, waiting for transfers between devices: 17.4 us -> 0.01 us  [the longest x1 0.01 us: on_device(): lax.all_gather(jnp.concatenate([x, grad, run_rows], 0), 'ctx', axis=0, ti...]
    all_to_all x8 -> x4, starting transfers between devices: 30.7 us -> 18.4 us  [spread_out(): return lax.all_to_all(pieces, axis, 0, 0, axis_index_groups=groups)]
    convert_element_type x8 -> x5, other arithmetic: 15.5 us -> 3.18 us  [the longest x2 2.42 us: give_half(): return (keep.astype(F32) + swap(give).astype(F32)).astype(BF)]
    ppermute x0 -> x9, waiting for transfers between devices: none -> 11.3 us  [at_distance(): lax.ppermute(pieces[k], 'fsdp', [(i, i ^ k) for i in range(count)])]
    another operation x4 -> x3, local copies, waits for them, and re-layouts: 12.4 us -> 1.41 us  [the longest x1 0.66 us: on_device(): gain_one[None]]
    ppermute x0 -> x9, starting transfers between devices: none -> 10.7 us  [at_distance(): lax.ppermute(pieces[k], 'fsdp', [(i, i ^ k) for i in range(count)])]
  transfers between devices with their start and end apart: 16 -> 22, of which waited for: 11 -> 10; matrix products, arithmetic and copies ran while one was open for 10% -> 12% of each run, Pallas kernels for 16% -> 28%
where the time goes in v2:
time: 308 us; the launch traced here: 306 us
  waiting for transfers between devices  109 us (35%)
  Pallas kernels  90.3 us (29%)
  local copies, waits for them, and re-layouts  31.6 us (10%)
  starting transfers between devices  29.6 us (10%)
  other arithmetic  23.2 us (8%)
  between operations  21.1 us (7%)
    all_to_all x4, waiting for transfers between devices, spread_out(): return lax.all_to_all(pieces, axis, 0, 0, axis_index_groups=groups)  93.2 us
    pallas_call x1, Pallas kernels, attend(): pl.pallas_call(functools.partial(attention_kernel, share, fused, held), g...  31.1 us
    all_to_all x4, starting transfers between devices, spread_out(): return lax.all_to_all(pieces, axis, 0, 0, axis_index_groups=groups)  18.4 us
    pallas_call x1, Pallas kernels, feed_forward(): pl.pallas_call(functools.partial(ff_kernel, bool(owners)), grid_spec=pltp...  16.2 us
    pallas_call x1, Pallas kernels, back_to_weight(): pl.pallas_call(back_weight_kernel, grid_spec=pltpu.PrefetchScalarGridSpec...  12.7 us
    pallas_call x1, Pallas kernels, project(): pl.pallas_call(qkv_kernel, grid_spec=pltpu.PrefetchScalarGridSpec(num_sca...  11.5 us
    ppermute x9, waiting for transfers between devices, at_distance(): lax.ppermute(pieces[k], 'fsdp', [(i, i ^ k) for i in range(count)])  11.3 us
    ppermute x9, starting transfers between devices, at_distance(): lax.ppermute(pieces[k], 'fsdp', [(i, i ^ k) for i in range(count)])  10.7 us
  transfers between devices with their start and end apart: 22, of which 10 were waited for; matrix products, arithmetic and copies ran while one was open for 12% of the time, Pallas kernels for 28%

profile of v2, /device:TPU:0, one launch (start us, length us, event | category | flops | bytes accessed | tf_op | source)
XLA Modules:
  0.0 306.4 jit_solution(4507594134390494790)
XLA Ops:
  9.5 2.1 pad_maximum_fusion.2
  11.9 2.2 pad_maximum_fusion
  14.2 5.3 %all-to-all-start = ((bf16[4,624,768]{2,1,0:T(8,128)(2,1)}), bf16[4,624,768]{2,1,0:T(8,128)(2,1)}, u32[]{:S(2)}, u32[]{:S(2)}) async-start(bf16[4,624,768]{2,1,0:T(8,128)(2,1)} %pad_maximum_fusion), calls=%async_computation | async-start | bytes 7667712 | tf_op jit(solution)/shard_map/all_to_all | solution.py:520
  19.9 44.3 %all-to-all-done.x_ref.g_ref.small_ref.mine_ref.mine_end_ref = bf16[4,624,768]{2,1,0:T(8,128)(2,1)} async-done(((bf16[4,624,768]{2,1,0:T(8,128)(2,1)}), bf16[4,624,768]{2,1,0:T(8,128)(2,1)}, u32[]{:S(2)}, u32[]{:S(2)}) %all-to-all-start) | async-done | bytes 3833888 | tf_op jit(solution)/shard_map/all_to_all | solution.py:520
  69.6 3.7 %all-to-all-start.1 = ((bf16[4,208,768]{2,1,0:T(8,128)(2,1)}), bf16[4,208,768]{2,1,0:T(8,128)(2,1)S(1)}, u32[]{:S(2)}, u32[]{:S(2)}) async-start(bf16[4,208,768]{2,1,0:T(8,128)(2,1)} %broadcast_in_dim.111), calls=%async_computation.1 | async-start | bytes 2555904 | tf_op jit(solution)/shard_map/all_to_all | solution.py:520
  76.7 12.4 %all-to-all-done.1 = bf16[4,208,768]{2,1,0:T(8,128)(2,1)S(1)} async-done(((bf16[4,208,768]{2,1,0:T(8,128)(2,1)}), bf16[4,208,768]{2,1,0:T(8,128)(2,1)S(1)}, u32[]{:S(2)}, u32[]{:S(2)}) %all-to-all-start.1) | async-done | bytes 1277984 | tf_op jit(solution)/shard_map/all_to_all | solution.py:520
  89.3 16.2 %feed_forward.1 = (bf16[512,768]{1,0:T(8,128)(2,1)}, bf16[512,768]{1,0:T(8,128)(2,1)}, bf16[512,768]{1,0:T(8,128)(2,1)}, bf16[512,768]{1,0:T(8,128)(2,1)}, bf16[...) custom-call(s32[2]{0:T(128)} %pad_add_fusion.1.core_ref, ...), custom_call_target="tpu_custom_call" | custom-call | flops 14495514624 | bytes 7667712 | tf_op jit(solution)/shard_map/feed_forward/pallas_call | solution.py:134
  109.8 2.4 broadcast_select_fusion
  114.7 3.2 %broadcast_add_fusion = bf16[8,192,768]{2,1,0:T(8,128)(2,1)} fusion(bf16[8,192,768]{2,1,0:T(8,128)(2,1)} %get-tuple-element.39, bf16[]{:T(256)} %bitcast.18), kind=kLoop, calls=%fused_computation.24 | loop fusion | flops 1179648 | bytes 4718594 | tf_op jit(solution)/shard_map/add | solution.py:638
  123.3 11.5 %project.1.q_ref.k_ref.v_ref.d_ref = bf16[12,8,64,256]{3,2,1,0:T(8,128)(2,1)} custom-call(s32[16]{0:T(128)} %copy-done.34, bf16[8,528,768]{2,1,0:T(8,128)(2,1)} %bitcast.109, bf16[8,528,768]{2,1,0:T(8,128)(2,1)} %bitcast.110, bf16[8,528,768]{2,1,0:T(8,128)(2,1)} %bitcast.111, bf16[8,528,768]{2,1,0:T(8,128)(2,1)} %bitcast.112, bf16[576,768]{1,0:T(8,128)(2,1)} %bitcast.97, ...), custom_call_target="tpu_custom_call" | custom-call | flops 12079595520 | bytes 12976128 | tf_op jit(solution)/shard_map/project/pallas_call | solution.py:194
  134.8 31.1 %attend.1 = (bf16[8,3,2,64,128]{4,3,2,1,0:T(8,128)(2,1)}, bf16[9,8,64,256]{3,2,1,0:T(8,128)(2,1)}) custom-call(s32[17]{0:T(128)} %pad_add_fusion.place_ref, bf16[12,8,64,256]{3,2,1,0:T(8,128)(2,1)} %project.1.q_ref.k_ref.v_ref.d_ref, bf16[12,8,64,256]{3,2,1,0:T(8,128)(2,1)} %project.1.q_ref.k_ref.v_ref.d_ref, ...), custom_call_target="tpu_custom_call" | custom-call | flops 32212254720 | bytes 6291456 | tf_op jit(solution)/shard_map/attend/pallas_call | solution.py:324
  169.5 1.5 collective-permute-start.8
  171.0 1.5 collective-permute-start.7
  173.1 3.4 %collective-permute-done.6 = bf16[24,768]{1,0:T(8,128)(2,1)S(1)} collective-permute-done((bf16[24,768]{1,0:T(8,128)(2,1)S(1)}, bf16[24,768]{1,0:T(8,128)(2,1)S(1)}, u32[]{:S(2)}, u32[]{:S(2)}) %collective-permute-start.6) | collective-permute-done | bytes 36896 | tf_op jit(solution)/shard_map/ppermute | solution.py:534
  178.4 1.7 collective-permute-done.1
  180.9 4.8 %all-to-all-start.2 = ((bf16[4,3,2,64,128]{4,3,2,1,0:T(8,128)(2,1)}), bf16[4,3,2,64,128]{4,3,2,1,0:T(8,128)(2,1)S(1)}, u32[]{:S(2)}, u32[]{:S(2)}) async-start(bf16[4,3,2,64,128]{4,3,2,1,0:T(8,128)(2,1)} %fusion.22._), calls=%async_computation.2 | async-start | bytes 786432 | tf_op jit(solution)/shard_map/all_to_all | solution.py:520
  185.7 12.7 %back_to_weight.1 = (bf16[768,576]{1,0:T(8,128)(2,1)}, f32[192,768]{1,0:T(8,128)}, f32[576,1]{1,0:T(8,128)}, f32[1,768]{1,0:T(1,128)}, f32[1,768]{1,0:T(1,128)}) custom-call(s32[16]{0:T(128)} %copy-done.34, bf16[9,8,64,256]{3,2,1,0:T(8,128)(2,1)} %get-tuple-element.40.b_ref, bf16[576,768]{1,0:T(8,128)(2,1)} %bitcast.98, bf16[8,528,768]{2,1,0:T(8,128)(2,1)} %bitcast.113, ...), custom_call_target="tpu_custom_call" | custom-call | flops 9059696640 | bytes 12976128 | tf_op jit(solution)/shard_map/back_to_weight/pallas_call | solution.py:406
  198.5 9.1 %all-to-all-done.2.__ = bf16[4,3,2,64,128]{4,3,2,1,0:T(8,128)(2,1)S(1)} async-done(((bf16[4,3,2,64,128]{4,3,2,1,0:T(8,128)(2,1)}), bf16[4,3,2,64,128]{4,3,2,1,0:T(8,128)(2,1)S(1)}, u32[]{:S(2)}, u32[]{:S(2)}) %all-to-all-start.2) | async-done | bytes 393248 | tf_op jit(solution)/shard_map/all_to_all | solution.py:520
  208.3 9.2 %back_to_input.1 = bf16[16,128,768]{2,1,0:T(8,128)(2,1)} custom-call(s32[16]{0:T(128)} %copy-done.34, bf16[9,8,64,256]{3,2,1,0:T(8,128)(2,1)} %get-tuple-element.40.b_ref, bf16[576,768]{1,0:T(8,128)(2,1)} %bitcast.99, f32[1,768]{1,0:T(1,128)} %broadcast_in_dim_reshape_squeeze.4.gain_ref, bf16[768,576]{1,0:T(8,128)(2,1)} %get-tuple-element.42._, ...), custom_call_target="tpu_custom_call" | custom-call | flops 9059696640 | bytes 9437184 | tf_op jit(solution)/shard_map/back_to_input/pallas_call | solution.py:430
  222.7 2.9 collective-permute-done.9
  225.7 1.5 fusion.5
  227.9 1.5 collective-permute-start.12
  229.4 1.4 collective-permute-start.11
  230.9 6.1 %place_ff.1 = (f32[192,3072]{1,0:T(8,128)}, f32[768,768]{1,0:T(8,128)}) custom-call(s32[1]{0:T(128)} %bitcast.17.at_ref, bf16[8,192,768]{2,1,0:T(8,128)(2,1)} %bitcast.90), custom_call_target="tpu_custom_call" | custom-call | tf_op jit(solution)/shard_map/place_ff/pallas_call | solution.py:459
  239.5 3.4 %collective-permute-done.12 = bf16[192,768]{1,0:T(8,128)(2,1)S(1)} collective-permute-done((bf16[192,768]{1,0:T(8,128)(2,1)S(1)}, bf16[192,768]{1,0:T(8,128)(2,1)S(1)}, u32[]{:S(2)}, u32[]{:S(2)}) %collective-permute-start.12) | collective-permute-done | bytes 294944 | tf_op jit(solution)/shard_map/ppermute | solution.py:534
  245.6 4.6 %all-to-all-start.3 = ((bf16[4,192,768]{2,1,0:T(8,128)(2,1)}), bf16[4,192,768]{2,1,0:T(8,128)(2,1)}, u32[]{:S(2)}, u32[]{:S(2)}) async-start(bf16[4,192,768]{2,1,0:T(8,128)(2,1)} %broadcast_in_dim.122), calls=%async_computation.5 | async-start | bytes 2359296 | tf_op jit(solution)/shard_map/all_to_all | solution.py:520
  250.2 1.5 collective-permute-start.3
  252.3 1.5 collective-permute-start.5
  255.3 27.4 %all-to-all-done.3.mine_ref = bf16[4,192,768]{2,1,0:T(8,128)(2,1)} async-done(((bf16[4,192,768]{2,1,0:T(8,128)(2,1)}), bf16[4,192,768]{2,1,0:T(8,128)(2,1)}, u32[]{:S(2)}, u32[]{:S(2)}) %all-to-all-start.3) | async-done | bytes 1179680 | tf_op jit(solution)/shard_map/all_to_all | solution.py:520
  282.8 3.1 %collective-permute-done.4 = bf16[512,768]{1,0:T(8,128)(2,1)S(1)} collective-permute-done((bf16[512,768]{1,0:T(8,128)(2,1)}, bf16[512,768]{1,0:T(8,128)(2,1)S(1)}, u32[]{:S(2)}, u32[]{:S(2)}) %collective-permute-start.4) | collective-permute-done | bytes 786464 | tf_op jit(solution)/shard_map/ppermute | solution.py:534
  287.1 2.3 add_add_fusion
  293.4 3.3 %place_io.1 = (f32[192,2304]{1,0:T(8,128)}, f32[192,768]{1,0:T(8,128)}, f32[192,192]{1,0:T(8,128)}) custom-call(s32[1]{0:T(128)} %bitcast.1.core_ref, bf16[4,192,768]{2,1,0:T(8,128)(2,1)} %all-to-all-done.3.mine_ref, bf16[4,192,768]{2,1,0:T(8,128)(2,1)} %collective-permute-done.13.other_ref), custom_call_target="tpu_custom_call" | custom-call | tf_op jit(solution)/shard_map/place_io/pallas_call | solution.py:502
  (211 shorter events, 46.1 us)
Async XLA Ops:
  7.2 105.0 %all-gather.5.cloned.1.call-start = ((), (), s32[]{:S(2)}) async-start(), calls=%async_computation.8 | async-start | bytes 7299072 | tf_op jit(solution)/shard_map/all_gather | solution.py:585
  14.2 5.4 %copy-start.31 = (bf16[192]{0:T(256)(128)(2,1)S(1)}, bf16[192]{0:T(256)(128)(2,1)}, u32[]{:S(2)}) copy-start(bf16[192]{0:T(256)(128)(2,1)} %param.24) | copy-start | bytes 1156
  14.2 5.4 %copy-start.32 = (bf16[192]{0:T(256)(128)(2,1)S(1)}, bf16[192]{0:T(256)(128)(2,1)}, u32[]{:S(2)}) copy-start(bf16[192]{0:T(256)(128)(2,1)} %param.25) | copy-start | bytes 1156
  14.2 5.4 %copy-start.33 = (bf16[192]{0:T(256)(128)(2,1)S(1)}, bf16[192]{0:T(256)(128)(2,1)}, u32[]{:S(2)}) copy-start(bf16[192]{0:T(256)(128)(2,1)} %param.26) | copy-start | bytes 1156
  14.2 5.5 %copy-start.28 = (bf16[576]{0:T(1024)(128)(2,1)S(1)}, bf16[576]{0:T(1024)(128)(2,1)}, u32[]{:S(2)}) copy-start(bf16[576]{0:T(1024)(128)(2,1)} %param.18) | copy-start | bytes 3460
  14.2 52.5 %copy-start.20 = (bf16[192,768]{1,0:T(8,128)(2,1)S(1)}, bf16[192,768]{1,0:T(8,128)(2,1)}, u32[]{:S(2)}) copy-start(bf16[192,768]{1,0:T(8,128)(2,1)} %param.19) | copy-start | bytes 884740
  14.2 52.7 %copy-start.18 = (bf16[192,2304]{1,0:T(8,128)(2,1)S(1)}, bf16[192,2304]{1,0:T(8,128)(2,1)}, u32[]{:S(2)}) copy-start(bf16[192,2304]{1,0:T(8,128)(2,1)} %param.17) | copy-start | bytes 2654212
  14.2 50.0 %all-to-all-start = ((bf16[4,624,768]{2,1,0:T(8,128)(2,1)}), bf16[4,624,768]{2,1,0:T(8,128)(2,1)}, u32[]{:S(2)}, u32[]{:S(2)}) async-start(bf16[4,624,768]{2,1,0:T(8,128)(2,1)} %pad_maximum_fusion), calls=%async_computation | async-start | bytes 7667712 | tf_op jit(solution)/shard_map/all_to_all | solution.py:520
  69.6 19.5 %all-to-all-start.1 = ((bf16[4,208,768]{2,1,0:T(8,128)(2,1)}), bf16[4,208,768]{2,1,0:T(8,128)(2,1)S(1)}, u32[]{:S(2)}, u32[]{:S(2)}) async-start(bf16[4,208,768]{2,1,0:T(8,128)(2,1)} %broadcast_in_dim.111), calls=%async_computation.1 | async-start | bytes 2555904 | tf_op jit(solution)/shard_map/all_to_all | solution.py:520
  73.3 95.3 %reduce-scatter.3.cloned.1.call-start = ((), (), s32[]{:S(2)}) async-start(), calls=%async_computation.6 | async-start | bytes 2654208 | tf_op jit(solution)/shard_map/reduce_scatter | solution.py:630
  74.5 14.8 %collective-permute-start.2 = (bf16[4,96,768]{2,1,0:T(8,128)(2,1)S(1)}, bf16[4,96,768]{2,1,0:T(8,128)(2,1)}, u32[]{:S(2)}, u32[]{:S(2)}) collective-permute-start(bf16[4,96,768]{2,1,0:T(8,128)(2,1)S(1)} %slice.138), channel_id=1, source_target_pairs={{0,1},{1,0},{2,3},{3,2},{4,5},{5,4},{6,7},{7,6},{8,9},{9,8},{10,11... | collective-permute-start | bytes 1769480 | tf_op jit(solution)/shard_map/ppermute | solution.py:579
  89.2 20.6 %collective-permute-start = (bf16[4,192,768]{2,1,0:T(8,128)(2,1)S(1)}, bf16[4,192,768]{2,1,0:T(8,128)(2,1)}, u32[]{:S(2)}, u32[]{:S(2)}) collective-permute-start(bf16[4,192,768]{2,1,0:T(8,128)(2,1)S(1)} %slice.129), channel_id=1, source_target_pairs={{0,1},{1,0},{2,3},{3,2},{4,5},{5,4},{6,7},{7,6},{8,9},{9,8},{10,11... | collective-permute-start | bytes 3538952 | tf_op jit(solution)/shard_map/ppermute | solution.py:579
  118.0 112.9 %all-gather.7.cloned.1.call-start = ((), (), s32[]{:S(2)}) async-start(), calls=%async_computation.9 | async-start | bytes 2654208 | tf_op jit(solution)/shard_map/all_gather | solution.py:670
  166.0 12.3 %copy-start.14 = (bf16[8,3,2,64,128]{4,3,2,1,0:T(8,128)(2,1)S(1)}, bf16[8,3,2,64,128]{4,3,2,1,0:T(8,128)(2,1)}, u32[]{:S(2)}) copy-start(bf16[8,3,2,64,128]{4,3,2,1,0:T(8,128)(2,1)} %get-tuple-element.34.ma_ref.mb_ref) | copy-start | bytes 2359300
  169.5 7.0 %collective-permute-start.8 = (bf16[24,768]{1,0:T(8,128)(2,1)S(1)}, bf16[24,768]{1,0:T(8,128)(2,1)S(1)}, u32[]{:S(2)}, u32[]{:S(2)}) collective-permute-start(bf16[24,768]{1,0:T(8,128)(2,1)S(1)} %get-tuple-element.69), channel_id=1, source_target_pairs={{0,24},{8,16},{16,8},{24,0},{1,25},{9,17},{17,9},{25,1},{2,26},{10... | collective-permute-start | bytes 110600 | tf_op jit(solution)/shard_map/ppermute | solution.py:534
  171.0 5.5 %collective-permute-start.7 = (bf16[24,768]{1,0:T(8,128)(2,1)S(1)}, bf16[24,768]{1,0:T(8,128)(2,1)S(1)}, u32[]{:S(2)}, u32[]{:S(2)}) collective-permute-start(bf16[24,768]{1,0:T(8,128)(2,1)S(1)} %get-tuple-element.70), channel_id=1, source_target_pairs={{0,16},{8,24},{16,0},{24,8},{1,17},{9,25},{17,1},{25,9},{2,18},{10... | collective-permute-start | bytes 110600 | tf_op jit(solution)/shard_map/ppermute | solution.py:534
  172.6 4.0 %collective-permute-start.6 = (bf16[24,768]{1,0:T(8,128)(2,1)S(1)}, bf16[24,768]{1,0:T(8,128)(2,1)S(1)}, u32[]{:S(2)}, u32[]{:S(2)}) collective-permute-start(bf16[24,768]{1,0:T(8,128)(2,1)S(1)} %get-tuple-element.71), channel_id=1, source_target_pairs={{0,8},{8,0},{16,24},{24,16},{1,9},{9,1},{17,25},{25,17},{2,10},{10... | collective-permute-start | bytes 110600 | tf_op jit(solution)/shard_map/ppermute | solution.py:534
  178.3 1.8 collective-permute-start.1
  180.9 26.6 %all-to-all-start.2 = ((bf16[4,3,2,64,128]{4,3,2,1,0:T(8,128)(2,1)}), bf16[4,3,2,64,128]{4,3,2,1,0:T(8,128)(2,1)S(1)}, u32[]{:S(2)}, u32[]{:S(2)}) async-start(bf16[4,3,2,64,128]{4,3,2,1,0:T(8,128)(2,1)} %fusion.22._), calls=%async_computation.2 | async-start | bytes 786432 | tf_op jit(solution)/shard_map/all_to_all | solution.py:520
  185.7 105.0 %reduce-scatter.5.cloned.1.call-start = ((), (), s32[]{:S(2)}) async-start(), calls=%async_computation.7 | async-start | bytes 3538944 | tf_op jit(solution)/shard_map/reduce_scatter | solution.py:679
  222.6 3.0 collective-permute-start.9
  227.3 12.2 %collective-permute-start.10 = (bf16[192,768]{1,0:T(8,128)(2,1)S(1)}, bf16[192,768]{1,0:T(8,128)(2,1)S(1)}, u32[]{:S(2)}, u32[]{:S(2)}) collective-permute-start(bf16[192,768]{1,0:T(8,128)(2,1)S(1)} %get-tuple-element.64), channel_id=1, source_target_pairs={{0,8},{8,0},{16,24},{24,16},{1,9},{9,1},{17,25},{25,17},{2,10},{10... | collective-permute-start | bytes 884744 | tf_op jit(solution)/shard_map/ppermute | solution.py:534
  227.9 15.0 %collective-permute-start.12 = (bf16[192,768]{1,0:T(8,128)(2,1)S(1)}, bf16[192,768]{1,0:T(8,128)(2,1)S(1)}, u32[]{:S(2)}, u32[]{:S(2)}) collective-permute-start(bf16[192,768]{1,0:T(8,128)(2,1)S(1)} %get-tuple-element.65), channel_id=1, source_target_pairs={{0,24},{8,16},{16,8},{24,0},{1,25},{9,17},{17,9},{25,1},{2,26},{10... | collective-permute-start | bytes 884744 | tf_op jit(solution)/shard_map/ppermute | solution.py:534
  229.4 14.8 %collective-permute-start.11 = (bf16[192,768]{1,0:T(8,128)(2,1)S(1)}, bf16[192,768]{1,0:T(8,128)(2,1)S(1)}, u32[]{:S(2)}, u32[]{:S(2)}) collective-permute-start(bf16[192,768]{1,0:T(8,128)(2,1)S(1)} %get-tuple-element.66), channel_id=1, source_target_pairs={{0,16},{8,24},{16,0},{24,8},{1,17},{9,25},{17,1},{25,9},{2,18},{10... | collective-permute-start | bytes 884744 | tf_op jit(solution)/shard_map/ppermute | solution.py:534
  244.4 9.3 %copy-start.2 = (bf16[1,256,768]{2,1,0:T(8,128)(2,1)S(1)}, bf16[1,256,768]{2,1,0:T(8,128)(2,1)}, u32[]{:S(2)}) copy-start(bf16[1,256,768]{2,1,0:T(8,128)(2,1)} %param.15) | copy-start | bytes 1179652
  245.6 9.3 %copy-start.9 = (bf16[4,3,2,64,128]{4,3,2,1,0:T(8,128)(2,1)S(1)}, bf16[4,3,2,64,128]{4,3,2,1,0:T(8,128)(2,1)}, u32[]{:S(2)}) copy-start(bf16[4,3,2,64,128]{4,3,2,1,0:T(8,128)(2,1)} %copy-done.8) | copy-start | bytes 1179652
  245.6 37.2 %all-to-all-start.3 = ((bf16[4,192,768]{2,1,0:T(8,128)(2,1)}), bf16[4,192,768]{2,1,0:T(8,128)(2,1)}, u32[]{:S(2)}, u32[]{:S(2)}) async-start(bf16[4,192,768]{2,1,0:T(8,128)(2,1)} %broadcast_in_dim.122), calls=%async_computation.5 | async-start | bytes 2359296 | tf_op jit(solution)/shard_map/all_to_all | solution.py:520
  250.2 32.6 %collective-permute-start.3 = (bf16[512,768]{1,0:T(8,128)(2,1)}, bf16[512,768]{1,0:T(8,128)(2,1)S(1)}, u32[]{:S(2)}, u32[]{:S(2)}) collective-permute-start(bf16[512,768]{1,0:T(8,128)(2,1)} %get-tuple-element.36), channel_id=1, source_target_pairs={{0,8},{8,0},{16,24},{24,16},{1,9},{9,1},{17,25},{25,17},{2,10},{10... | collective-permute-start | bytes 2359304 | tf_op jit(solution)/shard_map/ppermute | solution.py:534
  251.7 34.2 %collective-permute-start.4 = (bf16[512,768]{1,0:T(8,128)(2,1)}, bf16[512,768]{1,0:T(8,128)(2,1)S(1)}, u32[]{:S(2)}, u32[]{:S(2)}) collective-permute-start(bf16[512,768]{1,0:T(8,128)(2,1)} %get-tuple-element.37), channel_id=1, source_target_pairs={{0,16},{8,24},{16,0},{24,8},{1,17},{9,25},{17,1},{25,9},{2,18},{10... | collective-permute-start | bytes 2359304 | tf_op jit(solution)/shard_map/ppermute | solution.py:534
  252.3 33.7 %collective-permute-start.5 = (bf16[512,768]{1,0:T(8,128)(2,1)}, bf16[512,768]{1,0:T(8,128)(2,1)S(1)}, u32[]{:S(2)}, u32[]{:S(2)}) collective-permute-start(bf16[512,768]{1,0:T(8,128)(2,1)} %get-tuple-element.38), channel_id=1, source_target_pairs={{0,24},{8,16},{16,8},{24,0},{1,25},{9,17},{17,9},{25,1},{2,26},{10... | collective-permute-start | bytes 2359304 | tf_op jit(solution)/shard_map/ppermute | solution.py:534
  282.7 10.6 %collective-permute-start.13 = (bf16[4,192,768]{2,1,0:T(8,128)(2,1)}, bf16[4,192,768]{2,1,0:T(8,128)(2,1)}, u32[]{:S(2)}, u32[]{:S(2)}) collective-permute-start(bf16[4,192,768]{2,1,0:T(8,128)(2,1)} %all-to-all-done.3.mine_ref), channel_id=1, source_target_pairs={{0,1},{1,0},{2,3},{3,2},{4,5},{5,4},{6,7},{7,6},{8,9},{9,8},{10,11... | collective-permute-start | bytes 3538952 | tf_op jit(solution)/shard_map/ppermute | solution.py:579
  292.1 7.8 %copy-start.1 = (bf16[192,3072]{1,0:T(8,128)(2,1)S(1)}, bf16[192,3072]{1,0:T(8,128)(2,1)}, u32[]{:S(2)}) copy-start(bf16[192,3072]{1,0:T(8,128)(2,1)} %param.21) | copy-start | bytes 3538948
  (25 other events, 45.6 us)
Sparse Core Ops, SparseCore 0:
  11.7 69.0 all-gather.4
  118.1 36.5 reduce-scatter.2
  178.3 39.8 all-gather.6
  220.4 42.7 reduce-scatter.4

commit v3 on v2

--- a/solution.py
+++ b/solution.py
@@ -13,6 +13,7 @@
 HALF = ROT // 2
 RUN = 128
 TILE = 256
+SUB = 256
 NEG = -1e30
 EPS = 1e-05
 BF = jnp.bfloat16
@@ -107,6 +108,9 @@
         else:
             dup_ref[...] = acc_up[...].astype(BF)
             ddown_ref[...] = acc_down[...].astype(BF)
+
+
+ANY = pl.BlockSpec(memory_space=pl.ANY)
 
 
 def whole(shape):
@@ -234,14 +238,16 @@
     queries = [q_ref[h, 0] for h in every]
 
     def fold(x, op):
-        return op(x.reshape(TILE // 8, 8, TILE), 0)
+        return op(x.reshape(x.shape[0] // 8, 8, TILE), 0)
+
+    pieces = [(h, slice(i, i + SUB)) for h in every for i in range(0, TILE, SUB)]
 
     def score(j, peaks):
-        new = []
-        for h in every:
-            s = mm(keys[h, j], queries[h], (1, 0))
-            sbuf[h, j] = s
-            new.append(jnp.maximum(peaks[h], fold(s, jnp.max)))
+        new = list(peaks)
+        for h, at in pieces:
+            s = mm(keys[h, j, at], queries[h], (1, 0))
+            sbuf[h, j, at] = s
+            new[h] = jnp.maximum(new[h], fold(s, jnp.max))
         return tuple(new)
 
     peaks = lax.fori_loop(0, block, score, tuple(jnp.full((8, TILE), NEG, F32) for _ in every))
@@ -255,13 +261,16 @@
     peaks = last
 
     def weigh(j, carry):
-        new = []
-        for h in every:
-            total, mixed = carry[h]
-            p = jnp.exp(sbuf[h, j] - peaks[h])
+        new = list(carry)
+        for h, at in pieces:
+            total, mixed = new[h]
+            p = jnp.exp(sbuf[h, j, at] - peaks[h])
             low = p.astype(BF)
-            pbuf[h, j] = low
-            new.append((total + fold(p, jnp.sum), mixed + mm(v_ref[h, j], low, (1, 0))))
+            pbuf[h, j, at] = low
+            new[h] = (total + fold(p, jnp.sum), mixed)
+        for h, at in pieces:
+            total, mixed = new[h]
+            new[h] = (total, mixed + mm(v_ref[h, j, :, at], pbuf[h, j, at], (1, 0)))
         return tuple(new)
 
     sums = lax.fori_loop(
@@ -284,14 +293,18 @@
         query_rows.append(flip(queries[h]))
 
     def pull(j, dquery):
-        new = []
-        for h in every:
-            low = pbuf[h, j]
-            dp = mm(values[h, j], backs[h], (1, 0))
+        new = list(dquery)
+
+        def finish(h, at, dp):
+            low = pbuf[h, j, at]
             ds = (low.astype(F32) * (dp - spreads[h])).astype(BF)
-            dvalues[h, j] += mm(low, back_rows[h], (1, 0))
-            dkeys[h, j] += mm(ds, query_rows[h], (1, 0))
-            new.append(dquery[h] + mm(k_ref[h, j], ds, (1, 0)))
+            dvalues[h, j, at] += mm(low, back_rows[h], (1, 0))
+            dkeys[h, j, at] += mm(ds, query_rows[h], (1, 0))
+            new[h] = new[h] + mm(k_ref[h, j, :, at], ds, (1, 0))
+
+        dps = [mm(values[h, j, at], backs[h], (1, 0)) for h, at in pieces]
+        for (h, at), dp in zip(pieces, dps):
+            finish(h, at, dp)
         return tuple(new)
 
     dquery = lax.fori_loop(0, block + 1, pull, tuple(jnp.zeros((HEAD, TILE), F32) for _ in every))
@@ -387,9 +400,6 @@
     e_ref[order_ref[2 * step + 1]] = e[RUN:]
 
 
-ANY = pl.BlockSpec(memory_space=pl.ANY)
-
-
 def back_to_weight(order, back, w, both_all, mixed, gain, shift, earlier):
     owners, _, width = both_all.shape
     held = order.shape[0] // owners
@@ -635,13 +645,14 @@
 
     cut = shards * small_step
     if packed:
-        summed = reduce_owners(up_part + after(after(jnp.int32(0), both_all), io_got).astype(BF))
+        summed = reduce_owners(up_part + after(jnp.int32(0), both_all).astype(BF))
         up_sum, down_sum = summed[:cut], summed[cut:]
     else:
         up_pieces = up_part.reshape(shards, owners, small_step, hidden).transpose(1, 0, 2, 3)
         up_sum = reduce_owners(up_pieces.reshape(owners, cut, hidden))
         down_sum = reduce_owners(down_part.reshape(owners, hidden // owners, width))
 
+    io_got = io_got + after(jnp.int32(0), ff_parts[0]).astype(BF)
     io_full = both(io_got, swap(io_got)).reshape(shards, 2, 2, half, width)
     out_full = io_full[:, :, 0].reshape(width, width)
     in_full = io_full[:, :, 1].reshape(width, width)[:, :3 * cols].T
@@ -672,12 +683,10 @@
     else:
         ff_own = up_sum
         up_all, down_all = [lax.all_gather(v, "ctx", axis=0, tiled=False) for v in (up_sum, down_sum)]
+    x32, grad32 = x.astype(F32), grad.astype(F32)
     gain_row, shift_row = gain_one[None], shift_one[None]
     in_part, out_part, in_bias_part, gain_one_part, shift_one_part = back_to_weight(
         order, back_qkv, in_full, both_all, mixed_out, gain_row, shift_row, (mixed_own, ff_own))
-    e_runs = back_to_input(order, back_qkv, in_full, gain_row, (in_part, mixed_got))
-    e_sum = lax.psum_scatter(e_runs.reshape(length, width), "ctx", scatter_dimension=0, tiled=True)
-
     if packed:
         up_weight_gradient, down_weight_gradient = place_ff(shard[None], ff_all, shards, small_step)
     else:
@@ -686,8 +695,8 @@
         up_weight_gradient = jnp.concatenate(up_all, -1).reshape(rows, shards * hidden).astype(F32)
         down_weight_gradient = down_all.reshape(hidden, width).astype(F32)
 
+    mixed_got = mixed_got + after(jnp.int32(0), in_part).astype(BF)
     ff_sum = total(ff_got) + after(jnp.int32(0), down_weight_gradient).astype(F32)
-    x32, grad32 = x.astype(F32), grad.astype(F32)
     mixed = jnp.sum(mixed_got.astype(F32).reshape(groups, sharers // 2, own_heads, held, HEAD, RUN), 1)
     mixed = mixed.transpose(0, 1, 3, 2, 4).reshape(width, tokens).astype(BF)
     branch = mm(mixed, out_full, (0, 0))
@@ -708,7 +717,9 @@
         jnp.zeros((width, width), BF), out_part.astype(BF), group * cols, 0)
     in_pieces = jnp.concatenate([in_part.reshape(shards, 2, half, 3 * cols), lines], 3)
     pieces = jnp.concatenate([out_rows.reshape(shards, 2, half, width), in_pieces], 2)
-    pieces = give_half(pieces, 1)
+    pieces = give_half(pieces, 1, after(core, mixed_got))
+    e_runs = back_to_input(order, back_qkv, in_full, gain_row, (pieces, pieces))
+    e_sum = lax.psum_scatter(e_runs.reshape(length, width), "ctx", scatter_dimension=0, tiled=True)
     pieces = total(by_distance(pieces, shard)).astype(BF)
     pieces = pieces + after(jnp.int32(0), down_weight_gradient).astype(BF)
     in_weight_gradient, out_weight_gradient, line_sum = place_io(

time: 308 us -> 294 us (0.955)
  waiting for transfers between devices: 109 us -> 90.8 us
  Pallas kernels: 90.3 us -> 86.7 us
  local copies, waits for them, and re-layouts: 31.6 us -> 34.8 us
    all_to_all x4, waiting for transfers between devices: 93.2 us -> 79.8 us  [spread_out(): return lax.all_to_all(pieces, axis, 0, 0, axis_index_groups=groups)]
    pallas_call x1, Pallas kernels: 31.1 us -> 27.3 us  [attend(): pl.pallas_call(functools.partial(attention_kernel, share, fused, held), g...]
    ppermute x9, waiting for transfers between devices: 11.3 us -> 7.96 us  [at_distance(): lax.ppermute(pieces[k], 'fsdp', [(i, i ^ k) for i in range(count)])]
    slice x5 -> x7, local copies, waits for them, and re-layouts: 5.33 us -> 7.8 us  [after(): first = value[(0,) * value.ndim]]
    unnamed x79 -> x71, local copies, waits for them, and re-layouts: 7.48 us -> 6.82 us
  transfers between devices with their start and end apart: 22 -> 22, of which waited for: 10 -> 7; matrix products, arithmetic and copies ran while one was open for 12% -> 15% of each run, Pallas kernels for 28% -> 30%
where the time goes in v3:
time: 294 us; the launch traced here: 292 us
  waiting for transfers between devices  90.8 us (31%)
  Pallas kernels  86.7 us (29%)
  local copies, waits for them, and re-layouts  34.8 us (12%)
  starting transfers between devices  30.7 us (10%)
  other arithmetic  24.2 us (8%)
  between operations  23.7 us (8%)
    all_to_all x4, waiting for transfers between devices, spread_out(): return lax.all_to_all(pieces, axis, 0, 0, axis_index_groups=groups)  79.8 us
    pallas_call x1, Pallas kernels, attend(): pl.pallas_call(functools.partial(attention_kernel, share, fused, held), g...  27.3 us
    all_to_all x4, starting transfers between devices, spread_out(): return lax.all_to_all(pieces, axis, 0, 0, axis_index_groups=groups)  19 us
    pallas_call x1, Pallas kernels, feed_forward(): pl.pallas_call(functools.partial(ff_kernel, bool(owners)), grid_spec=pltp...  16.3 us
    pallas_call x1, Pallas kernels, back_to_weight(): pl.pallas_call(back_weight_kernel, grid_spec=pltpu.PrefetchScalarGridSpec...  12.8 us
    pallas_call x1, Pallas kernels, project(): pl.pallas_call(qkv_kernel, grid_spec=pltpu.PrefetchScalarGridSpec(num_sca...  11.5 us
    ppermute x9, starting transfers between devices, at_distance(): lax.ppermute(pieces[k], 'fsdp', [(i, i ^ k) for i in range(count)])  10.7 us
    pallas_call x1, Pallas kernels, back_to_input(): pl.pallas_call(back_input_kernel, grid_spec=pltpu.PrefetchScalarGridSpec(...  9.22 us
  transfers between devices with their start and end apart: 22, of which 7 were waited for; matrix products, arithmetic and copies ran while one was open for 15% of the time, Pallas kernels for 30%

profile of v3, /device:TPU:0, one launch (start us, length us, event | category | flops | bytes accessed | tf_op | source)
XLA Modules:
  0.0 292.2 jit_solution(10769698597569317773)
XLA Ops:
  9.5 2.1 pad_maximum_fusion.2
  11.9 2.2 pad_maximum_fusion
  14.2 5.3 %all-to-all-start = ((bf16[4,624,768]{2,1,0:T(8,128)(2,1)}), bf16[4,624,768]{2,1,0:T(8,128)(2,1)}, u32[]{:S(2)}, u32[]{:S(2)}) async-start(bf16[4,624,768]{2,1,0:T(8,128)(2,1)} %pad_maximum_fusion), calls=%async_computation | async-start | bytes 7667712 | tf_op jit(solution)/shard_map/all_to_all | solution.py:530
  21.1 43.2 %all-to-all-done.x_ref.g_ref.small_ref.mine_ref.mine_end_ref = bf16[4,624,768]{2,1,0:T(8,128)(2,1)} async-done(((bf16[4,624,768]{2,1,0:T(8,128)(2,1)}), bf16[4,624,768]{2,1,0:T(8,128)(2,1)}, u32[]{:S(2)}, u32[]{:S(2)}) %all-to-all-start) | async-done | bytes 3833888 | tf_op jit(solution)/shard_map/all_to_all | solution.py:530
  70.9 3.5 %all-to-all-start.1 = ((bf16[4,208,768]{2,1,0:T(8,128)(2,1)}), bf16[4,208,768]{2,1,0:T(8,128)(2,1)S(1)}, u32[]{:S(2)}, u32[]{:S(2)}) async-start(bf16[4,208,768]{2,1,0:T(8,128)(2,1)} %broadcast_in_dim.111), calls=%async_computation.1 | async-start | bytes 2555904 | tf_op jit(solution)/shard_map/all_to_all | solution.py:530
  74.7 16.3 %feed_forward.1 = (bf16[512,768]{1,0:T(8,128)(2,1)}, bf16[512,768]{1,0:T(8,128)(2,1)}, bf16[512,768]{1,0:T(8,128)(2,1)}, bf16[512,768]{1,0:T(8,128)(2,1)}, bf16[...) custom-call(s32[2]{0:T(128)} %pad_add_fusion.1.core_ref, ...), custom_call_target="tpu_custom_call" | custom-call | flops 14495514624 | bytes 7667712 | tf_op jit(solution)/shard_map/feed_forward/pallas_call | solution.py:138
  99.0 1.3 copy.95
  106.2 1.6 broadcast_add_fusion
  107.8 11.5 %project.1.q_ref.k_ref.v_ref.d_ref = bf16[12,8,64,256]{3,2,1,0:T(8,128)(2,1)} custom-call(s32[16]{0:T(128)} %copy-done.31, bf16[8,528,768]{2,1,0:T(8,128)(2,1)} %bitcast.112, bf16[8,528,768]{2,1,0:T(8,128)(2,1)} %bitcast.113, bf16[8,528,768]{2,1,0:T(8,128)(2,1)} %bitcast.114, bf16[8,528,768]{2,1,0:T(8,128)(2,1)} %bitcast.115, bf16[576,768]{1,0:T(8,128)(2,1)} %bitcast.100, ...), custom_call_target="tpu_custom_call" | custom-call | flops 12079595520 | bytes 12976128 | tf_op jit(solution)/shard_map/project/pallas_call | solution.py:198
  119.3 27.3 %attend.1 = (bf16[8,3,2,64,128]{4,3,2,1,0:T(8,128)(2,1)}, bf16[9,8,64,256]{3,2,1,0:T(8,128)(2,1)}) custom-call(s32[17]{0:T(128)} %pad_add_fusion.place_ref, bf16[12,8,64,256]{3,2,1,0:T(8,128)(2,1)} %project.1.q_ref.k_ref.v_ref.d_ref, bf16[12,8,64,256]{3,2,1,0:T(8,128)(2,1)} %project.1.q_ref.k_ref.v_ref.d_ref, ...), custom_call_target="tpu_custom_call" | custom-call | flops 32212254720 | bytes 6291456 | tf_op jit(solution)/shard_map/attend/pallas_call | solution.py:337
  150.9 1.9 fusion.22._
  152.8 4.9 %all-to-all-start.2 = ((bf16[4,3,2,64,128]{4,3,2,1,0:T(8,128)(2,1)}), bf16[4,3,2,64,128]{4,3,2,1,0:T(8,128)(2,1)S(1)}, u32[]{:S(2)}, u32[]{:S(2)}) async-start(bf16[4,3,2,64,128]{4,3,2,1,0:T(8,128)(2,1)} %fusion.22._), calls=%async_computation.2 | async-start | bytes 786432 | tf_op jit(solution)/shard_map/all_to_all | solution.py:530
  158.6 1.7 collective-permute-start.3
  160.4 1.5 collective-permute-start.4
  162.7 1.7 collective-permute-done.4
  164.3 2.4 collective-permute-done.5
  168.4 12.8 %back_to_weight.1 = (bf16[768,576]{1,0:T(8,128)(2,1)}, f32[192,768]{1,0:T(8,128)}, f32[576,1]{1,0:T(8,128)}, f32[1,768]{1,0:T(1,128)}, f32[1,768]{1,0:T(1,128)}) custom-call(s32[16]{0:T(128)} %copy-done.31, bf16[9,8,64,256]{3,2,1,0:T(8,128)(2,1)} %get-tuple-element.36.b_ref, bf16[576,768]{1,0:T(8,128)(2,1)} %bitcast.101, bf16[8,528,768]{2,1,0:T(8,128)(2,1)} %bitcast.116, ...), custom_call_target="tpu_custom_call" | custom-call | flops 9059696640 | bytes 12976128 | tf_op jit(solution)/shard_map/back_to_weight/pallas_call | solution.py:416
  189.8 1.4 fusion.4
  191.3 3.0 %collective-permute-done.9 = bf16[4,192,768]{2,1,0:T(8,128)(2,1)} collective-permute-done((bf16[4,192,768]{2,1,0:T(8,128)(2,1)S(1)}, bf16[4,192,768]{2,1,0:T(8,128)(2,1)}, u32[]{:S(2)}, u32[]{:S(2)}) %collective-permute-start.9) | collective-permute-done | bytes 1179680 | tf_op jit(solution)/shard_map/ppermute | solution.py:589
  194.3 2.6 fusion.5._.__
  196.9 9.2 %back_to_input.1 = bf16[16,128,768]{2,1,0:T(8,128)(2,1)} custom-call(s32[16]{0:T(128)} %copy-done.31, bf16[9,8,64,256]{3,2,1,0:T(8,128)(2,1)} %get-tuple-element.36.b_ref, bf16[576,768]{1,0:T(8,128)(2,1)} %bitcast.102, f32[1,768]{1,0:T(1,128)} %broadcast_in_dim_reshape_squeeze.4.gain_ref, bf16[4,192,768]{2,1,0:T(8,128)(2,1)} %fusion.5._.__, ...), custom_call_target="tpu_custom_call" | custom-call | flops 9059696640 | bytes 9437184 | tf_op jit(solution)/shard_map/back_to_input/pallas_call | solution.py:440
  208.4 2.6 collective-permute-start.12
  211.0 6.2 %place_ff.1 = (f32[192,3072]{1,0:T(8,128)}, f32[768,768]{1,0:T(8,128)}) custom-call(s32[1]{0:T(128)} %bitcast.8.at_ref, bf16[8,192,768]{2,1,0:T(8,128)(2,1)} %bitcast.94), custom_call_target="tpu_custom_call" | custom-call | tf_op jit(solution)/shard_map/place_ff/pallas_call | solution.py:469
  219.7 3.4 %collective-permute-done.11 = bf16[192,768]{1,0:T(8,128)(2,1)S(1)} collective-permute-done((bf16[192,768]{1,0:T(8,128)(2,1)S(1)}, bf16[192,768]{1,0:T(8,128)(2,1)S(1)}, u32[]{:S(2)}, u32[]{:S(2)}) %collective-permute-start.11) | collective-permute-done | bytes 294944 | tf_op jit(solution)/shard_map/ppermute | solution.py:544
  224.4 5.2 %all-to-all-start.3 = ((bf16[4,192,768]{2,1,0:T(8,128)(2,1)}), bf16[4,192,768]{2,1,0:T(8,128)(2,1)S(1)}, u32[]{:S(2)}, u32[]{:S(2)}) async-start(bf16[4,192,768]{2,1,0:T(8,128)(2,1)} %broadcast_in_dim.122), calls=%async_computation.5 | async-start | bytes 2359296 | tf_op jit(solution)/shard_map/all_to_all | solution.py:530
  229.8 1.5 collective-permute-start.6
  231.8 1.5 collective-permute-start.8
  233.3 36.6 %all-to-all-done.3.mine_ref = bf16[4,192,768]{2,1,0:T(8,128)(2,1)S(1)} async-done(((bf16[4,192,768]{2,1,0:T(8,128)(2,1)}), bf16[4,192,768]{2,1,0:T(8,128)(2,1)S(1)}, u32[]{:S(2)}, u32[]{:S(2)}) %all-to-all-start.3) | async-done | bytes 1179680 | tf_op jit(solution)/shard_map/all_to_all | solution.py:530
  272.6 2.3 add_add_fusion
  275.0 1.3 fusion.31
  276.3 3.4 %place_io.1 = (f32[192,2304]{1,0:T(8,128)}, f32[192,768]{1,0:T(8,128)}, f32[192,192]{1,0:T(8,128)}) custom-call(s32[1]{0:T(128)} %bitcast.1.core_ref, bf16[4,192,768]{2,1,0:T(8,128)(2,1)} %copy-done.3, bf16[4,192,768]{2,1,0:T(8,128)(2,1)} %collective-permute-done.13.other_ref), custom_call_target="tpu_custom_call" | custom-call | tf_op jit(solution)/shard_map/place_io/pallas_call | solution.py:512
  282.3 1.4 fusion.37
  (210 shorter events, 45.7 us)
Async XLA Ops:
  7.2 94.9 %all-gather.5.cloned.1.call-start = ((), (), s32[]{:S(2)}) async-start(), calls=%async_computation.8 | async-start | bytes 7299072 | tf_op jit(solution)/shard_map/all_gather | solution.py:595
  14.2 50.0 %all-to-all-start = ((bf16[4,624,768]{2,1,0:T(8,128)(2,1)}), bf16[4,624,768]{2,1,0:T(8,128)(2,1)}, u32[]{:S(2)}, u32[]{:S(2)}) async-start(bf16[4,624,768]{2,1,0:T(8,128)(2,1)} %pad_maximum_fusion), calls=%async_computation | async-start | bytes 7667712 | tf_op jit(solution)/shard_map/all_to_all | solution.py:530
  19.5 48.5 %copy-start.17 = (bf16[192,2304]{1,0:T(8,128)(2,1)S(1)}, bf16[192,2304]{1,0:T(8,128)(2,1)}, u32[]{:S(2)}) copy-start(bf16[192,2304]{1,0:T(8,128)(2,1)} %param.17) | copy-start | bytes 2654212
  67.9 6.8 %collective-permute-start = (bf16[4,96,768]{2,1,0:T(8,128)(2,1)S(1)}, bf16[4,96,768]{2,1,0:T(8,128)(2,1)}, u32[]{:S(2)}, u32[]{:S(2)}) collective-permute-start(bf16[4,96,768]{2,1,0:T(8,128)(2,1)S(1)} %slice.137), channel_id=1, source_target_pairs={{0,1},{1,0},{2,3},{3,2},{4,5},{5,4},{6,7},{7,6},{8,9},{9,8},{10,11... | collective-permute-start | bytes 1769480 | tf_op jit(solution)/shard_map/ppermute | solution.py:589
  70.9 22.6 %all-to-all-start.1 = ((bf16[4,208,768]{2,1,0:T(8,128)(2,1)}), bf16[4,208,768]{2,1,0:T(8,128)(2,1)S(1)}, u32[]{:S(2)}, u32[]{:S(2)}) async-start(bf16[4,208,768]{2,1,0:T(8,128)(2,1)} %broadcast_in_dim.111), calls=%async_computation.1 | async-start | bytes 2555904 | tf_op jit(solution)/shard_map/all_to_all | solution.py:530
  74.4 83.2 %reduce-scatter.3.cloned.1.call-start = ((), (), s32[]{:S(2)}) async-start(), calls=%async_computation.6 | async-start | bytes 2654208 | tf_op jit(solution)/shard_map/reduce_scatter | solution.py:640
  94.6 3.9 %collective-permute-start.1 = (bf16[4,192,768]{2,1,0:T(8,128)(2,1)}, bf16[4,192,768]{2,1,0:T(8,128)(2,1)S(1)}, u32[]{:S(2)}, u32[]{:S(2)}) collective-permute-start(bf16[4,192,768]{2,1,0:T(8,128)(2,1)} %slice_add_fusion), channel_id=1, source_target_pairs={{0,1},{1,0},{2,3},{3,2},{4,5},{5,4},{6,7},{7,6},{8,9},{9,8},{10,11... | collective-permute-start | bytes 3538952 | tf_op jit(solution)/shard_map/ppermute | solution.py:589
  100.3 5.9 %copy-start.9 = (bf16[8,192,768]{2,1,0:T(8,128)(2,1)S(1)}, bf16[8,192,768]{2,1,0:T(8,128)(2,1)}, u32[]{:S(2)}) copy-start(bf16[8,192,768]{2,1,0:T(8,128)(2,1)} %get-tuple-element.37) | copy-start | bytes 7077892
  119.3 28.6 %copy-start.5 = (bf16[1,256,768]{2,1,0:T(8,128)(2,1)S(1)}, bf16[1,256,768]{2,1,0:T(8,128)(2,1)}, u32[]{:S(2)}) copy-start(bf16[1,256,768]{2,1,0:T(8,128)(2,1)} %param.29) | copy-start | bytes 1179652
  119.3 28.8 %copy-start.23 = (f32[1,768]{1,0:T(1,128)S(1)}, f32[1,768]{1,0:T(1,128)}, u32[]{:S(2)}) copy-start(f32[1,768]{1,0:T(1,128)} %get-tuple-element.47) | copy-start | bytes 9220
  119.3 28.8 %copy-start.24 = (f32[1,768]{1,0:T(1,128)S(1)}, f32[1,768]{1,0:T(1,128)}, u32[]{:S(2)}) copy-start(f32[1,768]{1,0:T(1,128)} %get-tuple-element.48) | copy-start | bytes 9220
  119.3 29.0 %copy-start.22 = (f32[1,768]{1,0:T(1,128)S(1)}, f32[1,768]{1,0:T(1,128)}, u32[]{:S(2)}) copy-start(f32[1,768]{1,0:T(1,128)} %get-tuple-element.49) | copy-start | bytes 9220
  147.6 3.3 %collective-permute-start.2 = (bf16[4,3,2,64,128]{4,3,2,1,0:T(8,128)(2,1)S(1)}, bf16[4,3,2,64,128]{4,3,2,1,0:T(8,128)(2,1)S(1)}, u32[]{:S(2)}, u32[]{:S(2)}) collective-permute-start(bf16[4,3,2,64,128]{4,3,2,1,0:T(8,128)(2,1)S(1)} %dynamic-slice_bitcast_fusion.1), channel_id=1, source_target_pairs={{0,1},{1,0},{2,3},{3,2},{4,5},{5,4},{6,7},{7,6},{8,9},{9,8},{10,11... | collective-permute-start | bytes 1179656 | tf_op jit(solution)/shard_map/ppermute | solution.py:589
  152.8 31.0 %all-to-all-start.2 = ((bf16[4,3,2,64,128]{4,3,2,1,0:T(8,128)(2,1)}), bf16[4,3,2,64,128]{4,3,2,1,0:T(8,128)(2,1)S(1)}, u32[]{:S(2)}, u32[]{:S(2)}) async-start(bf16[4,3,2,64,128]{4,3,2,1,0:T(8,128)(2,1)} %fusion.22._), calls=%async_computation.2 | async-start | bytes 786432 | tf_op jit(solution)/shard_map/all_to_all | solution.py:530
  157.7 53.3 %all-gather.7.cloned.1.call-start = ((), (), s32[]{:S(2)}) async-start(), calls=%async_computation.9 | async-start | bytes 2654208 | tf_op jit(solution)/shard_map/all_gather | solution.py:681
  158.6 4.0 %collective-permute-start.3 = (bf16[24,768]{1,0:T(8,128)(2,1)S(1)}, bf16[24,768]{1,0:T(8,128)(2,1)S(1)}, u32[]{:S(2)}, u32[]{:S(2)}) collective-permute-start(bf16[24,768]{1,0:T(8,128)(2,1)S(1)} %get-tuple-element.71), channel_id=1, source_target_pairs={{0,8},{8,0},{16,24},{24,16},{1,9},{9,1},{17,25},{25,17},{2,10},{10... | collective-permute-start | bytes 110600 | tf_op jit(solution)/shard_map/ppermute | solution.py:544
  160.4 4.0 %collective-permute-start.4 = (bf16[24,768]{1,0:T(8,128)(2,1)S(1)}, bf16[24,768]{1,0:T(8,128)(2,1)S(1)}, u32[]{:S(2)}, u32[]{:S(2)}) collective-permute-start(bf16[24,768]{1,0:T(8,128)(2,1)S(1)} %get-tuple-element.70), channel_id=1, source_target_pairs={{0,16},{8,24},{16,0},{24,8},{1,17},{9,25},{17,1},{25,9},{2,18},{10... | collective-permute-start | bytes 110600 | tf_op jit(solution)/shard_map/ppermute | solution.py:544
  161.9 4.9 %collective-permute-start.5 = (bf16[24,768]{1,0:T(8,128)(2,1)S(1)}, bf16[24,768]{1,0:T(8,128)(2,1)S(1)}, u32[]{:S(2)}, u32[]{:S(2)}) collective-permute-start(bf16[24,768]{1,0:T(8,128)(2,1)S(1)} %get-tuple-element.69), channel_id=1, source_target_pairs={{0,24},{8,16},{16,8},{24,0},{1,25},{9,17},{17,9},{25,1},{2,26},{10... | collective-permute-start | bytes 110600 | tf_op jit(solution)/shard_map/ppermute | solution.py:544
  168.4 113.9 %reduce-scatter.5.cloned.1.call-start = ((), (), s32[]{:S(2)}) async-start(), calls=%async_computation.7 | async-start | bytes 3538944 | tf_op jit(solution)/shard_map/reduce_scatter | solution.py:722
  181.2 7.9 %copy-start.15 = (f32[192,768]{1,0:T(8,128)S(1)}, f32[192,768]{1,0:T(8,128)}, u32[]{:S(2)}) copy-start(f32[192,768]{1,0:T(8,128)} %get-tuple-element.43) | copy-start | bytes 1769476
  191.2 3.0 %collective-permute-start.9 = (bf16[4,192,768]{2,1,0:T(8,128)(2,1)S(1)}, bf16[4,192,768]{2,1,0:T(8,128)(2,1)}, u32[]{:S(2)}, u32[]{:S(2)}) collective-permute-start(bf16[4,192,768]{2,1,0:T(8,128)(2,1)S(1)} %dynamic-slice_bitcast_fusion), channel_id=1, source_target_pairs={{0,1},{1,0},{2,3},{3,2},{4,5},{5,4},{6,7},{7,6},{8,9},{9,8},{10,11... | collective-permute-start | bytes 3538952 | tf_op jit(solution)/shard_map/ppermute | solution.py:589
  207.4 12.3 %collective-permute-start.10 = (bf16[192,768]{1,0:T(8,128)(2,1)S(1)}, bf16[192,768]{1,0:T(8,128)(2,1)S(1)}, u32[]{:S(2)}, u32[]{:S(2)}) collective-permute-start(bf16[192,768]{1,0:T(8,128)(2,1)S(1)} %get-tuple-element.64), channel_id=1, source_target_pairs={{0,8},{8,0},{16,24},{24,16},{1,9},{9,1},{17,25},{25,17},{2,10},{10... | collective-permute-start | bytes 884744 | tf_op jit(solution)/shard_map/ppermute | solution.py:544
  208.0 15.1 %collective-permute-start.11 = (bf16[192,768]{1,0:T(8,128)(2,1)S(1)}, bf16[192,768]{1,0:T(8,128)(2,1)S(1)}, u32[]{:S(2)}, u32[]{:S(2)}) collective-permute-start(bf16[192,768]{1,0:T(8,128)(2,1)S(1)} %get-tuple-element.66), channel_id=1, source_target_pairs={{0,16},{8,24},{16,0},{24,8},{1,17},{9,25},{17,1},{25,9},{2,18},{10... | collective-permute-start | bytes 884744 | tf_op jit(solution)/shard_map/ppermute | solution.py:544
  208.4 14.8 %collective-permute-start.12 = (bf16[192,768]{1,0:T(8,128)(2,1)S(1)}, bf16[192,768]{1,0:T(8,128)(2,1)S(1)}, u32[]{:S(2)}, u32[]{:S(2)}) collective-permute-start(bf16[192,768]{1,0:T(8,128)(2,1)S(1)} %get-tuple-element.65), channel_id=1, source_target_pairs={{0,24},{8,16},{16,8},{24,0},{1,25},{9,17},{17,9},{25,1},{2,26},{10... | collective-permute-start | bytes 884744 | tf_op jit(solution)/shard_map/ppermute | solution.py:544
  223.3 6.3 %copy-start.2 = (bf16[1,256,768]{2,1,0:T(8,128)(2,1)S(1)}, bf16[1,256,768]{2,1,0:T(8,128)(2,1)}, u32[]{:S(2)}) copy-start(bf16[1,256,768]{2,1,0:T(8,128)(2,1)} %param.15) | copy-start | bytes 1179652
  224.4 46.6 %copy-start.8 = (bf16[4,3,2,64,128]{4,3,2,1,0:T(8,128)(2,1)S(1)}, bf16[4,3,2,64,128]{4,3,2,1,0:T(8,128)(2,1)}, u32[]{:S(2)}) copy-start(bf16[4,3,2,64,128]{4,3,2,1,0:T(8,128)(2,1)} %copy-done.7) | copy-start | bytes 1179652
  224.4 45.5 %all-to-all-start.3 = ((bf16[4,192,768]{2,1,0:T(8,128)(2,1)}), bf16[4,192,768]{2,1,0:T(8,128)(2,1)S(1)}, u32[]{:S(2)}, u32[]{:S(2)}) async-start(bf16[4,192,768]{2,1,0:T(8,128)(2,1)} %broadcast_in_dim.122), calls=%async_computation.5 | async-start | bytes 2359296 | tf_op jit(solution)/shard_map/all_to_all | solution.py:530
  229.8 41.7 %collective-permute-start.6 = (bf16[512,768]{1,0:T(8,128)(2,1)}, bf16[512,768]{1,0:T(8,128)(2,1)S(1)}, u32[]{:S(2)}, u32[]{:S(2)}) collective-permute-start(bf16[512,768]{1,0:T(8,128)(2,1)} %get-tuple-element.39), channel_id=1, source_target_pairs={{0,8},{8,0},{16,24},{24,16},{1,9},{9,1},{17,25},{25,17},{2,10},{10... | collective-permute-start | bytes 2359304 | tf_op jit(solution)/shard_map/ppermute | solution.py:544
  231.3 40.2 %collective-permute-start.7 = (bf16[512,768]{1,0:T(8,128)(2,1)}, bf16[512,768]{1,0:T(8,128)(2,1)S(1)}, u32[]{:S(2)}, u32[]{:S(2)}) collective-permute-start(bf16[512,768]{1,0:T(8,128)(2,1)} %get-tuple-element.40), channel_id=1, source_target_pairs={{0,16},{8,24},{16,0},{24,8},{1,17},{9,25},{17,1},{25,9},{2,18},{10... | collective-permute-start | bytes 2359304 | tf_op jit(solution)/shard_map/ppermute | solution.py:544
  231.8 39.6 %collective-permute-start.8 = (bf16[512,768]{1,0:T(8,128)(2,1)}, bf16[512,768]{1,0:T(8,128)(2,1)}, u32[]{:S(2)}, u32[]{:S(2)}) collective-permute-start(bf16[512,768]{1,0:T(8,128)(2,1)} %get-tuple-element.41), channel_id=1, source_target_pairs={{0,24},{8,16},{16,8},{24,0},{1,25},{9,17},{17,9},{25,1},{2,26},{10... | collective-permute-start | bytes 2359304 | tf_op jit(solution)/shard_map/ppermute | solution.py:544
  269.9 6.4 %collective-permute-start.13 = (bf16[4,192,768]{2,1,0:T(8,128)(2,1)S(1)}, bf16[4,192,768]{2,1,0:T(8,128)(2,1)}, u32[]{:S(2)}, u32[]{:S(2)}) collective-permute-start(bf16[4,192,768]{2,1,0:T(8,128)(2,1)S(1)} %all-to-all-done.3.mine_ref), channel_id=1, source_target_pairs={{0,1},{1,0},{2,3},{3,2},{4,5},{5,4},{6,7},{7,6},{8,9},{9,8},{10,11... | collective-permute-start | bytes 3538952 | tf_op jit(solution)/shard_map/ppermute | solution.py:589
  276.3 7.5 %copy-start.6 = (bf16[1,256,768]{2,1,0:T(8,128)(2,1)S(1)}, bf16[1,256,768]{2,1,0:T(8,128)(2,1)}, u32[]{:S(2)}) copy-start(bf16[1,256,768]{2,1,0:T(8,128)(2,1)} %param.29) | copy-start | bytes 1179652
  (22 other events, 68.8 us)
Sparse Core Ops, SparseCore 0:
  11.7 69.0 all-gather.4
  107.9 37.4 reduce-scatter.2
  168.5 31.1 all-gather.6
  206.2 50.6 reduce-scatter.4

commit v4 on v3

--- a/solution.py
+++ b/solution.py
@@ -69,6 +69,8 @@
         dgain_ref[...] = jnp.zeros_like(dgain_ref)
         dshift_ref[...] = jnp.zeros_like(dshift_ref)
 
+    grad = g_ref[0]
+    back_active = mm(grad, down_ref[...], (1, 1))
     xhat, _ = normalize(x_ref[0].astype(F32))
     second = (xhat * gain_ref[...] + shift_ref[...]).astype(BF)
     up = mm(second, up_ref[...], (1, 0)) + upb_ref[...]
@@ -77,9 +79,7 @@
     slope = phi + up * jnp.exp(-0.5 * up * up) * (1.0 / math.sqrt(2.0 * math.pi))
     tokens = x_ref.shape[1]
     part = mm(active, down_ref[...], (1, 0)).astype(BF)
-    grad = g_ref[0]
-    back_up = mm(grad, down_ref[...], (1, 1)) * slope
-    low_up = back_up.astype(BF)
+    low_up = (back_active * slope).astype(BF)
     dbias_ref[...] += jnp.sum(low_up.astype(F32), 0, keepdims=True)
     acc_up[...] += mm(second, low_up, (0, 0))
     acc_down[...] += mm(active, grad, (0, 0))
@@ -161,6 +161,7 @@
 
 def qkv_kernel(order_ref, xa_ref, xb_ref, ga_ref, gb_ref, w_ref, wo_ref, bias_ref, gain_ref, shift_ref, cos_ref,
                sin_ref, out_ref):
+    back = mm(wo_ref[...], jnp.concatenate([ga_ref[0], gb_ref[0]], 0), (1, 1)).astype(BF)
     values = jnp.concatenate([xa_ref[0], xb_ref[0]], 0).astype(F32)
     xhat, _ = normalize(values)
     first = (xhat * gain_ref[...] + shift_ref[...]).astype(BF)
@@ -175,7 +176,6 @@
         if i < heads:
             part = part * jnp.asarray(1.0 / math.sqrt(HEAD), BF)
         out_ref[i, 0] = part
-    back = mm(wo_ref[...], jnp.concatenate([ga_ref[0], gb_ref[0]], 0), (1, 1)).astype(BF)
     for i in range(heads):
         out_ref[3 * heads + i, 0] = back[i * HEAD:(i + 1) * HEAD]
 
@@ -223,7 +223,8 @@
     @pl.when((turn_at == 0) & (step == 0))
     def _():
         mix_ref[...] = jnp.zeros_like(mix_ref)
-        back_ref[...] = jnp.zeros_like(back_ref)
+        queries_end = back_ref.shape[0] // 3
+        back_ref[:queries_end] = jnp.zeros((queries_end,) + back_ref.shape[1:], BF)
 
     @pl.when(step == 0)
     def _():
@@ -375,12 +376,12 @@
         dout_ref[...] = jnp.zeros_like(dout_ref)
         dbias_ref[...] = jnp.zeros_like(dbias_ref)
 
+    rows, cols = b_ref.shape[0] * HEAD, ma_ref.shape[1] * HEAD
+    mixed = jnp.concatenate([r[0, :, 0].reshape(cols, RUN) for r in (ma_ref, mb_ref)], 1)
+    dout_ref[...] += mm(mixed, jnp.concatenate([ga_ref[0], gb_ref[0]], 0), (1, 0))
     xhat, _ = normalize(jnp.concatenate([xa_ref[0], xb_ref[0]], 0).astype(F32))
-    rows, cols = b_ref.shape[0] * HEAD, ma_ref.shape[1] * HEAD
     back = b_ref[...].reshape(rows, TILE)
     acc[...] += mm(back, xhat.astype(BF), (1, 0))
-    mixed = jnp.concatenate([r[0, :, 0].reshape(cols, RUN) for r in (ma_ref, mb_ref)], 1)
-    dout_ref[...] += mm(mixed, jnp.concatenate([ga_ref[0], gb_ref[0]], 0), (1, 0))
     dbias_ref[...] += jnp.sum(back.astype(F32), 1, keepdims=True)
 
     @pl.when(step == pl.num_programs(0) - 1)
@@ -639,8 +640,8 @@
     def reduce_owners(pieces):
         return lax.psum_scatter(pieces, "ctx", scatter_dimension=0, tiled=False)
 
-    def gather_owners(value):
-        mine = to_all(value, "ctx", parity, owners // 2)
+    def gather_owners(value, earlier):
+        mine = to_all(value, "ctx", parity, owners // 2) + after(jnp.int32(0), earlier).astype(BF)
         return mine, swap(mine)
 
     cut = shards * small_step
@@ -723,7 +724,7 @@
     pieces = total(by_distance(pieces, shard)).astype(BF)
     pieces = pieces + after(jnp.int32(0), down_weight_gradient).astype(BF)
     in_weight_gradient, out_weight_gradient, line_sum = place_io(
-        core, *gather_owners(pieces), cols)
+        core, *gather_owners(pieces, output), cols)
     line_sum = line_sum.reshape(2, half, -1)[:, :line_rows].reshape(-1)
     totals, at = [], 0
     for size in line_sizes:

time: 294 us -> 297 us (1.010)
  other arithmetic: 24.2 us -> 29.2 us
    all_to_all x4, waiting for transfers between devices: 79.8 us -> 43.2 us  [spread_out(): return lax.all_to_all(pieces, axis, 0, 0, axis_index_groups=groups)]
    ppermute x9, waiting for transfers between devices: 7.96 us -> 40.5 us  [at_distance(): lax.ppermute(pieces[k], 'fsdp', [(i, i ^ k) for i in range(count)])]
    unnamed x71 -> x67, local copies, waits for them, and re-layouts: 6.82 us -> 5.61 us
    slice x7 -> x8, local copies, waits for them, and re-layouts: 7.8 us -> 8.28 us  [after(): first = value[(0,) * value.ndim]]
  transfers between devices with their start and end apart: 22 -> 22, of which waited for: 7 -> 9; matrix products, arithmetic and copies ran while one was open for 15% -> 16% of each run, Pallas kernels for 30% -> 29%
where the time goes in v4:
time: 297 us; the launch traced here: 295 us
  waiting for transfers between devices  88.7 us (30%)
  Pallas kernels  85.8 us (29%)
  local copies, waits for them, and re-layouts  35.1 us (12%)
  starting transfers between devices  30.6 us (10%)
  other arithmetic  29.2 us (10%)
  between operations  25 us (8%)
    all_to_all x4, waiting for transfers between devices, spread_out(): return lax.all_to_all(pieces, axis, 0, 0, axis_index_groups=groups)  43.2 us
    ppermute x9, waiting for transfers between devices, at_distance(): lax.ppermute(pieces[k], 'fsdp', [(i, i ^ k) for i in range(count)])  40.5 us
    pallas_call x1, Pallas kernels, attend(): pl.pallas_call(functools.partial(attention_kernel, share, fused, held), g...  27.2 us
    all_to_all x4, starting transfers between devices, spread_out(): return lax.all_to_all(pieces, axis, 0, 0, axis_index_groups=groups)  18.8 us
    pallas_call x1, Pallas kernels, feed_forward(): pl.pallas_call(functools.partial(ff_kernel, bool(owners)), grid_spec=pltp...  15.6 us
    pallas_call x1, Pallas kernels, back_to_weight(): pl.pallas_call(back_weight_kernel, grid_spec=pltpu.PrefetchScalarGridSpec...  12.8 us
    pallas_call x1, Pallas kernels, project(): pl.pallas_call(qkv_kernel, grid_spec=pltpu.PrefetchScalarGridSpec(num_sca...  11.5 us
    ppermute x9, starting transfers between devices, at_distance(): lax.ppermute(pieces[k], 'fsdp', [(i, i ^ k) for i in range(count)])  10.5 us
  transfers between devices with their start and end apart: 22, of which 9 were waited for; matrix products, arithmetic and copies ran while one was open for 16% of the time, Pallas kernels for 29%

profile of v4, /device:TPU:0, one launch (start us, length us, event | category | flops | bytes accessed | tf_op | source)
XLA Modules:
  0.0 294.9 jit_solution(8563976934712295719)
XLA Ops:
  9.5 2.1 pad_maximum_fusion.2
  11.9 2.2 pad_maximum_fusion
  14.2 5.3 %all-to-all-start = ((bf16[4,624,768]{2,1,0:T(8,128)(2,1)}), bf16[4,624,768]{2,1,0:T(8,128)(2,1)}, u32[]{:S(2)}, u32[]{:S(2)}) async-start(bf16[4,624,768]{2,1,0:T(8,128)(2,1)} %pad_maximum_fusion), calls=%async_computation | async-start | bytes 7667712 | tf_op jit(solution)/shard_map/all_to_all | solution.py:531
  21.1 43.2 %all-to-all-done.x_ref.g_ref.small_ref.mine_ref.mine_end_ref = bf16[4,624,768]{2,1,0:T(8,128)(2,1)} async-done(((bf16[4,624,768]{2,1,0:T(8,128)(2,1)}), bf16[4,624,768]{2,1,0:T(8,128)(2,1)}, u32[]{:S(2)}, u32[]{:S(2)}) %all-to-all-start) | async-done | bytes 3833888 | tf_op jit(solution)/shard_map/all_to_all | solution.py:531
  70.8 3.5 %all-to-all-start.1 = ((bf16[4,208,768]{2,1,0:T(8,128)(2,1)}), bf16[4,208,768]{2,1,0:T(8,128)(2,1)S(1)}, u32[]{:S(2)}, u32[]{:S(2)}) async-start(bf16[4,208,768]{2,1,0:T(8,128)(2,1)} %broadcast_in_dim.111), calls=%async_computation.1 | async-start | bytes 2555904 | tf_op jit(solution)/shard_map/all_to_all | solution.py:531
  74.6 15.6 %feed_forward.1 = (bf16[512,768]{1,0:T(8,128)(2,1)}, bf16[512,768]{1,0:T(8,128)(2,1)}, bf16[512,768]{1,0:T(8,128)(2,1)}, bf16[512,768]{1,0:T(8,128)(2,1)}, bf16[...) custom-call(s32[2]{0:T(128)} %pad_add_fusion.1.core_ref, ...), custom_call_target="tpu_custom_call" | custom-call | flops 14495514624 | bytes 7667712 | tf_op jit(solution)/shard_map/feed_forward/pallas_call | solution.py:138
  96.8 1.4 broadcast_select_fusion
  104.8 3.2 %broadcast_add_fusion = bf16[8,192,768]{2,1,0:T(8,128)(2,1)} fusion(bf16[8,192,768]{2,1,0:T(8,128)(2,1)} %get-tuple-element.37, bf16[]{:T(256)} %bitcast.18), kind=kLoop, calls=%fused_computation.25 | loop fusion | flops 1179648 | bytes 4718594 | tf_op jit(solution)/shard_map/add | solution.py:649
  108.0 11.5 %project.1.q_ref.k_ref.v_ref.d_ref = bf16[12,8,64,256]{3,2,1,0:T(8,128)(2,1)} custom-call(s32[16]{0:T(128)} %copy-done.29, bf16[8,528,768]{2,1,0:T(8,128)(2,1)} %bitcast.113, bf16[8,528,768]{2,1,0:T(8,128)(2,1)} %bitcast.114, bf16[8,528,768]{2,1,0:T(8,128)(2,1)} %bitcast.115, bf16[8,528,768]{2,1,0:T(8,128)(2,1)} %bitcast.116, bf16[576,768]{1,0:T(8,128)(2,1)} %bitcast.102, ...), custom_call_target="tpu_custom_call" | custom-call | flops 12079595520 | bytes 12976128 | tf_op jit(solution)/shard_map/project/pallas_call | solution.py:198
  119.6 27.2 %attend.1 = (bf16[8,3,2,64,128]{4,3,2,1,0:T(8,128)(2,1)}, bf16[9,8,64,256]{3,2,1,0:T(8,128)(2,1)}) custom-call(s32[17]{0:T(128)} %pad_add_fusion.place_ref, bf16[12,8,64,256]{3,2,1,0:T(8,128)(2,1)} %project.1.q_ref.k_ref.v_ref.d_ref, bf16[12,8,64,256]{3,2,1,0:T(8,128)(2,1)} %project.1.q_ref.k_ref.v_ref.d_ref, ...), custom_call_target="tpu_custom_call" | custom-call | flops 32212254720 | bytes 6291456 | tf_op jit(solution)/shard_map/attend/pallas_call | solution.py:338
  151.1 1.9 fusion.21._
  152.9 4.9 %all-to-all-start.2 = ((bf16[4,3,2,64,128]{4,3,2,1,0:T(8,128)(2,1)}), bf16[4,3,2,64,128]{4,3,2,1,0:T(8,128)(2,1)S(1)}, u32[]{:S(2)}, u32[]{:S(2)}) async-start(bf16[4,3,2,64,128]{4,3,2,1,0:T(8,128)(2,1)} %fusion.21._), calls=%async_computation.2 | async-start | bytes 786432 | tf_op jit(solution)/shard_map/all_to_all | solution.py:531
  158.8 1.7 collective-permute-start.3
  160.5 1.5 collective-permute-start.4
  162.9 1.6 collective-permute-done.4
  164.5 2.4 collective-permute-done.5
  168.6 12.8 %back_to_weight.1 = (bf16[768,576]{1,0:T(8,128)(2,1)}, f32[192,768]{1,0:T(8,128)}, f32[576,1]{1,0:T(8,128)}, f32[1,768]{1,0:T(1,128)}, f32[1,768]{1,0:T(1,128)}) custom-call(s32[16]{0:T(128)} %copy-done.29, bf16[9,8,64,256]{3,2,1,0:T(8,128)(2,1)} %get-tuple-element.36.b_ref, bf16[576,768]{1,0:T(8,128)(2,1)} %bitcast.103, bf16[8,528,768]{2,1,0:T(8,128)(2,1)} %bitcast.117, ...), custom_call_target="tpu_custom_call" | custom-call | flops 9059696640 | bytes 12976128 | tf_op jit(solution)/shard_map/back_to_weight/pallas_call | solution.py:417
  192.5 3.2 %collective-permute-done.9 = bf16[4,192,768]{2,1,0:T(8,128)(2,1)} collective-permute-done((bf16[4,192,768]{2,1,0:T(8,128)(2,1)}, bf16[4,192,768]{2,1,0:T(8,128)(2,1)}, u32[]{:S(2)}, u32[]{:S(2)}) %collective-permute-start.9) | collective-permute-done | bytes 1179680 | tf_op jit(solution)/shard_map/ppermute | solution.py:590
  195.7 2.6 fusion.5._.__
  198.2 9.2 %back_to_input.1 = bf16[16,128,768]{2,1,0:T(8,128)(2,1)} custom-call(s32[16]{0:T(128)} %copy-done.29, bf16[9,8,64,256]{3,2,1,0:T(8,128)(2,1)} %get-tuple-element.36.b_ref, bf16[576,768]{1,0:T(8,128)(2,1)} %bitcast.104, f32[1,768]{1,0:T(1,128)} %broadcast_in_dim_reshape_squeeze.4.gain_ref, bf16[4,192,768]{2,1,0:T(8,128)(2,1)} %fusion.5._.__, ...), custom_call_target="tpu_custom_call" | custom-call | flops 9059696640 | bytes 9437184 | tf_op jit(solution)/shard_map/back_to_input/pallas_call | solution.py:441
  210.5 2.5 collective-permute-start.12
  213.0 6.1 %place_ff.1 = (f32[192,3072]{1,0:T(8,128)}, f32[768,768]{1,0:T(8,128)}) custom-call(s32[1]{0:T(128)} %bitcast.8.at_ref, bf16[8,192,768]{2,1,0:T(8,128)(2,1)} %bitcast.97), custom_call_target="tpu_custom_call" | custom-call | tf_op jit(solution)/shard_map/place_ff/pallas_call | solution.py:470
  221.6 3.7 %collective-permute-done.12 = bf16[192,768]{1,0:T(8,128)(2,1)} collective-permute-done((bf16[192,768]{1,0:T(8,128)(2,1)S(1)}, bf16[192,768]{1,0:T(8,128)(2,1)}, u32[]{:S(2)}, u32[]{:S(2)}) %collective-permute-start.12) | collective-permute-done | bytes 294944 | tf_op jit(solution)/shard_map/ppermute | solution.py:545
  227.6 5.1 %all-to-all-start.3 = ((bf16[4,192,768]{2,1,0:T(8,128)(2,1)}), bf16[4,192,768]{2,1,0:T(8,128)(2,1)}, u32[]{:S(2)}, u32[]{:S(2)}) async-start(bf16[4,192,768]{2,1,0:T(8,128)(2,1)} %broadcast_in_dim.122), calls=%async_computation.5 | async-start | bytes 2359296 | tf_op jit(solution)/shard_map/all_to_all | solution.py:531
  234.6 1.5 collective-permute-start.8
  236.7 16.6 %collective-permute-done.6 = bf16[512,768]{1,0:T(8,128)(2,1)S(1)} collective-permute-done((bf16[512,768]{1,0:T(8,128)(2,1)}, bf16[512,768]{1,0:T(8,128)(2,1)S(1)}, u32[]{:S(2)}, u32[]{:S(2)}) %collective-permute-start.6) | collective-permute-done | bytes 786464 | tf_op jit(solution)/shard_map/ppermute | solution.py:545
  253.3 15.7 %collective-permute-done.8 = bf16[512,768]{1,0:T(8,128)(2,1)} collective-permute-done((bf16[512,768]{1,0:T(8,128)(2,1)}, bf16[512,768]{1,0:T(8,128)(2,1)}, u32[]{:S(2)}, u32[]{:S(2)}) %collective-permute-start.8) | collective-permute-done | bytes 786464 | tf_op jit(solution)/shard_map/ppermute | solution.py:545
  269.0 2.3 add_add_fusion
  274.6 1.4 broadcast_add_fusion.1.mine_ref
  277.4 1.8 collective-permute-done.13.other_ref
  279.1 3.3 %place_io.1 = (f32[192,2304]{1,0:T(8,128)}, f32[192,768]{1,0:T(8,128)}, f32[192,192]{1,0:T(8,128)}) custom-call(s32[1]{0:T(128)} %bitcast.1.core_ref, bf16[4,192,768]{2,1,0:T(8,128)(2,1)} %copy-done.3, bf16[4,192,768]{2,1,0:T(8,128)(2,1)} %collective-permute-done.13.other_ref), custom_call_target="tpu_custom_call" | custom-call | tf_op jit(solution)/shard_map/place_io/pallas_call | solution.py:513
  285.1 1.4 fusion.35
  (209 shorter events, 51.4 us)
Async XLA Ops:
  7.2 93.5 %all-gather.5.cloned.1.call-start = ((), (), s32[]{:S(2)}) async-start(), calls=%async_computation.8 | async-start | bytes 7299072 | tf_op jit(solution)/shard_map/all_gather | solution.py:596
  14.2 50.1 %all-to-all-start = ((bf16[4,624,768]{2,1,0:T(8,128)(2,1)}), bf16[4,624,768]{2,1,0:T(8,128)(2,1)}, u32[]{:S(2)}, u32[]{:S(2)}) async-start(bf16[4,624,768]{2,1,0:T(8,128)(2,1)} %pad_maximum_fusion), calls=%async_computation | async-start | bytes 7667712 | tf_op jit(solution)/shard_map/all_to_all | solution.py:531
  19.5 48.5 %copy-start.16 = (bf16[192,2304]{1,0:T(8,128)(2,1)S(1)}, bf16[192,2304]{1,0:T(8,128)(2,1)}, u32[]{:S(2)}) copy-start(bf16[192,2304]{1,0:T(8,128)(2,1)} %param.17) | copy-start | bytes 2654212
  67.9 6.8 %collective-permute-start = (bf16[4,96,768]{2,1,0:T(8,128)(2,1)S(1)}, bf16[4,96,768]{2,1,0:T(8,128)(2,1)}, u32[]{:S(2)}, u32[]{:S(2)}) collective-permute-start(bf16[4,96,768]{2,1,0:T(8,128)(2,1)S(1)} %slice.141), channel_id=1, source_target_pairs={{0,1},{1,0},{2,3},{3,2},{4,5},{5,4},{6,7},{7,6},{8,9},{9,8},{10,11... | collective-permute-start | bytes 1769480 | tf_op jit(solution)/shard_map/ppermute | solution.py:590
  70.8 21.9 %all-to-all-start.1 = ((bf16[4,208,768]{2,1,0:T(8,128)(2,1)}), bf16[4,208,768]{2,1,0:T(8,128)(2,1)S(1)}, u32[]{:S(2)}, u32[]{:S(2)}) async-start(bf16[4,208,768]{2,1,0:T(8,128)(2,1)} %broadcast_in_dim.111), calls=%async_computation.1 | async-start | bytes 2555904 | tf_op jit(solution)/shard_map/all_to_all | solution.py:531
  74.4 83.5 %reduce-scatter.3.cloned.1.call-start = ((), (), s32[]{:S(2)}) async-start(), calls=%async_computation.6 | async-start | bytes 2654208 | tf_op jit(solution)/shard_map/reduce_scatter | solution.py:641
  92.8 4.0 %collective-permute-start.1 = (bf16[4,192,768]{2,1,0:T(8,128)(2,1)S(1)}, bf16[4,192,768]{2,1,0:T(8,128)(2,1)}, u32[]{:S(2)}, u32[]{:S(2)}) collective-permute-start(bf16[4,192,768]{2,1,0:T(8,128)(2,1)S(1)} %slice_add_fusion), channel_id=1, source_target_pairs={{0,1},{1,0},{2,3},{3,2},{4,5},{5,4},{6,7},{7,6},{8,9},{9,8},{10,11... | collective-permute-start | bytes 3538952 | tf_op jit(solution)/shard_map/ppermute | solution.py:590
  119.5 28.5 %copy-start.5 = (bf16[1,256,768]{2,1,0:T(8,128)(2,1)S(1)}, bf16[1,256,768]{2,1,0:T(8,128)(2,1)}, u32[]{:S(2)}) copy-start(bf16[1,256,768]{2,1,0:T(8,128)(2,1)} %param.29) | copy-start | bytes 1179652
  119.5 28.7 %copy-start.21 = (f32[1,768]{1,0:T(1,128)S(1)}, f32[1,768]{1,0:T(1,128)}, u32[]{:S(2)}) copy-start(f32[1,768]{1,0:T(1,128)} %get-tuple-element.47) | copy-start | bytes 9220
  119.6 28.7 %copy-start.22 = (f32[1,768]{1,0:T(1,128)S(1)}, f32[1,768]{1,0:T(1,128)}, u32[]{:S(2)}) copy-start(f32[1,768]{1,0:T(1,128)} %get-tuple-element.48) | copy-start | bytes 9220
  119.6 28.9 %copy-start.20 = (f32[1,768]{1,0:T(1,128)S(1)}, f32[1,768]{1,0:T(1,128)}, u32[]{:S(2)}) copy-start(f32[1,768]{1,0:T(1,128)} %get-tuple-element.49) | copy-start | bytes 9220
  147.8 3.3 %collective-permute-start.2 = (bf16[4,3,2,64,128]{4,3,2,1,0:T(8,128)(2,1)S(1)}, bf16[4,3,2,64,128]{4,3,2,1,0:T(8,128)(2,1)S(1)}, u32[]{:S(2)}, u32[]{:S(2)}) collective-permute-start(bf16[4,3,2,64,128]{4,3,2,1,0:T(8,128)(2,1)S(1)} %dynamic-slice_bitcast_fusion.1), channel_id=1, source_target_pairs={{0,1},{1,0},{2,3},{3,2},{4,5},{5,4},{6,7},{7,6},{8,9},{9,8},{10,11... | collective-permute-start | bytes 1179656 | tf_op jit(solution)/shard_map/ppermute | solution.py:590
  152.9 31.1 %all-to-all-start.2 = ((bf16[4,3,2,64,128]{4,3,2,1,0:T(8,128)(2,1)}), bf16[4,3,2,64,128]{4,3,2,1,0:T(8,128)(2,1)S(1)}, u32[]{:S(2)}, u32[]{:S(2)}) async-start(bf16[4,3,2,64,128]{4,3,2,1,0:T(8,128)(2,1)} %fusion.21._), calls=%async_computation.2 | async-start | bytes 786432 | tf_op jit(solution)/shard_map/all_to_all | solution.py:531
  157.9 55.1 %all-gather.7.cloned.1.call-start = ((), (), s32[]{:S(2)}) async-start(), calls=%async_computation.9 | async-start | bytes 2654208 | tf_op jit(solution)/shard_map/all_gather | solution.py:682
  158.8 4.0 %collective-permute-start.3 = (bf16[24,768]{1,0:T(8,128)(2,1)S(1)}, bf16[24,768]{1,0:T(8,128)(2,1)S(1)}, u32[]{:S(2)}, u32[]{:S(2)}) collective-permute-start(bf16[24,768]{1,0:T(8,128)(2,1)S(1)} %get-tuple-element.71), channel_id=1, source_target_pairs={{0,8},{8,0},{16,24},{24,16},{1,9},{9,1},{17,25},{25,17},{2,10},{10... | collective-permute-start | bytes 110600 | tf_op jit(solution)/shard_map/ppermute | solution.py:545
  160.5 4.0 %collective-permute-start.4 = (bf16[24,768]{1,0:T(8,128)(2,1)S(1)}, bf16[24,768]{1,0:T(8,128)(2,1)S(1)}, u32[]{:S(2)}, u32[]{:S(2)}) collective-permute-start(bf16[24,768]{1,0:T(8,128)(2,1)S(1)} %get-tuple-element.70), channel_id=1, source_target_pairs={{0,16},{8,24},{16,0},{24,8},{1,17},{9,25},{17,1},{25,9},{2,18},{10... | collective-permute-start | bytes 110600 | tf_op jit(solution)/shard_map/ppermute | solution.py:545
  162.0 4.9 %collective-permute-start.5 = (bf16[24,768]{1,0:T(8,128)(2,1)S(1)}, bf16[24,768]{1,0:T(8,128)(2,1)S(1)}, u32[]{:S(2)}, u32[]{:S(2)}) collective-permute-start(bf16[24,768]{1,0:T(8,128)(2,1)S(1)} %get-tuple-element.69), channel_id=1, source_target_pairs={{0,24},{8,16},{16,8},{24,0},{1,25},{9,17},{17,9},{25,1},{2,26},{10... | collective-permute-start | bytes 110600 | tf_op jit(solution)/shard_map/ppermute | solution.py:545
  168.5 116.5 %reduce-scatter.5.cloned.1.call-start = ((), (), s32[]{:S(2)}) async-start(), calls=%async_computation.7 | async-start | bytes 3538944 | tf_op jit(solution)/shard_map/reduce_scatter | solution.py:723
  181.4 7.9 %copy-start.14 = (f32[192,768]{1,0:T(8,128)S(1)}, f32[192,768]{1,0:T(8,128)}, u32[]{:S(2)}) copy-start(f32[192,768]{1,0:T(8,128)} %get-tuple-element.43) | copy-start | bytes 1769476
  192.5 3.2 %collective-permute-start.9 = (bf16[4,192,768]{2,1,0:T(8,128)(2,1)}, bf16[4,192,768]{2,1,0:T(8,128)(2,1)}, u32[]{:S(2)}, u32[]{:S(2)}) collective-permute-start(bf16[4,192,768]{2,1,0:T(8,128)(2,1)} %dynamic-slice_bitcast_fusion), channel_id=1, source_target_pairs={{0,1},{1,0},{2,3},{3,2},{4,5},{5,4},{6,7},{7,6},{8,9},{9,8},{10,11... | collective-permute-start | bytes 3538952 | tf_op jit(solution)/shard_map/ppermute | solution.py:590
  209.5 12.1 %collective-permute-start.10 = (bf16[192,768]{1,0:T(8,128)(2,1)}, bf16[192,768]{1,0:T(8,128)(2,1)S(1)}, u32[]{:S(2)}, u32[]{:S(2)}) collective-permute-start(bf16[192,768]{1,0:T(8,128)(2,1)} %get-tuple-element.64), channel_id=1, source_target_pairs={{0,8},{8,0},{16,24},{24,16},{1,9},{9,1},{17,25},{25,17},{2,10},{10... | collective-permute-start | bytes 884744 | tf_op jit(solution)/shard_map/ppermute | solution.py:545
  210.1 11.5 %collective-permute-start.11 = (bf16[192,768]{1,0:T(8,128)(2,1)S(1)}, bf16[192,768]{1,0:T(8,128)(2,1)S(1)}, u32[]{:S(2)}, u32[]{:S(2)}) collective-permute-start(bf16[192,768]{1,0:T(8,128)(2,1)S(1)} %get-tuple-element.66), channel_id=1, source_target_pairs={{0,16},{8,24},{16,0},{24,8},{1,17},{9,25},{17,1},{25,9},{2,18},{10... | collective-permute-start | bytes 884744 | tf_op jit(solution)/shard_map/ppermute | solution.py:545
  210.5 14.9 %collective-permute-start.12 = (bf16[192,768]{1,0:T(8,128)(2,1)S(1)}, bf16[192,768]{1,0:T(8,128)(2,1)}, u32[]{:S(2)}, u32[]{:S(2)}) collective-permute-start(bf16[192,768]{1,0:T(8,128)(2,1)S(1)} %get-tuple-element.65), channel_id=1, source_target_pairs={{0,24},{8,16},{16,8},{24,0},{1,25},{9,17},{17,9},{25,1},{2,26},{10... | collective-permute-start | bytes 884744 | tf_op jit(solution)/shard_map/ppermute | solution.py:545
  226.5 9.8 %copy-start.8 = (bf16[4,3,2,64,128]{4,3,2,1,0:T(8,128)(2,1)S(1)}, bf16[4,3,2,64,128]{4,3,2,1,0:T(8,128)(2,1)}, u32[]{:S(2)}) copy-start(bf16[4,3,2,64,128]{4,3,2,1,0:T(8,128)(2,1)} %copy-done.7) | copy-start | bytes 1179652
  227.6 47.1 %all-to-all-start.3 = ((bf16[4,192,768]{2,1,0:T(8,128)(2,1)}), bf16[4,192,768]{2,1,0:T(8,128)(2,1)}, u32[]{:S(2)}, u32[]{:S(2)}) async-start(bf16[4,192,768]{2,1,0:T(8,128)(2,1)} %broadcast_in_dim.122), calls=%async_computation.5 | async-start | bytes 2359296 | tf_op jit(solution)/shard_map/all_to_all | solution.py:531
  232.6 20.7 %collective-permute-start.6 = (bf16[512,768]{1,0:T(8,128)(2,1)}, bf16[512,768]{1,0:T(8,128)(2,1)S(1)}, u32[]{:S(2)}, u32[]{:S(2)}) collective-permute-start(bf16[512,768]{1,0:T(8,128)(2,1)} %get-tuple-element.39), channel_id=1, source_target_pairs={{0,8},{8,0},{16,24},{24,16},{1,9},{9,1},{17,25},{25,17},{2,10},{10... | collective-permute-start | bytes 2359304 | tf_op jit(solution)/shard_map/ppermute | solution.py:545
  233.9 19.4 %collective-permute-start.7 = (bf16[512,768]{1,0:T(8,128)(2,1)}, bf16[512,768]{1,0:T(8,128)(2,1)S(1)}, u32[]{:S(2)}, u32[]{:S(2)}) collective-permute-start(bf16[512,768]{1,0:T(8,128)(2,1)} %get-tuple-element.40), channel_id=1, source_target_pairs={{0,16},{8,24},{16,0},{24,8},{1,17},{9,25},{17,1},{25,9},{2,18},{10... | collective-permute-start | bytes 2359304 | tf_op jit(solution)/shard_map/ppermute | solution.py:545
  234.6 34.4 %collective-permute-start.8 = (bf16[512,768]{1,0:T(8,128)(2,1)}, bf16[512,768]{1,0:T(8,128)(2,1)}, u32[]{:S(2)}, u32[]{:S(2)}) collective-permute-start(bf16[512,768]{1,0:T(8,128)(2,1)} %get-tuple-element.41), channel_id=1, source_target_pairs={{0,24},{8,16},{16,8},{24,0},{1,25},{9,17},{17,9},{25,1},{2,26},{10... | collective-permute-start | bytes 2359304 | tf_op jit(solution)/shard_map/ppermute | solution.py:545
  253.3 15.7 %copy-start.12 = (bf16[512,768]{1,0:T(8,128)(2,1)}, bf16[512,768]{1,0:T(8,128)(2,1)S(1)}, u32[]{:S(2)}) copy-start(bf16[512,768]{1,0:T(8,128)(2,1)S(1)} %collective-permute-done.6) | copy-start | bytes 2359300
  253.3 15.7 %copy-start.13 = (bf16[512,768]{1,0:T(8,128)(2,1)}, bf16[512,768]{1,0:T(8,128)(2,1)S(1)}, u32[]{:S(2)}) copy-start(bf16[512,768]{1,0:T(8,128)(2,1)S(1)} %collective-permute-done.7) | copy-start | bytes 2359300
  276.1 3.0 %collective-permute-start.13 = (bf16[4,192,768]{2,1,0:T(8,128)(2,1)S(1)}, bf16[4,192,768]{2,1,0:T(8,128)(2,1)}, u32[]{:S(2)}, u32[]{:S(2)}) collective-permute-start(bf16[4,192,768]{2,1,0:T(8,128)(2,1)S(1)} %broadcast_add_fusion.1.mine_ref), channel_id=1, source_target_pairs={{0,1},{1,0},{2,3},{3,2},{4,5},{5,4},{6,7},{7,6},{8,9},{9,8},{10,11... | collective-permute-start | bytes 3538952 | tf_op jit(solution)/shard_map/ppermute | solution.py:590
  277.4 9.2 %copy-start.6 = (bf16[1,256,768]{2,1,0:T(8,128)(2,1)S(1)}, bf16[1,256,768]{2,1,0:T(8,128)(2,1)}, u32[]{:S(2)}) copy-start(bf16[1,256,768]{2,1,0:T(8,128)(2,1)} %param.29) | copy-start | bytes 1179652
  (20 other events, 67.4 us)
Sparse Core Ops, SparseCore 0:
  11.7 69.0 all-gather.4
  108.1 37.5 reduce-scatter.2
  168.7 31.2 all-gather.6
  207.6 49.6 reduce-scatter.4

commit v5 on v4

--- a/solution.py
+++ b/solution.py
@@ -640,8 +640,8 @@
     def reduce_owners(pieces):
         return lax.psum_scatter(pieces, "ctx", scatter_dimension=0, tiled=False)
 
-    def gather_owners(value, earlier):
-        mine = to_all(value, "ctx", parity, owners // 2) + after(jnp.int32(0), earlier).astype(BF)
+    def gather_owners(value):
+        mine = to_all(value, "ctx", parity, owners // 2)
         return mine, swap(mine)
 
     cut = shards * small_step
@@ -724,7 +724,7 @@
     pieces = total(by_distance(pieces, shard)).astype(BF)
     pieces = pieces + after(jnp.int32(0), down_weight_gradient).astype(BF)
     in_weight_gradient, out_weight_gradient, line_sum = place_io(
-        core, *gather_owners(pieces, output), cols)
+        core, *gather_owners(pieces), cols)
     line_sum = line_sum.reshape(2, half, -1)[:, :line_rows].reshape(-1)
     totals, at = [], 0
     for size in line_sizes:

time: 297 us -> 293 us (0.987)
  other arithmetic: 29.2 us -> 24.2 us
    all_to_all x4, waiting for transfers between devices: 43.2 us -> 79.8 us  [spread_out(): return lax.all_to_all(pieces, axis, 0, 0, axis_index_groups=groups)]
    ppermute x9, waiting for transfers between devices: 40.5 us -> 7.96 us  [at_distance(): lax.ppermute(pieces[k], 'fsdp', [(i, i ^ k) for i in range(count)])]
    unnamed x67 -> x71, local copies, waits for them, and re-layouts: 5.61 us -> 6.82 us
    slice x8 -> x7, local copies, waits for them, and re-layouts: 8.28 us -> 7.8 us  [after(): first = value[(0,) * value.ndim]]
  transfers between devices with their start and end apart: 22 -> 22, of which waited for: 9 -> 7; matrix products, arithmetic and copies ran while one was open for 16% -> 15% of each run, Pallas kernels for 29% -> 29%
where the time goes in v5:
time: 293 us; the launch traced here: 291 us
  waiting for transfers between devices  90.8 us (31%)
  Pallas kernels  85.9 us (29%)
  local copies, waits for them, and re-layouts  34.8 us (12%)
  starting transfers between devices  30.7 us (10%)
  other arithmetic  24.2 us (8%)
  between operations  23.7 us (8%)
    all_to_all x4, waiting for transfers between devices, spread_out(): return lax.all_to_all(pieces, axis, 0, 0, axis_index_groups=groups)  79.8 us
    pallas_call x1, Pallas kernels, attend(): pl.pallas_call(functools.partial(attention_kernel, share, fused, held), g...  27.2 us
    all_to_all x4, starting transfers between devices, spread_out(): return lax.all_to_all(pieces, axis, 0, 0, axis_index_groups=groups)  19 us
    pallas_call x1, Pallas kernels, feed_forward(): pl.pallas_call(functools.partial(ff_kernel, bool(owners)), grid_spec=pltp...  15.6 us
    pallas_call x1, Pallas kernels, back_to_weight(): pl.pallas_call(back_weight_kernel, grid_spec=pltpu.PrefetchScalarGridSpec...  12.8 us
    pallas_call x1, Pallas kernels, project(): pl.pallas_call(qkv_kernel, grid_spec=pltpu.PrefetchScalarGridSpec(num_sca...  11.5 us
    ppermute x9, starting transfers between devices, at_distance(): lax.ppermute(pieces[k], 'fsdp', [(i, i ^ k) for i in range(count)])  10.7 us
    pallas_call x1, Pallas kernels, back_to_input(): pl.pallas_call(back_input_kernel, grid_spec=pltpu.PrefetchScalarGridSpec(...  9.21 us
  transfers between devices with their start and end apart: 22, of which 7 were waited for; matrix products, arithmetic and copies ran while one was open for 15% of the time, Pallas kernels for 29%

profile of v5, /device:TPU:0, one launch (start us, length us, event | category | flops | bytes accessed | tf_op | source)
XLA Modules:
  0.0 291.4 jit_solution(17542723965374380026)
XLA Ops:
  9.5 2.1 pad_maximum_fusion.2
  11.9 2.2 pad_maximum_fusion
  14.2 5.3 %all-to-all-start = ((bf16[4,624,768]{2,1,0:T(8,128)(2,1)}), bf16[4,624,768]{2,1,0:T(8,128)(2,1)}, u32[]{:S(2)}, u32[]{:S(2)}) async-start(bf16[4,624,768]{2,1,0:T(8,128)(2,1)} %pad_maximum_fusion), calls=%async_computation | async-start | bytes 7667712 | tf_op jit(solution)/shard_map/all_to_all | solution.py:531
  21.1 43.2 %all-to-all-done.x_ref.g_ref.small_ref.mine_ref.mine_end_ref = bf16[4,624,768]{2,1,0:T(8,128)(2,1)} async-done(((bf16[4,624,768]{2,1,0:T(8,128)(2,1)}), bf16[4,624,768]{2,1,0:T(8,128)(2,1)}, u32[]{:S(2)}, u32[]{:S(2)}) %all-to-all-start) | async-done | bytes 3833888 | tf_op jit(solution)/shard_map/all_to_all | solution.py:531
  70.9 3.5 %all-to-all-start.1 = ((bf16[4,208,768]{2,1,0:T(8,128)(2,1)}), bf16[4,208,768]{2,1,0:T(8,128)(2,1)S(1)}, u32[]{:S(2)}, u32[]{:S(2)}) async-start(bf16[4,208,768]{2,1,0:T(8,128)(2,1)} %broadcast_in_dim.111), calls=%async_computation.1 | async-start | bytes 2555904 | tf_op jit(solution)/shard_map/all_to_all | solution.py:531
  74.7 15.6 %feed_forward.1 = (bf16[512,768]{1,0:T(8,128)(2,1)}, bf16[512,768]{1,0:T(8,128)(2,1)}, bf16[512,768]{1,0:T(8,128)(2,1)}, bf16[512,768]{1,0:T(8,128)(2,1)}, bf16[...) custom-call(s32[2]{0:T(128)} %pad_add_fusion.1.core_ref, ...), custom_call_target="tpu_custom_call" | custom-call | flops 14495514624 | bytes 7667712 | tf_op jit(solution)/shard_map/feed_forward/pallas_call | solution.py:138
  98.3 1.3 copy.95
  105.5 1.6 broadcast_add_fusion
  107.1 11.5 %project.1.q_ref.k_ref.v_ref.d_ref = bf16[12,8,64,256]{3,2,1,0:T(8,128)(2,1)} custom-call(s32[16]{0:T(128)} %copy-done.31, bf16[8,528,768]{2,1,0:T(8,128)(2,1)} %bitcast.112, bf16[8,528,768]{2,1,0:T(8,128)(2,1)} %bitcast.113, bf16[8,528,768]{2,1,0:T(8,128)(2,1)} %bitcast.114, bf16[8,528,768]{2,1,0:T(8,128)(2,1)} %bitcast.115, bf16[576,768]{1,0:T(8,128)(2,1)} %bitcast.100, ...), custom_call_target="tpu_custom_call" | custom-call | flops 12079595520 | bytes 12976128 | tf_op jit(solution)/shard_map/project/pallas_call | solution.py:198
  118.6 27.2 %attend.1 = (bf16[8,3,2,64,128]{4,3,2,1,0:T(8,128)(2,1)}, bf16[9,8,64,256]{3,2,1,0:T(8,128)(2,1)}) custom-call(s32[17]{0:T(128)} %pad_add_fusion.place_ref, bf16[12,8,64,256]{3,2,1,0:T(8,128)(2,1)} %project.1.q_ref.k_ref.v_ref.d_ref, bf16[12,8,64,256]{3,2,1,0:T(8,128)(2,1)} %project.1.q_ref.k_ref.v_ref.d_ref, ...), custom_call_target="tpu_custom_call" | custom-call | flops 32212254720 | bytes 6291456 | tf_op jit(solution)/shard_map/attend/pallas_call | solution.py:338
  150.1 1.9 fusion.22._
  152.0 4.9 %all-to-all-start.2 = ((bf16[4,3,2,64,128]{4,3,2,1,0:T(8,128)(2,1)}), bf16[4,3,2,64,128]{4,3,2,1,0:T(8,128)(2,1)S(1)}, u32[]{:S(2)}, u32[]{:S(2)}) async-start(bf16[4,3,2,64,128]{4,3,2,1,0:T(8,128)(2,1)} %fusion.22._), calls=%async_computation.2 | async-start | bytes 786432 | tf_op jit(solution)/shard_map/all_to_all | solution.py:531
  157.8 1.7 collective-permute-start.3
  159.6 1.5 collective-permute-start.4
  161.8 1.7 collective-permute-done.4
  163.5 2.4 collective-permute-done.5
  167.6 12.8 %back_to_weight.1 = (bf16[768,576]{1,0:T(8,128)(2,1)}, f32[192,768]{1,0:T(8,128)}, f32[576,1]{1,0:T(8,128)}, f32[1,768]{1,0:T(1,128)}, f32[1,768]{1,0:T(1,128)}) custom-call(s32[16]{0:T(128)} %copy-done.31, bf16[9,8,64,256]{3,2,1,0:T(8,128)(2,1)} %get-tuple-element.36.b_ref, bf16[576,768]{1,0:T(8,128)(2,1)} %bitcast.101, bf16[8,528,768]{2,1,0:T(8,128)(2,1)} %bitcast.116, ...), custom_call_target="tpu_custom_call" | custom-call | flops 9059696640 | bytes 12976128 | tf_op jit(solution)/shard_map/back_to_weight/pallas_call | solution.py:417
  189.0 1.4 fusion.4
  190.5 3.0 %collective-permute-done.9 = bf16[4,192,768]{2,1,0:T(8,128)(2,1)} collective-permute-done((bf16[4,192,768]{2,1,0:T(8,128)(2,1)S(1)}, bf16[4,192,768]{2,1,0:T(8,128)(2,1)}, u32[]{:S(2)}, u32[]{:S(2)}) %collective-permute-start.9) | collective-permute-done | bytes 1179680 | tf_op jit(solution)/shard_map/ppermute | solution.py:590
  193.5 2.6 fusion.5._.__
  196.1 9.2 %back_to_input.1 = bf16[16,128,768]{2,1,0:T(8,128)(2,1)} custom-call(s32[16]{0:T(128)} %copy-done.31, bf16[9,8,64,256]{3,2,1,0:T(8,128)(2,1)} %get-tuple-element.36.b_ref, bf16[576,768]{1,0:T(8,128)(2,1)} %bitcast.102, f32[1,768]{1,0:T(1,128)} %broadcast_in_dim_reshape_squeeze.4.gain_ref, bf16[4,192,768]{2,1,0:T(8,128)(2,1)} %fusion.5._.__, ...), custom_call_target="tpu_custom_call" | custom-call | flops 9059696640 | bytes 9437184 | tf_op jit(solution)/shard_map/back_to_input/pallas_call | solution.py:441
  207.7 2.4 collective-permute-start.12
  210.2 6.2 %place_ff.1 = (f32[192,3072]{1,0:T(8,128)}, f32[768,768]{1,0:T(8,128)}) custom-call(s32[1]{0:T(128)} %bitcast.8.at_ref, bf16[8,192,768]{2,1,0:T(8,128)(2,1)} %bitcast.94), custom_call_target="tpu_custom_call" | custom-call | tf_op jit(solution)/shard_map/place_ff/pallas_call | solution.py:470
  218.9 3.4 %collective-permute-done.11 = bf16[192,768]{1,0:T(8,128)(2,1)S(1)} collective-permute-done((bf16[192,768]{1,0:T(8,128)(2,1)S(1)}, bf16[192,768]{1,0:T(8,128)(2,1)S(1)}, u32[]{:S(2)}, u32[]{:S(2)}) %collective-permute-start.11) | collective-permute-done | bytes 294944 | tf_op jit(solution)/shard_map/ppermute | solution.py:545
  223.6 5.3 %all-to-all-start.3 = ((bf16[4,192,768]{2,1,0:T(8,128)(2,1)}), bf16[4,192,768]{2,1,0:T(8,128)(2,1)S(1)}, u32[]{:S(2)}, u32[]{:S(2)}) async-start(bf16[4,192,768]{2,1,0:T(8,128)(2,1)} %broadcast_in_dim.122), calls=%async_computation.5 | async-start | bytes 2359296 | tf_op jit(solution)/shard_map/all_to_all | solution.py:531
  229.0 1.5 collective-permute-start.6
  231.1 1.5 collective-permute-start.8
  232.6 36.6 %all-to-all-done.3.mine_ref = bf16[4,192,768]{2,1,0:T(8,128)(2,1)S(1)} async-done(((bf16[4,192,768]{2,1,0:T(8,128)(2,1)}), bf16[4,192,768]{2,1,0:T(8,128)(2,1)S(1)}, u32[]{:S(2)}, u32[]{:S(2)}) %all-to-all-start.3) | async-done | bytes 1179680 | tf_op jit(solution)/shard_map/all_to_all | solution.py:531
  271.9 2.3 add_add_fusion
  274.2 1.3 fusion.31
  275.5 3.4 %place_io.1 = (f32[192,2304]{1,0:T(8,128)}, f32[192,768]{1,0:T(8,128)}, f32[192,192]{1,0:T(8,128)}) custom-call(s32[1]{0:T(128)} %bitcast.1.core_ref, bf16[4,192,768]{2,1,0:T(8,128)(2,1)} %copy-done.3, bf16[4,192,768]{2,1,0:T(8,128)(2,1)} %collective-permute-done.13.other_ref), custom_call_target="tpu_custom_call" | custom-call | tf_op jit(solution)/shard_map/place_io/pallas_call | solution.py:513
  281.6 1.4 fusion.37
  (210 shorter events, 45.9 us)
Async XLA Ops:
  7.2 94.2 %all-gather.5.cloned.1.call-start = ((), (), s32[]{:S(2)}) async-start(), calls=%async_computation.8 | async-start | bytes 7299072 | tf_op jit(solution)/shard_map/all_gather | solution.py:596
  14.2 50.0 %all-to-all-start = ((bf16[4,624,768]{2,1,0:T(8,128)(2,1)}), bf16[4,624,768]{2,1,0:T(8,128)(2,1)}, u32[]{:S(2)}, u32[]{:S(2)}) async-start(bf16[4,624,768]{2,1,0:T(8,128)(2,1)} %pad_maximum_fusion), calls=%async_computation | async-start | bytes 7667712 | tf_op jit(solution)/shard_map/all_to_all | solution.py:531
  19.5 48.5 %copy-start.17 = (bf16[192,2304]{1,0:T(8,128)(2,1)S(1)}, bf16[192,2304]{1,0:T(8,128)(2,1)}, u32[]{:S(2)}) copy-start(bf16[192,2304]{1,0:T(8,128)(2,1)} %param.17) | copy-start | bytes 2654212
  67.9 6.8 %collective-permute-start = (bf16[4,96,768]{2,1,0:T(8,128)(2,1)S(1)}, bf16[4,96,768]{2,1,0:T(8,128)(2,1)}, u32[]{:S(2)}, u32[]{:S(2)}) collective-permute-start(bf16[4,96,768]{2,1,0:T(8,128)(2,1)S(1)} %slice.137), channel_id=1, source_target_pairs={{0,1},{1,0},{2,3},{3,2},{4,5},{5,4},{6,7},{7,6},{8,9},{9,8},{10,11... | collective-permute-start | bytes 1769480 | tf_op jit(solution)/shard_map/ppermute | solution.py:590
  70.9 21.9 %all-to-all-start.1 = ((bf16[4,208,768]{2,1,0:T(8,128)(2,1)}), bf16[4,208,768]{2,1,0:T(8,128)(2,1)S(1)}, u32[]{:S(2)}, u32[]{:S(2)}) async-start(bf16[4,208,768]{2,1,0:T(8,128)(2,1)} %broadcast_in_dim.111), calls=%async_computation.1 | async-start | bytes 2555904 | tf_op jit(solution)/shard_map/all_to_all | solution.py:531
  74.4 82.4 %reduce-scatter.3.cloned.1.call-start = ((), (), s32[]{:S(2)}) async-start(), calls=%async_computation.6 | async-start | bytes 2654208 | tf_op jit(solution)/shard_map/reduce_scatter | solution.py:641
  93.9 3.9 %collective-permute-start.1 = (bf16[4,192,768]{2,1,0:T(8,128)(2,1)}, bf16[4,192,768]{2,1,0:T(8,128)(2,1)S(1)}, u32[]{:S(2)}, u32[]{:S(2)}) collective-permute-start(bf16[4,192,768]{2,1,0:T(8,128)(2,1)} %slice_add_fusion), channel_id=1, source_target_pairs={{0,1},{1,0},{2,3},{3,2},{4,5},{5,4},{6,7},{7,6},{8,9},{9,8},{10,11... | collective-permute-start | bytes 3538952 | tf_op jit(solution)/shard_map/ppermute | solution.py:590
  99.6 5.9 %copy-start.9 = (bf16[8,192,768]{2,1,0:T(8,128)(2,1)S(1)}, bf16[8,192,768]{2,1,0:T(8,128)(2,1)}, u32[]{:S(2)}) copy-start(bf16[8,192,768]{2,1,0:T(8,128)(2,1)} %get-tuple-element.37) | copy-start | bytes 7077892
  118.6 28.5 %copy-start.5 = (bf16[1,256,768]{2,1,0:T(8,128)(2,1)S(1)}, bf16[1,256,768]{2,1,0:T(8,128)(2,1)}, u32[]{:S(2)}) copy-start(bf16[1,256,768]{2,1,0:T(8,128)(2,1)} %param.29) | copy-start | bytes 1179652
  118.6 28.7 %copy-start.23 = (f32[1,768]{1,0:T(1,128)S(1)}, f32[1,768]{1,0:T(1,128)}, u32[]{:S(2)}) copy-start(f32[1,768]{1,0:T(1,128)} %get-tuple-element.47) | copy-start | bytes 9220
  118.6 28.7 %copy-start.24 = (f32[1,768]{1,0:T(1,128)S(1)}, f32[1,768]{1,0:T(1,128)}, u32[]{:S(2)}) copy-start(f32[1,768]{1,0:T(1,128)} %get-tuple-element.48) | copy-start | bytes 9220
  118.6 28.9 %copy-start.22 = (f32[1,768]{1,0:T(1,128)S(1)}, f32[1,768]{1,0:T(1,128)}, u32[]{:S(2)}) copy-start(f32[1,768]{1,0:T(1,128)} %get-tuple-element.49) | copy-start | bytes 9220
  146.8 3.2 %collective-permute-start.2 = (bf16[4,3,2,64,128]{4,3,2,1,0:T(8,128)(2,1)S(1)}, bf16[4,3,2,64,128]{4,3,2,1,0:T(8,128)(2,1)S(1)}, u32[]{:S(2)}, u32[]{:S(2)}) collective-permute-start(bf16[4,3,2,64,128]{4,3,2,1,0:T(8,128)(2,1)S(1)} %dynamic-slice_bitcast_fusion.1), channel_id=1, source_target_pairs={{0,1},{1,0},{2,3},{3,2},{4,5},{5,4},{6,7},{7,6},{8,9},{9,8},{10,11... | collective-permute-start | bytes 1179656 | tf_op jit(solution)/shard_map/ppermute | solution.py:590
  152.0 31.0 %all-to-all-start.2 = ((bf16[4,3,2,64,128]{4,3,2,1,0:T(8,128)(2,1)}), bf16[4,3,2,64,128]{4,3,2,1,0:T(8,128)(2,1)S(1)}, u32[]{:S(2)}, u32[]{:S(2)}) async-start(bf16[4,3,2,64,128]{4,3,2,1,0:T(8,128)(2,1)} %fusion.22._), calls=%async_computation.2 | async-start | bytes 786432 | tf_op jit(solution)/shard_map/all_to_all | solution.py:531
  156.9 53.3 %all-gather.7.cloned.1.call-start = ((), (), s32[]{:S(2)}) async-start(), calls=%async_computation.9 | async-start | bytes 2654208 | tf_op jit(solution)/shard_map/all_gather | solution.py:682
  157.8 4.0 %collective-permute-start.3 = (bf16[24,768]{1,0:T(8,128)(2,1)S(1)}, bf16[24,768]{1,0:T(8,128)(2,1)S(1)}, u32[]{:S(2)}, u32[]{:S(2)}) collective-permute-start(bf16[24,768]{1,0:T(8,128)(2,1)S(1)} %get-tuple-element.71), channel_id=1, source_target_pairs={{0,8},{8,0},{16,24},{24,16},{1,9},{9,1},{17,25},{25,17},{2,10},{10... | collective-permute-start | bytes 110600 | tf_op jit(solution)/shard_map/ppermute | solution.py:545
  159.6 4.0 %collective-permute-start.4 = (bf16[24,768]{1,0:T(8,128)(2,1)S(1)}, bf16[24,768]{1,0:T(8,128)(2,1)S(1)}, u32[]{:S(2)}, u32[]{:S(2)}) collective-permute-start(bf16[24,768]{1,0:T(8,128)(2,1)S(1)} %get-tuple-element.70), channel_id=1, source_target_pairs={{0,16},{8,24},{16,0},{24,8},{1,17},{9,25},{17,1},{25,9},{2,18},{10... | collective-permute-start | bytes 110600 | tf_op jit(solution)/shard_map/ppermute | solution.py:545
  161.0 4.9 %collective-permute-start.5 = (bf16[24,768]{1,0:T(8,128)(2,1)S(1)}, bf16[24,768]{1,0:T(8,128)(2,1)S(1)}, u32[]{:S(2)}, u32[]{:S(2)}) collective-permute-start(bf16[24,768]{1,0:T(8,128)(2,1)S(1)} %get-tuple-element.69), channel_id=1, source_target_pairs={{0,24},{8,16},{16,8},{24,0},{1,25},{9,17},{17,9},{25,1},{2,26},{10... | collective-permute-start | bytes 110600 | tf_op jit(solution)/shard_map/ppermute | solution.py:545
  167.5 114.0 %reduce-scatter.5.cloned.1.call-start = ((), (), s32[]{:S(2)}) async-start(), calls=%async_computation.7 | async-start | bytes 3538944 | tf_op jit(solution)/shard_map/reduce_scatter | solution.py:723
  180.4 7.9 %copy-start.15 = (f32[192,768]{1,0:T(8,128)S(1)}, f32[192,768]{1,0:T(8,128)}, u32[]{:S(2)}) copy-start(f32[192,768]{1,0:T(8,128)} %get-tuple-element.43) | copy-start | bytes 1769476
  190.4 3.0 %collective-permute-start.9 = (bf16[4,192,768]{2,1,0:T(8,128)(2,1)S(1)}, bf16[4,192,768]{2,1,0:T(8,128)(2,1)}, u32[]{:S(2)}, u32[]{:S(2)}) collective-permute-start(bf16[4,192,768]{2,1,0:T(8,128)(2,1)S(1)} %dynamic-slice_bitcast_fusion), channel_id=1, source_target_pairs={{0,1},{1,0},{2,3},{3,2},{4,5},{5,4},{6,7},{7,6},{8,9},{9,8},{10,11... | collective-permute-start | bytes 3538952 | tf_op jit(solution)/shard_map/ppermute | solution.py:590
  206.6 12.3 %collective-permute-start.10 = (bf16[192,768]{1,0:T(8,128)(2,1)S(1)}, bf16[192,768]{1,0:T(8,128)(2,1)S(1)}, u32[]{:S(2)}, u32[]{:S(2)}) collective-permute-start(bf16[192,768]{1,0:T(8,128)(2,1)S(1)} %get-tuple-element.64), channel_id=1, source_target_pairs={{0,8},{8,0},{16,24},{24,16},{1,9},{9,1},{17,25},{25,17},{2,10},{10... | collective-permute-start | bytes 884744 | tf_op jit(solution)/shard_map/ppermute | solution.py:545
  207.3 15.1 %collective-permute-start.11 = (bf16[192,768]{1,0:T(8,128)(2,1)S(1)}, bf16[192,768]{1,0:T(8,128)(2,1)S(1)}, u32[]{:S(2)}, u32[]{:S(2)}) collective-permute-start(bf16[192,768]{1,0:T(8,128)(2,1)S(1)} %get-tuple-element.66), channel_id=1, source_target_pairs={{0,16},{8,24},{16,0},{24,8},{1,17},{9,25},{17,1},{25,9},{2,18},{10... | collective-permute-start | bytes 884744 | tf_op jit(solution)/shard_map/ppermute | solution.py:545
  207.7 14.6 %collective-permute-start.12 = (bf16[192,768]{1,0:T(8,128)(2,1)S(1)}, bf16[192,768]{1,0:T(8,128)(2,1)S(1)}, u32[]{:S(2)}, u32[]{:S(2)}) collective-permute-start(bf16[192,768]{1,0:T(8,128)(2,1)S(1)} %get-tuple-element.65), channel_id=1, source_target_pairs={{0,24},{8,16},{16,8},{24,0},{1,25},{9,17},{17,9},{25,1},{2,26},{10... | collective-permute-start | bytes 884744 | tf_op jit(solution)/shard_map/ppermute | solution.py:545
  222.5 6.4 %copy-start.2 = (bf16[1,256,768]{2,1,0:T(8,128)(2,1)S(1)}, bf16[1,256,768]{2,1,0:T(8,128)(2,1)}, u32[]{:S(2)}) copy-start(bf16[1,256,768]{2,1,0:T(8,128)(2,1)} %param.15) | copy-start | bytes 1179652
  223.6 46.6 %copy-start.8 = (bf16[4,3,2,64,128]{4,3,2,1,0:T(8,128)(2,1)S(1)}, bf16[4,3,2,64,128]{4,3,2,1,0:T(8,128)(2,1)}, u32[]{:S(2)}) copy-start(bf16[4,3,2,64,128]{4,3,2,1,0:T(8,128)(2,1)} %copy-done.7) | copy-start | bytes 1179652
  223.6 45.5 %all-to-all-start.3 = ((bf16[4,192,768]{2,1,0:T(8,128)(2,1)}), bf16[4,192,768]{2,1,0:T(8,128)(2,1)S(1)}, u32[]{:S(2)}, u32[]{:S(2)}) async-start(bf16[4,192,768]{2,1,0:T(8,128)(2,1)} %broadcast_in_dim.122), calls=%async_computation.5 | async-start | bytes 2359296 | tf_op jit(solution)/shard_map/all_to_all | solution.py:531
  229.0 41.7 %collective-permute-start.6 = (bf16[512,768]{1,0:T(8,128)(2,1)}, bf16[512,768]{1,0:T(8,128)(2,1)S(1)}, u32[]{:S(2)}, u32[]{:S(2)}) collective-permute-start(bf16[512,768]{1,0:T(8,128)(2,1)} %get-tuple-element.39), channel_id=1, source_target_pairs={{0,8},{8,0},{16,24},{24,16},{1,9},{9,1},{17,25},{25,17},{2,10},{10... | collective-permute-start | bytes 2359304 | tf_op jit(solution)/shard_map/ppermute | solution.py:545
  230.5 40.2 %collective-permute-start.7 = (bf16[512,768]{1,0:T(8,128)(2,1)}, bf16[512,768]{1,0:T(8,128)(2,1)S(1)}, u32[]{:S(2)}, u32[]{:S(2)}) collective-permute-start(bf16[512,768]{1,0:T(8,128)(2,1)} %get-tuple-element.40), channel_id=1, source_target_pairs={{0,16},{8,24},{16,0},{24,8},{1,17},{9,25},{17,1},{25,9},{2,18},{10... | collective-permute-start | bytes 2359304 | tf_op jit(solution)/shard_map/ppermute | solution.py:545
  231.1 39.6 %collective-permute-start.8 = (bf16[512,768]{1,0:T(8,128)(2,1)}, bf16[512,768]{1,0:T(8,128)(2,1)}, u32[]{:S(2)}, u32[]{:S(2)}) collective-permute-start(bf16[512,768]{1,0:T(8,128)(2,1)} %get-tuple-element.41), channel_id=1, source_target_pairs={{0,24},{8,16},{16,8},{24,0},{1,25},{9,17},{17,9},{25,1},{2,26},{10... | collective-permute-start | bytes 2359304 | tf_op jit(solution)/shard_map/ppermute | solution.py:545
  269.2 6.4 %collective-permute-start.13 = (bf16[4,192,768]{2,1,0:T(8,128)(2,1)S(1)}, bf16[4,192,768]{2,1,0:T(8,128)(2,1)}, u32[]{:S(2)}, u32[]{:S(2)}) collective-permute-start(bf16[4,192,768]{2,1,0:T(8,128)(2,1)S(1)} %all-to-all-done.3.mine_ref), channel_id=1, source_target_pairs={{0,1},{1,0},{2,3},{3,2},{4,5},{5,4},{6,7},{7,6},{8,9},{9,8},{10,11... | collective-permute-start | bytes 3538952 | tf_op jit(solution)/shard_map/ppermute | solution.py:590
  275.5 7.5 %copy-start.6 = (bf16[1,256,768]{2,1,0:T(8,128)(2,1)S(1)}, bf16[1,256,768]{2,1,0:T(8,128)(2,1)}, u32[]{:S(2)}) copy-start(bf16[1,256,768]{2,1,0:T(8,128)(2,1)} %param.29) | copy-start | bytes 1179652
  (22 other events, 68.8 us)
Sparse Core Ops, SparseCore 0:
  11.7 69.0 all-gather.4
  107.2 37.5 reduce-scatter.2
  167.7 31.2 all-gather.6
  205.4 50.6 reduce-scatter.4
